TPU v7x, 32 devices: a whole 2x2x4 slice. The times are simulated.
32 devices in a mesh: inst: 16 (over z, y, core), tp: 2 (over x).
Axes of the slice: x: 2, y: 2, z: 4, core: 2. Of those that a mesh axis runs over, the one named last changes fastest.
Arguments:
- new_pages: bfloat16 [256, 8, 128, 256], P(('inst', 'tp')), may hold values from -6 to 6
- routes: int32 [256], P('inst'), may hold values from 0 to 15, as said below
- resident: bfloat16 [128, 8, 128, 256], P('inst', 'tp'), may hold values from -8 to 8
- queries: bfloat16 [512, 8, 5, 128], P('inst', 'tp'), may hold values from -24 to 24
- own_kv: bfloat16 [512, 8, 256], P('inst', 'tp'), may hold values from -6 to 6
- tables: int32 [512, 16], P('inst'), may hold values from 0 to 39, as said below
- lengths: int32 [512], P('inst'), may hold values from 128 to 2048, as said below
Outputs:
- attention: bfloat16 [512, 8, 5, 128], P('inst', 'tp')
Inputs may be any that keep to these rules, and one draw needn't show every extreme that they name: `routes`: each instance sends at most 2 of its 16 new pages to any one instance, and exactly 2 to some instance; in every draw one instance receives 2 pages from every instance. `tables`: entry 0 of every table is pool page 0, a prefix shared by the instance's requests. An entry below 8 names a resident page; entry 8 + i * 2 + c names the page with copy number c that instance i sends to this instance, and only pages that are sent are named. `lengths`: every instance has a request of the greatest length.
All inputs are finite; a program needn't handle non-finite values.
Results may differ from a plain program's by a relative error of at most 0.0044.
Values may be sent and summed in bfloat16 or wider, within the bound.
No kernel may reach another device: no remote copies, remote signals or barrier semaphores. Data moves between devices by JAX's collectives and lax.ppermute only.
A program may use at most 128 MiB of HBM per device.

v0:
```python
import jax
import jax.numpy as jnp
from jax import lax
from jax.sharding import PartitionSpec as P

CAP = 2


def widen_queries(queries):
    return jnp.concatenate([queries, jnp.zeros_like(queries)], axis=-1)


def cache_scores(wide_queries, whole_pages):
    scaling = (wide_queries.shape[-1] // 2) ** (-0.5)
    return (
        jnp.einsum(
            "bhqd,bmhpd->bhqmp", wide_queries, whole_pages, preferred_element_type=jnp.float32
        )
        * scaling
    )


def softmax_mix(queries, own_pairs, raw_scores, whole_pages, lengths):
    head_dim = queries.shape[-1]
    scaling = head_dim ** (-0.5)
    own_keys = own_pairs[..., :head_dim]
    own_values = own_pairs[..., head_dim:]
    own_scores = (
        jnp.einsum("bhqd,bhd->bhq", queries, own_keys, preferred_element_type=jnp.float32) * scaling
    )
    page_count, page_width = (raw_scores.shape[3], raw_scores.shape[4])
    places = lax.broadcasted_iota(
        jnp.int32, (page_count, page_width), 0
    ) * page_width + lax.broadcasted_iota(jnp.int32, (page_count, page_width), 1)
    usable = places[None, None, None] < lengths[:, None, None, None, None]
    masked = jnp.where(usable, raw_scores, -jnp.inf)
    highest = jnp.maximum(jnp.max(masked, axis=(3, 4)), own_scores)
    exponent = jnp.exp(masked - highest[..., None, None])
    own_exponent = jnp.exp(own_scores - highest)
    totals = jnp.sum(exponent, axis=(3, 4)) + own_exponent
    weights = exponent.astype(jnp.bfloat16)
    own_weights = own_exponent.astype(jnp.bfloat16)
    combined = jnp.einsum(
        "bhqmp,bmhpd->bhqd", weights, whole_pages, preferred_element_type=jnp.float32
    )
    mixture = combined[..., head_dim:]
    mixture = (
        mixture
        + own_weights.astype(jnp.float32)[..., None] * own_values.astype(jnp.float32)[:, :, None, :]
    )
    return (mixture / totals[..., None]).astype(jnp.bfloat16)


def receive_pages(outgoing, arrived_count, page_shape):
    return lax.all_to_all(outgoing, "inst", split_axis=0, concat_axis=0, tiled=True).reshape(
        (arrived_count,) + page_shape
    )


def on_device(new_pages, routes, resident, queries, own_kv, tables, lengths):
    instances = lax.axis_size("inst")
    regrouped = lax.all_to_all(new_pages, "tp", split_axis=1, concat_axis=0, tiled=True)
    page_total = routes.shape[0]
    same_dest = routes[:, None] == routes[None, :]
    earlier = lax.broadcasted_iota(jnp.int32, (page_total, page_total), 1) < lax.broadcasted_iota(
        jnp.int32, (page_total, page_total), 0
    )
    copy_rank = jnp.sum(jnp.where(same_dest & earlier, 1, 0), axis=1).astype(jnp.int32)
    slot_index = routes * CAP + copy_rank
    page_shape = regrouped.shape[1:]
    outgoing = (
        jnp.zeros((instances * CAP,) + page_shape, regrouped.dtype).at[slot_index].set(regrouped)
    )
    outgoing = outgoing.reshape((instances, CAP) + page_shape)
    arrived_count = instances * CAP
    block_rows = 4
    groups = queries.shape[0] // block_rows
    query_blocks = queries.reshape((groups, block_rows) + queries.shape[1:])
    pair_blocks = own_kv.reshape((groups, block_rows) + own_kv.shape[1:])
    table_blocks = tables.reshape(groups, block_rows, tables.shape[1])
    length_blocks = lengths.reshape(groups, block_rows)
    arrived = receive_pages(outgoing, arrived_count, page_shape)
    page_pool = jnp.concatenate([resident, arrived], axis=0)

    def pooled_block(items):
        query_block, pair_block, table_block, length_block = items
        pages = page_pool[table_block]
        raw_scores = cache_scores(widen_queries(query_block), pages)
        return softmax_mix(query_block, pair_block, raw_scores, pages, length_block)

    result = lax.map(pooled_block, (query_blocks, pair_blocks, table_blocks, length_blocks))
    return result.reshape(queries.shape)


def solution(mesh):
    return jax.shard_map(
        on_device,
        mesh=mesh,
        in_specs=(
            P(("inst", "tp"), None, None, None),
            P("inst"),
            P("inst", "tp", None, None),
            P("inst", "tp", None, None),
            P("inst", "tp", None),
            P("inst", None),
            P("inst"),
        ),
        out_specs=P("inst", "tp", None, None),
        check_vma=False,
    )
```

profile of v0, /device:TPU:13, one launch (start us, length us, event | category | flops | bytes accessed | tf_op | source)
XLA Modules:
  0.0 503.3 jit_solution(17289140263553881423)
XLA Ops:
  0.0 4.6 copy.36
  4.6 5.6 %all-to-all-start = ((bf16[8,8,128,256]{3,2,0,1:T(8,128)(2,1)}), bf16[8,8,128,256]{3,2,0,1:T(8,128)(2,1)}, u32[]{:S(2)}, u32[]{:S(2)}) async-start(bf16[8,8,128,256]{3,2,0,1:T(8,128)(2,1)} %copy.36), calls=%async_computation | async-start | bytes 8388608 | tf_op jit(solution)/shard_map/all_to_all | solution.py:62
  10.4 46.6 %all-to-all-done = bf16[8,8,128,256]{3,2,0,1:T(8,128)(2,1)} async-done(((bf16[8,8,128,256]{3,2,0,1:T(8,128)(2,1)}), bf16[8,8,128,256]{3,2,0,1:T(8,128)(2,1)}, u32[]{:S(2)}, u32[]{:S(2)}) %all-to-all-start) | async-done | bytes 4194336 | tf_op jit(solution)/shard_map/all_to_all | solution.py:62
  65.9 11.0 %scatter_fusion = bf16[32,4,128,256]{3,2,1,0:T(8,128)(2,1)} fusion(bf16[32,4,128,256]{3,2,1,0:T(8,128)(2,1)} %broadcast_in_dim.43, s32[16]{0:T(128)S(1)} %compare_select_fusion.1, bf16[16,4,128,256]{3,2,1,0:T(8,128)(2,1)} %bitcast.61), kind=kCustom, calls=%fused_computation.1 | custom fusion | bytes 12582976 | tf_op jit(solution)/shard_map/scatter | solution.py:72
  77.0 7.5 %all-to-all-start.1 = ((bf16[16,2,4,128,256]{4,3,2,1,0:T(8,128)(2,1)}), bf16[16,2,4,128,256]{4,3,2,1,0:T(8,128)(2,1)}, u32[]{:S(2)}, u32[]{:S(2)}) async-start(bf16[16,2,4,128,256]{4,3,2,1,0:T(8,128)(2,1)} %bitcast.60), calls=%async_computation.1 | async-start | bytes 16777216 | tf_op jit(solution)/shard_map/all_to_all | solution.py:55
  84.7 182.1 %all-to-all-done.1 = bf16[16,2,4,128,256]{4,3,2,1,0:T(8,128)(2,1)} async-done(((bf16[16,2,4,128,256]{4,3,2,1,0:T(8,128)(2,1)}), bf16[16,2,4,128,256]{4,3,2,1,0:T(8,128)(2,1)}, u32[]{:S(2)}, u32[]{:S(2)}) %all-to-all-start.1) | async-done | bytes 8388640 | tf_op jit(solution)/shard_map/all_to_all | solution.py:55
  266.8 8.6 %pad_maximum_fusion = bf16[40,4,128,256]{3,2,1,0:T(8,128)(2,1)} fusion(bf16[32,4,128,256]{3,2,1,0:T(8,128)(2,1)} %bitcast.20, bf16[8,4,128,256]{3,2,1,0:T(8,128)(2,1)S(1)} %copy-done), kind=kLoop, calls=%fused_computation.38 | loop fusion | flops 5242880 | bytes 20971520 | tf_op jit(solution)/shard_map/concatenate | solution.py:83
  275.4 227.2 %while.10 = (s32[]{:T(128)}, bf16[8,4,4,5,128]{4,2,3,1,0:T(4,128)(2,1)S(1)}, s32[8,4]{1,0:T(8,128)S(1)}, bf16[8,4,4,5,128]{4,3,2,1,0:T(8,128)(2,1)S(1)}, s32[8,4...) while((s32[]{:T(128)}, ...), condition=%wide.region_5.6_spmd, body=%wide.region_2.5_spmd.sunk | while | flops 168994480 | bytes 69446104 | solution.py:91
  275.5 11.5 %gather_fusion = bf16[64,4,128,256]{3,2,1,0:T(8,128)(2,1)} fusion(bf16[40,4,128,256]{3,2,1,0:T(8,128)(2,1)} %get-tuple-element.139, s32[1024]{0:T(1024)S(1)} %pad_clamp_fusion.2), kind=kCustom, calls=%fused_computation.clone.1 | custom fusion | bytes 33554688 | tf_op jit(solution)/shard_map/while/body/eval_jaxpr/gather | solution.py:87
  287.3 8.1 %fusion.46 = (f32[4,4,5]{2,1,0:T(4,128)S(1)}, f32[4,4,5,16,128]{4,2,3,1,0:T(8,128)S(1)}) fusion(bf16[4,16,4,128,256]{4,3,2,1,0:T(8,128)(2,1)} %bitcast.58, bf16[4,4,5,128]{3,2,1,0:T(8,128)(2,1)S(1)} %dynamic-slice_bitcast_fusion.4, pred[4,16,128]{2,1,0:T(8,128)(4,1)S(1)} %broadcast_compare_fusion.2), kind=kOutput, calls=%fused_computation.43.clone.1 | convolution fusion | flops 84377520 | bytes 17461568 | tf_op jit(solution)/shard_map/while/body/eval_jaxpr/bhqd,bmhpd->bhqmp/dot_general | solution.py:16
  296.3 7.1 %fusion.48 = f32[4,4,5,256]{3,2,1,0:T(8,128)S(1)} fusion(bf16[4,16,4,128,256]{4,3,2,1,0:T(8,128)(2,1)} %bitcast.59, f32[4,4,5,16,128]{4,2,3,1,0:T(8,128)S(1)} %get-tuple-element.114, f32[4,4,5]{2,1,0:T(4,128)S(1)} %multiply_maximum_fusion.2), kind=kOutput, calls=%fused_computation.8.clone.1 | convolution fusion | flops 84213760 | bytes 17514816 | tf_op jit(solution)/shard_map/while/body/eval_jaxpr/bhqmp,bmhpd->bhqd/dot_general | solution.py:43
  303.9 11.6 %gather_fusion = bf16[64,4,128,256]{3,2,1,0:T(8,128)(2,1)} fusion(bf16[40,4,128,256]{3,2,1,0:T(8,128)(2,1)} %get-tuple-element.139, s32[1024]{0:T(1024)S(1)} %pad_clamp_fusion.2), kind=kCustom, calls=%fused_computation.clone.1 | custom fusion | bytes 33554688 | tf_op jit(solution)/shard_map/while/body/eval_jaxpr/gather | solution.py:87
  315.7 8.1 %fusion.46 = (f32[4,4,5]{2,1,0:T(4,128)S(1)}, f32[4,4,5,16,128]{4,2,3,1,0:T(8,128)S(1)}) fusion(bf16[4,16,4,128,256]{4,3,2,1,0:T(8,128)(2,1)} %bitcast.58, bf16[4,4,5,128]{3,2,1,0:T(8,128)(2,1)S(1)} %dynamic-slice_bitcast_fusion.4, pred[4,16,128]{2,1,0:T(8,128)(4,1)S(1)} %broadcast_compare_fusion.2), kind=kOutput, calls=%fused_computation.43.clone.1 | convolution fusion | flops 84377520 | bytes 17461568 | tf_op jit(solution)/shard_map/while/body/eval_jaxpr/bhqd,bmhpd->bhqmp/dot_general | solution.py:16
  324.7 7.1 %fusion.48 = f32[4,4,5,256]{3,2,1,0:T(8,128)S(1)} fusion(bf16[4,16,4,128,256]{4,3,2,1,0:T(8,128)(2,1)} %bitcast.59, f32[4,4,5,16,128]{4,2,3,1,0:T(8,128)S(1)} %get-tuple-element.114, f32[4,4,5]{2,1,0:T(4,128)S(1)} %multiply_maximum_fusion.2), kind=kOutput, calls=%fused_computation.8.clone.1 | convolution fusion | flops 84213760 | bytes 17514816 | tf_op jit(solution)/shard_map/while/body/eval_jaxpr/bhqmp,bmhpd->bhqd/dot_general | solution.py:43
  332.3 11.5 %gather_fusion = bf16[64,4,128,256]{3,2,1,0:T(8,128)(2,1)} fusion(bf16[40,4,128,256]{3,2,1,0:T(8,128)(2,1)} %get-tuple-element.139, s32[1024]{0:T(1024)S(1)} %pad_clamp_fusion.2), kind=kCustom, calls=%fused_computation.clone.1 | custom fusion | bytes 33554688 | tf_op jit(solution)/shard_map/while/body/eval_jaxpr/gather | solution.py:87
  344.1 8.1 %fusion.46 = (f32[4,4,5]{2,1,0:T(4,128)S(1)}, f32[4,4,5,16,128]{4,2,3,1,0:T(8,128)S(1)}) fusion(bf16[4,16,4,128,256]{4,3,2,1,0:T(8,128)(2,1)} %bitcast.58, bf16[4,4,5,128]{3,2,1,0:T(8,128)(2,1)S(1)} %dynamic-slice_bitcast_fusion.4, pred[4,16,128]{2,1,0:T(8,128)(4,1)S(1)} %broadcast_compare_fusion.2), kind=kOutput, calls=%fused_computation.43.clone.1 | convolution fusion | flops 84377520 | bytes 17461568 | tf_op jit(solution)/shard_map/while/body/eval_jaxpr/bhqd,bmhpd->bhqmp/dot_general | solution.py:16
  353.1 7.1 %fusion.48 = f32[4,4,5,256]{3,2,1,0:T(8,128)S(1)} fusion(bf16[4,16,4,128,256]{4,3,2,1,0:T(8,128)(2,1)} %bitcast.59, f32[4,4,5,16,128]{4,2,3,1,0:T(8,128)S(1)} %get-tuple-element.114, f32[4,4,5]{2,1,0:T(4,128)S(1)} %multiply_maximum_fusion.2), kind=kOutput, calls=%fused_computation.8.clone.1 | convolution fusion | flops 84213760 | bytes 17514816 | tf_op jit(solution)/shard_map/while/body/eval_jaxpr/bhqmp,bmhpd->bhqd/dot_general | solution.py:43
  360.7 11.6 %gather_fusion = bf16[64,4,128,256]{3,2,1,0:T(8,128)(2,1)} fusion(bf16[40,4,128,256]{3,2,1,0:T(8,128)(2,1)} %get-tuple-element.139, s32[1024]{0:T(1024)S(1)} %pad_clamp_fusion.2), kind=kCustom, calls=%fused_computation.clone.1 | custom fusion | bytes 33554688 | tf_op jit(solution)/shard_map/while/body/eval_jaxpr/gather | solution.py:87
  372.5 8.1 %fusion.46 = (f32[4,4,5]{2,1,0:T(4,128)S(1)}, f32[4,4,5,16,128]{4,2,3,1,0:T(8,128)S(1)}) fusion(bf16[4,16,4,128,256]{4,3,2,1,0:T(8,128)(2,1)} %bitcast.58, bf16[4,4,5,128]{3,2,1,0:T(8,128)(2,1)S(1)} %dynamic-slice_bitcast_fusion.4, pred[4,16,128]{2,1,0:T(8,128)(4,1)S(1)} %broadcast_compare_fusion.2), kind=kOutput, calls=%fused_computation.43.clone.1 | convolution fusion | flops 84377520 | bytes 17461568 | tf_op jit(solution)/shard_map/while/body/eval_jaxpr/bhqd,bmhpd->bhqmp/dot_general | solution.py:16
  381.5 7.1 %fusion.48 = f32[4,4,5,256]{3,2,1,0:T(8,128)S(1)} fusion(bf16[4,16,4,128,256]{4,3,2,1,0:T(8,128)(2,1)} %bitcast.59, f32[4,4,5,16,128]{4,2,3,1,0:T(8,128)S(1)} %get-tuple-element.114, f32[4,4,5]{2,1,0:T(4,128)S(1)} %multiply_maximum_fusion.2), kind=kOutput, calls=%fused_computation.8.clone.1 | convolution fusion | flops 84213760 | bytes 17514816 | tf_op jit(solution)/shard_map/while/body/eval_jaxpr/bhqmp,bmhpd->bhqd/dot_general | solution.py:43
  389.2 11.5 %gather_fusion = bf16[64,4,128,256]{3,2,1,0:T(8,128)(2,1)} fusion(bf16[40,4,128,256]{3,2,1,0:T(8,128)(2,1)} %get-tuple-element.139, s32[1024]{0:T(1024)S(1)} %pad_clamp_fusion.2), kind=kCustom, calls=%fused_computation.clone.1 | custom fusion | bytes 33554688 | tf_op jit(solution)/shard_map/while/body/eval_jaxpr/gather | solution.py:87
  400.9 8.1 %fusion.46 = (f32[4,4,5]{2,1,0:T(4,128)S(1)}, f32[4,4,5,16,128]{4,2,3,1,0:T(8,128)S(1)}) fusion(bf16[4,16,4,128,256]{4,3,2,1,0:T(8,128)(2,1)} %bitcast.58, bf16[4,4,5,128]{3,2,1,0:T(8,128)(2,1)S(1)} %dynamic-slice_bitcast_fusion.4, pred[4,16,128]{2,1,0:T(8,128)(4,1)S(1)} %broadcast_compare_fusion.2), kind=kOutput, calls=%fused_computation.43.clone.1 | convolution fusion | flops 84377520 | bytes 17461568 | tf_op jit(solution)/shard_map/while/body/eval_jaxpr/bhqd,bmhpd->bhqmp/dot_general | solution.py:16
  409.9 7.1 %fusion.48 = f32[4,4,5,256]{3,2,1,0:T(8,128)S(1)} fusion(bf16[4,16,4,128,256]{4,3,2,1,0:T(8,128)(2,1)} %bitcast.59, f32[4,4,5,16,128]{4,2,3,1,0:T(8,128)S(1)} %get-tuple-element.114, f32[4,4,5]{2,1,0:T(4,128)S(1)} %multiply_maximum_fusion.2), kind=kOutput, calls=%fused_computation.8.clone.1 | convolution fusion | flops 84213760 | bytes 17514816 | tf_op jit(solution)/shard_map/while/body/eval_jaxpr/bhqmp,bmhpd->bhqd/dot_general | solution.py:43
  417.5 11.5 %gather_fusion = bf16[64,4,128,256]{3,2,1,0:T(8,128)(2,1)} fusion(bf16[40,4,128,256]{3,2,1,0:T(8,128)(2,1)} %get-tuple-element.139, s32[1024]{0:T(1024)S(1)} %pad_clamp_fusion.2), kind=kCustom, calls=%fused_computation.clone.1 | custom fusion | bytes 33554688 | tf_op jit(solution)/shard_map/while/body/eval_jaxpr/gather | solution.py:87
  429.3 8.1 %fusion.46 = (f32[4,4,5]{2,1,0:T(4,128)S(1)}, f32[4,4,5,16,128]{4,2,3,1,0:T(8,128)S(1)}) fusion(bf16[4,16,4,128,256]{4,3,2,1,0:T(8,128)(2,1)} %bitcast.58, bf16[4,4,5,128]{3,2,1,0:T(8,128)(2,1)S(1)} %dynamic-slice_bitcast_fusion.4, pred[4,16,128]{2,1,0:T(8,128)(4,1)S(1)} %broadcast_compare_fusion.2), kind=kOutput, calls=%fused_computation.43.clone.1 | convolution fusion | flops 84377520 | bytes 17461568 | tf_op jit(solution)/shard_map/while/body/eval_jaxpr/bhqd,bmhpd->bhqmp/dot_general | solution.py:16
  438.3 7.1 %fusion.48 = f32[4,4,5,256]{3,2,1,0:T(8,128)S(1)} fusion(bf16[4,16,4,128,256]{4,3,2,1,0:T(8,128)(2,1)} %bitcast.59, f32[4,4,5,16,128]{4,2,3,1,0:T(8,128)S(1)} %get-tuple-element.114, f32[4,4,5]{2,1,0:T(4,128)S(1)} %multiply_maximum_fusion.2), kind=kOutput, calls=%fused_computation.8.clone.1 | convolution fusion | flops 84213760 | bytes 17514816 | tf_op jit(solution)/shard_map/while/body/eval_jaxpr/bhqmp,bmhpd->bhqd/dot_general | solution.py:43
  445.9 11.5 %gather_fusion = bf16[64,4,128,256]{3,2,1,0:T(8,128)(2,1)} fusion(bf16[40,4,128,256]{3,2,1,0:T(8,128)(2,1)} %get-tuple-element.139, s32[1024]{0:T(1024)S(1)} %pad_clamp_fusion.2), kind=kCustom, calls=%fused_computation.clone.1 | custom fusion | bytes 33554688 | tf_op jit(solution)/shard_map/while/body/eval_jaxpr/gather | solution.py:87
  457.7 8.1 %fusion.46 = (f32[4,4,5]{2,1,0:T(4,128)S(1)}, f32[4,4,5,16,128]{4,2,3,1,0:T(8,128)S(1)}) fusion(bf16[4,16,4,128,256]{4,3,2,1,0:T(8,128)(2,1)} %bitcast.58, bf16[4,4,5,128]{3,2,1,0:T(8,128)(2,1)S(1)} %dynamic-slice_bitcast_fusion.4, pred[4,16,128]{2,1,0:T(8,128)(4,1)S(1)} %broadcast_compare_fusion.2), kind=kOutput, calls=%fused_computation.43.clone.1 | convolution fusion | flops 84377520 | bytes 17461568 | tf_op jit(solution)/shard_map/while/body/eval_jaxpr/bhqd,bmhpd->bhqmp/dot_general | solution.py:16
  466.7 7.1 %fusion.48 = f32[4,4,5,256]{3,2,1,0:T(8,128)S(1)} fusion(bf16[4,16,4,128,256]{4,3,2,1,0:T(8,128)(2,1)} %bitcast.59, f32[4,4,5,16,128]{4,2,3,1,0:T(8,128)S(1)} %get-tuple-element.114, f32[4,4,5]{2,1,0:T(4,128)S(1)} %multiply_maximum_fusion.2), kind=kOutput, calls=%fused_computation.8.clone.1 | convolution fusion | flops 84213760 | bytes 17514816 | tf_op jit(solution)/shard_map/while/body/eval_jaxpr/bhqmp,bmhpd->bhqd/dot_general | solution.py:43
  474.3 11.6 %gather_fusion = bf16[64,4,128,256]{3,2,1,0:T(8,128)(2,1)} fusion(bf16[40,4,128,256]{3,2,1,0:T(8,128)(2,1)} %get-tuple-element.139, s32[1024]{0:T(1024)S(1)} %pad_clamp_fusion.2), kind=kCustom, calls=%fused_computation.clone.1 | custom fusion | bytes 33554688 | tf_op jit(solution)/shard_map/while/body/eval_jaxpr/gather | solution.py:87
  486.1 8.1 %fusion.46 = (f32[4,4,5]{2,1,0:T(4,128)S(1)}, f32[4,4,5,16,128]{4,2,3,1,0:T(8,128)S(1)}) fusion(bf16[4,16,4,128,256]{4,3,2,1,0:T(8,128)(2,1)} %bitcast.58, bf16[4,4,5,128]{3,2,1,0:T(8,128)(2,1)S(1)} %dynamic-slice_bitcast_fusion.4, pred[4,16,128]{2,1,0:T(8,128)(4,1)S(1)} %broadcast_compare_fusion.2), kind=kOutput, calls=%fused_computation.43.clone.1 | convolution fusion | flops 84377520 | bytes 17461568 | tf_op jit(solution)/shard_map/while/body/eval_jaxpr/bhqd,bmhpd->bhqmp/dot_general | solution.py:16
  495.1 7.1 %fusion.48 = f32[4,4,5,256]{3,2,1,0:T(8,128)S(1)} fusion(bf16[4,16,4,128,256]{4,3,2,1,0:T(8,128)(2,1)} %bitcast.59, f32[4,4,5,16,128]{4,2,3,1,0:T(8,128)S(1)} %get-tuple-element.114, f32[4,4,5]{2,1,0:T(4,128)S(1)} %multiply_maximum_fusion.2), kind=kOutput, calls=%fused_computation.8.clone.1 | convolution fusion | flops 84213760 | bytes 17514816 | tf_op jit(solution)/shard_map/while/body/eval_jaxpr/bhqmp,bmhpd->bhqd/dot_general | solution.py:43
  (148 shorter events, 22.8 us)
Async XLA Ops:
  0.0 10.2 %copy-start.5 = (s32[16]{0:T(128)S(1)}, s32[16]{0:T(128)}, u32[]{:S(2)}) copy-start(s32[16]{0:T(128)} %param.10) | copy-start | bytes 196
  4.6 52.4 %all-to-all-start = ((bf16[8,8,128,256]{3,2,0,1:T(8,128)(2,1)}), bf16[8,8,128,256]{3,2,0,1:T(8,128)(2,1)}, u32[]{:S(2)}, u32[]{:S(2)}) async-start(bf16[8,8,128,256]{3,2,0,1:T(8,128)(2,1)} %copy.36), calls=%async_computation | async-start | bytes 8388608 | tf_op jit(solution)/shard_map/all_to_all | solution.py:62
  77.0 7.5 %copy-start.1 = (bf16[32,4,5,128]{3,1,2,0:T(4,128)(2,1)S(1)}, bf16[32,4,5,128]{3,1,2,0:T(4,128)(2,1)}, u32[]{:S(2)}) copy-start(bf16[32,4,5,128]{3,1,2,0:T(4,128)(2,1)} %param.12) | copy-start | bytes 491524
  77.0 7.6 %copy-start.2 = (s32[32,16]{0,1:T(8,128)S(1)}, s32[32,16]{0,1:T(8,128)}, u32[]{:S(2)}) copy-start(s32[32,16]{0,1:T(8,128)} %param.14) | copy-start | bytes 6148
  77.0 7.7 %copy-start.3 = (s32[32]{0:T(128)S(1)}, s32[32]{0:T(128)}, u32[]{:S(2)}) copy-start(s32[32]{0:T(128)} %param.15) | copy-start | bytes 388
  77.0 189.8 %copy-start = (bf16[8,4,128,256]{3,2,1,0:T(8,128)(2,1)S(1)}, bf16[8,4,128,256]{3,2,1,0:T(8,128)(2,1)}, u32[]{:S(2)}) copy-start(bf16[8,4,128,256]{3,2,1,0:T(8,128)(2,1)} %param.11) | copy-start | bytes 6291460
  77.0 189.8 %all-to-all-start.1 = ((bf16[16,2,4,128,256]{4,3,2,1,0:T(8,128)(2,1)}), bf16[16,2,4,128,256]{4,3,2,1,0:T(8,128)(2,1)}, u32[]{:S(2)}, u32[]{:S(2)}) async-start(bf16[16,2,4,128,256]{4,3,2,1,0:T(8,128)(2,1)} %bitcast.60), calls=%async_computation.1 | async-start | bytes 16777216 | tf_op jit(solution)/shard_map/all_to_all | solution.py:55
  502.6 0.7 copy-start.4
where the time goes:
time: 504 us; the launch traced here: 503 us
  waiting for transfers between devices  229 us (45%)
  local copies, waits for them, and re-layouts  125 us (25%)
  matrix products  123 us (24%)
  other arithmetic  13.9 us (3%)
  starting transfers between devices  13.1 us (3%)
    all_to_all x1, waiting for transfers between devices, receive_pages(): lax.all_to_all(outgoing, 'inst', split_axis=0, concat_axis=0, tiled=True)  182 us
    gather x8, local copies, waits for them, and re-layouts, pooled_block(): pages = page_pool[table_block]  92.4 us
    dot_general x8, matrix products, cache_scores(): jnp.einsum('bhqd,bmhpd->bhqmp', wide_queries, whole_pages, preferred_elem...  65 us
    dot_general x8, matrix products, softmax_mix(): jnp.einsum('bhqmp,bmhpd->bhqd', weights, whole_pages, preferred_element_t...  56.5 us
    all_to_all x1, waiting for transfers between devices, on_device(): lax.all_to_all(new_pages, 'tp', split_axis=1, concat_axis=0, tiled=True)  46.6 us
    scatter x1, local copies, waits for them, and re-layouts, on_device(): jnp.zeros((instances * CAP,) + page_shape, regrouped.dtype).at[slot_index]  11 us
  transfers between devices with their start and end apart: 2, of which 2 were waited for; matrix products, arithmetic and copies ran while one was open for 0% of the time, Pallas kernels for 0%

commit v1 on v0

v1 whole, which is shorter than its diff:
```python
import functools

import jax
import jax.numpy as jnp
from jax import lax
from jax.experimental import pallas as pl
from jax.experimental.pallas import tpu as pltpu
from jax.sharding import PartitionSpec as P

CAP = 2
LANES = 128
NEG = -1e30
VMEM_LIMIT = 56 * 1024 * 1024


def tail_rows(blocks, per_block):
    return -(-3 * blocks * per_block // 16) * 16


class Layout:
    def __init__(self, groups, requests):
        self.groups = groups
        self.requests = requests
        self.rows = groups * requests
        self.per_row = LANES // requests
        self.lse_rows = -(-groups // self.per_row)

    def parcel(self, blocks):
        return blocks * self.rows + tail_rows(blocks, self.lse_rows)

    def lane_masks(self):
        lane = lax.broadcasted_iota(jnp.int32, (self.requests, LANES), 1)
        row = lax.broadcasted_iota(jnp.int32, (self.requests, LANES), 0)
        return [lane == row + quarter * self.requests for quarter in range(self.per_row)]

    def column_to_rows(self, column, masks):
        out = []
        for line in range(self.lse_rows):
            total = None
            for quarter in range(self.per_row):
                g = line * self.per_row + quarter
                if g < self.groups:
                    part = column[g * self.requests : (g + 1) * self.requests]
                    part = jnp.where(masks[quarter], part, 0.0)
                    total = part if total is None else total + part
            out.append(jnp.sum(total, axis=0, keepdims=True))
        return out

    def row_to_column(self, line, quarter, masks):
        wide = jnp.broadcast_to(line, (self.requests, LANES))
        return jnp.sum(jnp.where(masks[quarter], wide, 0.0), axis=1, keepdims=True)


def store_tail(out, first, lse, tail):
    count = lse.shape[0]
    tail[...] = jnp.zeros_like(tail)
    high = lse.astype(jnp.bfloat16).astype(jnp.float32)
    middle = (lse - high).astype(jnp.bfloat16).astype(jnp.float32)
    tail[0:count] = high
    tail[count : 2 * count] = middle
    tail[2 * count : 3 * count] = lse - high - middle
    out[first : first + tail.shape[0]] = tail[...].astype(jnp.bfloat16)


def load_tail(ref, first, count, tail):
    tail[...] = ref[first : first + tail.shape[0]].astype(jnp.float32)
    return tail[0:count] + tail[count : 2 * count] + tail[2 * count : 3 * count]


def attend_kernel(shape, lay, lists, *refs):
    (na, nb, nt, order, width) = shape
    q_refs, refs = refs[: nt if order == "b" else nb], refs[nt if order == "b" else nb :]
    meta, own_pages, other_pages = refs[:3]
    outs = refs[3 : 3 + len(q_refs)]
    bias, acc, top, total, lse = refs[3 + len(q_refs) : 8 + len(q_refs)]
    tail = refs[8 + len(q_refs)]
    rows, head_dim = lay.rows, own_pages.shape[-1] // 2
    page = own_pages.shape[-2]
    scaling = head_dim ** (-0.5)
    dests = na * nb
    masks = lay.lane_masks()
    lane = lax.broadcasted_iota(jnp.int32, (lay.requests, LANES), 1)
    position = lax.broadcasted_iota(jnp.int32, (lay.requests, page), 1)

    def column_of(dest, index):
        plane = meta[dest, pl.ds(pl.multiple_of(index // LANES * lay.requests, lay.requests), lay.requests)]
        picked = jnp.where(lane == index % LANES, plane.astype(jnp.float32), 0.0)
        return jnp.sum(picked, axis=1, keepdims=True)

    def place(sb, sa, st):
        if order == "b":
            return st, sb * na + sa
        return sb, st * na + sa

    for sb in range(nb):

        def one_dest(sa, carry, sb=sb):
            dest = sb * na + sa
            entry = dest * 5
            count_own = lists[entry]
            count_other = lists[5 * dests + entry]

            @pl.when(count_own + count_other == 0)
            def _():
                for st in range(nt):
                    which, block = place(sb, sa, st)
                    outs[which][pl.ds(pl.multiple_of(block * rows, rows), rows)] = jnp.zeros(
                        (rows, head_dim), jnp.bfloat16
                    )
                    lse[which, pl.ds(block * lay.lse_rows, lay.lse_rows)] = jnp.full(
                        (lay.lse_rows, LANES), NEG, jnp.float32
                    )

            @pl.when(count_own + count_other > 0)
            def _():
                acc[...] = jnp.zeros_like(acc)
                total[...] = jnp.zeros_like(total)
                top[...] = jnp.full_like(top, 2 * NEG)
                for source, (pages, count) in enumerate(
                    ((own_pages, count_own), (other_pages, count_other))
                ):

                    def one_page(j, carry, source=source, pages=pages):
                        base = source * 5 * dests + entry
                        index = lists[base + 1 + j]
                        column = lists[base + 3 + j]
                        full = column_of(dest, column)
                        part = column_of(dest, width + column)
                        times = full + jnp.where(position < part.astype(jnp.int32), 1.0, 0.0)
                        bias[...] = jnp.where(times > 0, jnp.log(jnp.maximum(times, 1.0)), NEG)
                        for st in range(nt):
                            which, block = place(sb, sa, st)
                            if order == "b":
                                query = q_refs[st][dest]
                            else:
                                query = q_refs[sb][block]
                            head = lists[10 * dests + st]
                            keys = pages[index, head, 0, :, :head_dim]
                            values = pages[index, head, 0, :, head_dim:]
                            scores = lax.dot_general(
                                query, keys, (((1,), (1,)), ((), ())),
                                preferred_element_type=jnp.float32,
                            )
                            scores = scores * scaling
                            scores = scores + jnp.concatenate([bias[...]] * lay.groups, axis=0)
                            before = top[st]
                            now = jnp.maximum(before, jnp.max(scores, axis=1, keepdims=True))
                            shrink = jnp.exp(before - now)
                            weights = jnp.exp(scores - now)
                            total[st] = total[st] * shrink + jnp.sum(weights, axis=1, keepdims=True)
                            acc[st] = acc[st] * shrink + jnp.dot(
                                weights.astype(jnp.bfloat16), values,
                                preferred_element_type=jnp.float32,
                            )
                            top[st] = now
                        return carry

                    lax.fori_loop(0, count, one_page, 0)
                for st in range(nt):
                    which, block = place(sb, sa, st)
                    outs[which][pl.ds(pl.multiple_of(block * rows, rows), rows)] = (
                        acc[st] / total[st]
                    ).astype(jnp.bfloat16)
                    lines = lay.column_to_rows(top[st] + jnp.log(total[st]), masks)
                    for number, line in enumerate(lines):
                        lse[which, pl.ds(block * lay.lse_rows + number, 1)] = line

            return carry

        lax.fori_loop(0, na, one_dest, 0)
    for which, out in enumerate(outs):
        store_tail(out, out.shape[0] - tail.shape[0], lse[which], tail)


def merge_kernel(n, blocks, parts, lay, *refs):
    ins, outs = refs[:n], refs[n : n + parts]
    weights, merged, tail_in, tail_out = refs[n + parts :]
    lines = blocks * lay.lse_rows
    each = blocks // parts
    masks = lay.lane_masks()
    parts_lse = [load_tail(ref, blocks * lay.rows, lines, tail_in) for ref in ins]
    highest = functools.reduce(jnp.maximum, parts_lse)
    exps = [jnp.exp(value - highest) for value in parts_lse]
    total = functools.reduce(jnp.add, exps)
    for i in range(n):
        weights[i] = exps[i] / total
    merged[...] = highest + jnp.log(total)
    for which in range(parts):

        def one_block(b, carry, which=which):
            source = which * each + b
            for g in range(lay.groups):
                line = source * lay.lse_rows + g // lay.per_row
                start = pl.multiple_of(source * lay.rows, lay.rows) + g * lay.requests
                mixed = None
                for i in range(n):
                    column = lay.row_to_column(weights[i, pl.ds(line, 1)], g % lay.per_row, masks)
                    term = column * ins[i][pl.ds(start, lay.requests)].astype(jnp.float32)
                    mixed = term if mixed is None else mixed + term
                goal = pl.multiple_of(b * lay.rows, lay.rows) + g * lay.requests
                outs[which][pl.ds(goal, lay.requests)] = mixed.astype(jnp.bfloat16)
            return carry

        lax.fori_loop(0, each, one_block, 0)
        span = each * lay.lse_rows
        store_tail(outs[which], each * lay.rows, merged[which * span : (which + 1) * span], tail_out)


def resident_kernel(lay, q_ref, pages, own, meta, out, lse, scores):
    heads, count, page = q_ref.shape[0], pages.shape[0], pages.shape[2]
    head_dim = pages.shape[-1] // 2
    scaling = head_dim ** (-0.5)
    masks = lay.lane_masks()
    position = lax.broadcasted_iota(jnp.int32, (lay.requests, page), 1)
    lane = lax.broadcasted_iota(jnp.int32, (lay.requests, LANES), 1)
    plane = meta[...].astype(jnp.float32)

    def column_of(index):
        return jnp.sum(jnp.where(lane == index, plane, 0.0), axis=1, keepdims=True)

    biases = []
    for p in range(count):
        part = column_of(count + p).astype(jnp.int32)
        times = column_of(p) + jnp.where(position < part, 1.0, 0.0)
        biases.append(jnp.where(times > 0, jnp.log(jnp.maximum(times, 1.0)), NEG))
    lse[...] = jnp.zeros_like(lse)
    for h in range(heads):
        query = q_ref[h]
        own_keys = jnp.concatenate([own[h, :, :head_dim].astype(jnp.float32)] * lay.groups, axis=0)
        own_values = jnp.concatenate([own[h, :, head_dim:].astype(jnp.float32)] * lay.groups, axis=0)
        own_scores = jnp.sum(query.astype(jnp.float32) * own_keys, axis=1, keepdims=True) * scaling
        highest = jnp.broadcast_to(own_scores, (lay.rows, page))
        for p in range(count):
            value = lax.dot_general(
                query, pages[p, h, :, :head_dim], (((1,), (1,)), ((), ())),
                preferred_element_type=jnp.float32,
            )
            value = value * scaling + jnp.concatenate([biases[p]] * lay.groups, axis=0)
            scores[p] = value
            highest = jnp.maximum(highest, value)
        highest = jnp.max(highest, axis=1, keepdims=True)
        own_weights = jnp.exp(own_scores - highest)
        total = jnp.zeros((lay.rows, page), jnp.float32)
        mixed = own_weights * own_values
        for p in range(count):
            weights = jnp.exp(scores[p] - highest)
            total = total + weights
            mixed = mixed + jnp.dot(
                weights.astype(jnp.bfloat16), pages[p, h, :, head_dim:],
                preferred_element_type=jnp.float32,
            )
        total = jnp.sum(total, axis=1, keepdims=True) + own_weights
        out[h] = mixed / total
        column = jnp.broadcast_to(highest + jnp.log(total), (lay.rows, LANES))
        for number, line in enumerate(lay.column_to_rows(column, masks)):
            at = h * lay.lse_rows + number
            lse[at : at + 1] = line


def final_kernel(n, heads, lay, *refs):
    ins, refs = refs[: n * heads], refs[n * heads :]
    local, local_lse, out, weights, tail = refs
    masks = lay.lane_masks()
    for h in range(heads):
        parcels = ins[h * n : (h + 1) * n]
        parts = [load_tail(ref, lay.rows, lay.lse_rows, tail) for ref in parcels]
        parts.append(local_lse[h * lay.lse_rows : (h + 1) * lay.lse_rows])
        highest = functools.reduce(jnp.maximum, parts)
        exps = [jnp.exp(value - highest) for value in parts]
        total = functools.reduce(jnp.add, exps)
        for i in range(n + 1):
            weights[i] = exps[i] / total
        for g in range(lay.groups):
            line, quarter = g // lay.per_row, g % lay.per_row
            span = slice(g * lay.requests, (g + 1) * lay.requests)
            mixed = lay.row_to_column(weights[n, line : line + 1], quarter, masks) * local[h, span]
            for i in range(n):
                column = lay.row_to_column(weights[i, line : line + 1], quarter, masks)
                mixed = mixed + column * parcels[i][span].astype(jnp.float32)
            out[h, span] = mixed.astype(out.dtype)


def vmem(count):
    return [pl.BlockSpec(memory_space=pltpu.VMEM)] * count


def params():
    return pltpu.CompilerParams(vmem_limit_bytes=VMEM_LIMIT)


def on_device(new_pages, routes, resident, queries, own_kv, tables, lengths):
    n_inst, nt = lax.axis_size("inst"), lax.axis_size("tp")
    half = n_inst // 2
    nb = max(b for b in range(1, half + 1) if half % b == 0 and b * b <= half)
    na = half // nb
    requests, heads, groups, head_dim = queries.shape
    resident_count, page = resident.shape[0], resident.shape[2]
    lay = Layout(groups, requests)
    rows = lay.rows
    me, tp = lax.axis_index("inst"), lax.axis_index("tp")
    core, b_at, a_at = me % 2, me // 2 % nb, me // (2 * nb)

    def shift(x, axis, by):
        if axis == "t":
            return lax.ppermute(x, "tp", [(i, (i + by) % nt) for i in range(nt)])
        pairs = []
        for i in range(n_inst):
            c, b, a = i % 2, i // 2 % nb, i // (2 * nb)
            if axis == "a":
                a = (a + by) % na
            elif axis == "b":
                b = (b + by) % nb
            else:
                c = (c + by) % 2
            pairs.append((i, (a * nb + b) * 2 + c))
        return lax.ppermute(x, "inst", pairs)

    sizes = {"a": na, "b": nb, "t": nt}

    def gather(x, axis):
        return [x] + [shift(x, axis, by) for by in range(1, sizes[axis])]

    pool = resident_count + n_inst * CAP
    whole = lengths // page
    places = lax.broadcasted_iota(jnp.int32, tables.shape, 1)
    names = tables[:, :, None] == lax.broadcasted_iota(jnp.int32, (1, 1, pool), 2)
    full = jnp.sum(jnp.where(names & (places < whole[:, None])[:, :, None], 1, 0), axis=1)
    rest = jnp.where(places == whole[:, None], (lengths % page)[:, None], 0)
    part = jnp.sum(jnp.where(names, rest[:, :, None], 0), axis=1)
    width = n_inst * CAP
    planes = -(-2 * width // LANES)
    meta = jnp.concatenate([full[:, resident_count:], part[:, resident_count:]], axis=1)
    meta = jnp.pad(meta, ((0, 0), (0, planes * LANES - 2 * width))).astype(jnp.bfloat16)
    meta = meta.reshape(requests, planes, LANES).transpose(1, 0, 2).reshape(planes * requests, LANES)
    meta_local = jnp.concatenate([full[:, :resident_count], part[:, :resident_count]], axis=1)
    meta_local = jnp.pad(meta_local, ((0, 0), (0, LANES - 2 * resident_count))).astype(jnp.bfloat16)

    query_rows = queries.transpose(1, 2, 0, 3).reshape(heads, rows, head_dim)

    orders = ["b" if k % 2 == 0 else "t" for k in range(heads)]
    gathered = []
    for k in range(heads):
        piece = query_rows[k]
        if k == 0:
            piece = jnp.concatenate([piece, meta], axis=0)
        gathered.append(jnp.stack(gather(piece, "a")))
    other_pages = shift(new_pages, "c", 1)
    first = []
    for k in range(heads):
        first.append(jnp.concatenate(gather(gathered[k], orders[k]), axis=0))
    second = []
    for k in range(heads):
        second.append(gather(first[k], "t" if orders[k] == "b" else "b"))
    metas = first[0][:, rows:]

    page_count = new_pages.shape[0]
    same = routes[:, None] == routes[None, :]
    total_pages = routes.shape[0]
    earlier = lax.broadcasted_iota(jnp.int32, (total_pages, total_pages), 1) < lax.broadcasted_iota(
        jnp.int32, (total_pages, total_pages), 0
    )
    rank = jnp.sum(jnp.where(same & earlier, 1, 0), axis=1).astype(jnp.int32)
    mine = jnp.stack([routes, me * CAP + rank])
    mine = lax.dynamic_slice_in_dim(mine, tp * page_count, page_count, axis=1)
    both = jnp.stack([mine, shift(mine, "c", 1)])
    dest_b = (b_at - jnp.arange(nb, dtype=jnp.int32)) % nb
    dest_a = (a_at - jnp.arange(na, dtype=jnp.int32)) % na
    dest = ((dest_a[None, :] * nb + dest_b[:, None]) * 2 + core).reshape(na * nb)
    hit = both[:, 0][:, None, :] == dest[None, :, None]
    order = lax.broadcasted_iota(jnp.int32, hit.shape, 2)
    count = jnp.sum(jnp.where(hit, 1, 0), axis=2)
    index = jnp.stack(
        [jnp.min(jnp.where(hit, order, page_count - 1), axis=2), jnp.max(jnp.where(hit, order, 0), axis=2)], axis=2
    )
    chosen = index[..., None] == lax.broadcasted_iota(jnp.int32, index.shape + (page_count,), 3)
    column = jnp.sum(jnp.where(chosen, both[:, 1][:, None, None, :], 0), axis=3)
    lists = jnp.concatenate([count[..., None], index, column], axis=2).reshape(-1)
    tp_of_slot = (tp - jnp.arange(nt, dtype=jnp.int32)) % nt
    lists = jnp.concatenate([lists, tp_of_slot]).astype(jnp.int32)

    local, local_lse = pl.pallas_call(
        functools.partial(resident_kernel, lay),
        out_shape=(
            jax.ShapeDtypeStruct((heads, rows, head_dim), jnp.float32),
            jax.ShapeDtypeStruct((-(-heads * lay.lse_rows // 8) * 8, LANES), jnp.float32),
        ),
        in_specs=vmem(4),
        out_specs=tuple(vmem(2)),
        scratch_shapes=[pltpu.VMEM((resident_count, rows, page), jnp.float32)],
        compiler_params=params(),
        name="resident",
    )(query_rows, resident, own_kv.transpose(1, 0, 2), meta_local)

    own_split = new_pages.reshape(page_count, nt, heads, page, 2 * head_dim)
    other_split = other_pages.reshape(page_count, nt, heads, page, 2 * head_dim)

    def attend(k):
        way = orders[k]
        n_out = nt if way == "b" else nb
        blocks = na * nb * nt // n_out
        q_blocks = [x[:, :rows] if k == 0 else x for x in second[k]]
        page_spec = pl.BlockSpec(
            (page_count, nt, 1, page, 2 * head_dim), lambda i: (0, 0, k, 0, 0)
        )
        full_spec = lambda x: pl.BlockSpec(x.shape, lambda i: (0,) * x.ndim)
        lse_lines = blocks * lay.lse_rows
        out = jax.ShapeDtypeStruct((lay.parcel(blocks), head_dim), jnp.bfloat16)
        return pl.pallas_call(
            functools.partial(attend_kernel, (na, nb, nt, way, width), lay),
            grid=(1,),
            out_shape=(out,) * n_out,
            in_specs=[pl.BlockSpec(memory_space=pltpu.SMEM)]
            + [full_spec(x) for x in q_blocks]
            + [full_spec(metas), page_spec, page_spec],
            out_specs=(full_spec(out),) * n_out,
            scratch_shapes=[
                pltpu.VMEM((requests, page), jnp.float32),
                pltpu.VMEM((nt, rows, head_dim), jnp.float32),
                pltpu.VMEM((nt, rows, head_dim), jnp.float32),
                pltpu.VMEM((nt, rows, head_dim), jnp.float32),
                pltpu.VMEM((n_out, lse_lines, LANES), jnp.float32),
                pltpu.VMEM((tail_rows(blocks, lay.lse_rows), LANES), jnp.float32),
            ],
            compiler_params=params(),
            name="attend",
        )(lists, *q_blocks, metas, own_split, other_split)

    def merge(parcels, blocks, parts):
        n = len(parcels)
        each = blocks // parts
        out = jax.ShapeDtypeStruct((lay.parcel(each), head_dim), jnp.bfloat16)
        return pl.pallas_call(
            functools.partial(merge_kernel, n, blocks, parts, lay),
            out_shape=(out,) * parts,
            in_specs=vmem(n),
            out_specs=tuple(vmem(parts)),
            scratch_shapes=[
                pltpu.VMEM((n, blocks * lay.lse_rows, LANES), jnp.float32),
                pltpu.VMEM((blocks * lay.lse_rows, LANES), jnp.float32),
                pltpu.VMEM((tail_rows(blocks, lay.lse_rows), LANES), jnp.float32),
                pltpu.VMEM((tail_rows(each, lay.lse_rows), LANES), jnp.float32),
            ],
            compiler_params=params(),
            name="merge",
        )(*parcels)

    def send_back(parcels, axis):
        return [parcels[0]] + [shift(parcels[by], axis, -by) for by in range(1, len(parcels))]

    arrived = []
    for k in range(heads):
        outer, inner = ("t", "b") if orders[k] == "b" else ("b", "t")
        parcels = send_back(attend(k), outer)
        blocks = na * sizes[inner]
        parcels = send_back(merge(parcels, blocks, sizes[inner]), inner)
        arrived += send_back(merge(parcels, na, na), "a")

    result = pl.pallas_call(
        functools.partial(final_kernel, na, heads, lay),
        out_shape=jax.ShapeDtypeStruct((heads, rows, head_dim), queries.dtype),
        in_specs=vmem(len(arrived) + 2),
        out_specs=vmem(1)[0],
        scratch_shapes=[
            pltpu.VMEM((na + 1, lay.lse_rows, LANES), jnp.float32),
            pltpu.VMEM((tail_rows(1, lay.lse_rows), LANES), jnp.float32),
        ],
        compiler_params=params(),
        name="final",
    )(*arrived, local, local_lse)
    return result.reshape(heads, groups, requests, head_dim).transpose(2, 0, 1, 3)


def solution(mesh):
    return jax.shard_map(
        on_device,
        mesh=mesh,
        in_specs=(
            P(("inst", "tp"), None, None, None),
            P("inst"),
            P("inst", "tp", None, None),
            P("inst", "tp", None, None),
            P("inst", "tp", None),
            P("inst", None),
            P("inst"),
        ),
        out_specs=P("inst", "tp", None, None),
        check_vma=False,
    )
```

time: 504 us -> 175 us (0.35)
  the two profiles are of different devices: /device:TPU:13 before, /device:TPU:0 now
where the time goes in v1:
time: 175 us; the launch traced here: 173 us
  Pallas kernels  56.2 us (32%)
  waiting for transfers between devices  49.1 us (28%)
  starting transfers between devices  47.6 us (27%)
  local copies, waits for them, and re-layouts  14.8 us (8%)
  other arithmetic  4.81 us (3%)
    ppermute x34, waiting for transfers between devices, shift(): return lax.ppermute(x, 'inst', pairs)  41 us
    ppermute x34, starting transfers between devices, shift(): return lax.ppermute(x, 'inst', pairs)  39.1 us
    pallas_call x4, Pallas kernels, attend(): pl.pallas_call(functools.partial(attend_kernel, (na, nb, nt, way, width),...  30.4 us
    pallas_call x8, Pallas kernels, merge(): pl.pallas_call(functools.partial(merge_kernel, n, blocks, parts, lay), ou...  18.7 us
    ppermute x8, starting transfers between devices, shift(): return lax.ppermute(x, 'tp', [(i, (i + by) % nt) for i in range(nt)])  8.52 us
    ppermute x8, waiting for transfers between devices, shift(): return lax.ppermute(x, 'tp', [(i, (i + by) % nt) for i in range(nt)])  8.18 us
    unnamed x73, local copies, waits for them, and re-layouts  7.93 us
    pallas_call x1, Pallas kernels, on_device(): pl.pallas_call(functools.partial(resident_kernel, lay), out_shape=(jax.Sh...  4.5 us
  transfers between devices with their start and end apart: 42, of which 12 were waited for; matrix products, arithmetic and copies ran while one was open for 4% of the time, Pallas kernels for 31%

profile of v1, /device:TPU:0, one launch (start us, length us, event | category | flops | bytes accessed | tf_op | source)
XLA Modules:
  0.0 173.0 jit_solution(11065829772973832530)
XLA Ops:
  3.8 3.1 %collective-permute-start.1 = (bf16[192,128]{1,0:T(8,128)(2,1)S(1)}, bf16[192,128]{1,0:T(8,128)(2,1)S(1)}, u32[]{:S(2)}, u32[]{:S(2)}) collective-permute-start(bf16[192,128]{1,0:T(8,128)(2,1)S(1)} %get-tuple-element.83), channel_id=1, source_target_pairs={{0,8},{2,10},{4,12},{6,14},{8,16},{10,18},{12,20},{14,22},{16,24},... | collective-permute-start | bytes 147464 | tf_op jit(solution)/shard_map/ppermute | solution.py:316
  6.9 2.6 %collective-permute-start.2 = (bf16[192,128]{1,0:T(8,128)(2,1)S(1)}, bf16[192,128]{1,0:T(8,128)(2,1)S(1)}, u32[]{:S(2)}, u32[]{:S(2)}) collective-permute-start(bf16[192,128]{1,0:T(8,128)(2,1)S(1)} %get-tuple-element.83), channel_id=1, source_target_pairs={{0,16},{2,18},{4,20},{6,22},{8,24},{10,26},{12,28},{14,30},{16,0},... | collective-permute-start | bytes 147464 | tf_op jit(solution)/shard_map/ppermute | solution.py:316
  14.6 4.8 %collective-permute-done.12 = bf16[160,128]{1,0:T(8,128)(2,1)S(1)} collective-permute-done((bf16[160,128]{1,0:T(8,128)(2,1)S(1)}, bf16[160,128]{1,0:T(8,128)(2,1)S(1)}, u32[]{:S(2)}, u32[]{:S(2)}) %collective-permute-start.12) | collective-permute-done | bytes 40992 | tf_op jit(solution)/shard_map/ppermute | solution.py:316
  19.5 4.9 %collective-permute-done.13 = bf16[160,128]{1,0:T(8,128)(2,1)S(1)} collective-permute-done((bf16[160,128]{1,0:T(8,128)(2,1)S(1)}, bf16[160,128]{1,0:T(8,128)(2,1)S(1)}, u32[]{:S(2)}, u32[]{:S(2)}) %collective-permute-start.13) | collective-permute-done | bytes 40992 | tf_op jit(solution)/shard_map/ppermute | solution.py:316
  24.4 4.0 %collective-permute-done.14 = bf16[160,128]{1,0:T(8,128)(2,1)S(1)} collective-permute-done((bf16[160,128]{1,0:T(8,128)(2,1)S(1)}, bf16[160,128]{1,0:T(8,128)(2,1)S(1)}, u32[]{:S(2)}, u32[]{:S(2)}) %collective-permute-start.14) | collective-permute-done | bytes 40992 | tf_op jit(solution)/shard_map/ppermute | solution.py:316
  28.4 5.9 %collective-permute-done.22 = bf16[160,128]{1,0:T(8,128)(2,1)S(1)} collective-permute-done((bf16[160,128]{1,0:T(8,128)(2,1)S(1)}, bf16[160,128]{1,0:T(8,128)(2,1)S(1)}, u32[]{:S(2)}, u32[]{:S(2)}) %collective-permute-start.22) | collective-permute-done | bytes 40992 | tf_op jit(solution)/shard_map/ppermute | solution.py:316
  34.3 4.9 %collective-permute-done.23 = bf16[160,128]{1,0:T(8,128)(2,1)S(1)} collective-permute-done((bf16[160,128]{1,0:T(8,128)(2,1)S(1)}, bf16[160,128]{1,0:T(8,128)(2,1)S(1)}, u32[]{:S(2)}, u32[]{:S(2)}) %collective-permute-start.23) | collective-permute-done | bytes 40992 | tf_op jit(solution)/shard_map/ppermute | solution.py:316
  40.4 2.8 %collective-permute-done.24 = bf16[160,128]{1,0:T(8,128)(2,1)S(1)} collective-permute-done((bf16[160,128]{1,0:T(8,128)(2,1)S(1)}, bf16[160,128]{1,0:T(8,128)(2,1)S(1)}, u32[]{:S(2)}, u32[]{:S(2)}) %collective-permute-start.24) | collective-permute-done | bytes 40992 | tf_op jit(solution)/shard_map/ppermute | solution.py:316
  43.2 5.9 %collective-permute-done.32 = bf16[160,128]{1,0:T(8,128)(2,1)S(1)} collective-permute-done((bf16[160,128]{1,0:T(8,128)(2,1)S(1)}, bf16[160,128]{1,0:T(8,128)(2,1)S(1)}, u32[]{:S(2)}, u32[]{:S(2)}) %collective-permute-start.32) | collective-permute-done | bytes 40992 | tf_op jit(solution)/shard_map/ppermute | solution.py:316
  49.1 4.9 %collective-permute-done.33 = bf16[160,128]{1,0:T(8,128)(2,1)S(1)} collective-permute-done((bf16[160,128]{1,0:T(8,128)(2,1)S(1)}, bf16[160,128]{1,0:T(8,128)(2,1)S(1)}, u32[]{:S(2)}, u32[]{:S(2)}) %collective-permute-start.33) | collective-permute-done | bytes 40992 | tf_op jit(solution)/shard_map/ppermute | solution.py:316
  55.3 2.6 %collective-permute-done.34 = bf16[160,128]{1,0:T(8,128)(2,1)S(1)} collective-permute-done((bf16[160,128]{1,0:T(8,128)(2,1)S(1)}, bf16[160,128]{1,0:T(8,128)(2,1)S(1)}, u32[]{:S(2)}, u32[]{:S(2)}) %collective-permute-start.34) | collective-permute-done | bytes 40992 | tf_op jit(solution)/shard_map/ppermute | solution.py:316
  62.3 2.8 %collective-permute-done.15 = bf16[4,160,128]{2,1,0:T(8,128)(2,1)S(1)} collective-permute-done((bf16[4,160,128]{2,1,0:T(8,128)(2,1)S(1)}, bf16[4,160,128]{2,1,0:T(8,128)(2,1)S(1)}, u32[]{:S(2)}, u32[]{:S(2)}) %collective-permute-start.15) | collective-permute-done | bytes 163872 | tf_op jit(solution)/shard_map/ppermute | solution.py:305
  72.8 5.3 %collective-permute-done.5 = bf16[8,192,128]{2,1,0:T(8,128)(2,1)S(1)} collective-permute-done((bf16[8,192,128]{2,1,0:T(8,128)(2,1)S(1)}, bf16[8,192,128]{2,1,0:T(8,128)(2,1)S(1)}, u32[]{:S(2)}, u32[]{:S(2)}) %collective-permute-start.5) | collective-permute-done | bytes 393248 | tf_op jit(solution)/shard_map/ppermute | solution.py:305
  78.9 7.6 %attend.4 = (bf16[1328,128]{1,0:T(8,128)(2,1)}, bf16[1328,128]{1,0:T(8,128)(2,1)}) custom-call(s32[82]{0:T(128)} %pad_add_fusion.4.lists, bf16[8,160,128]{2,1,0:T(8,128)(2,1)} %slice.74.refs_0_, bf16[8,160,128]{2,1,0:T(8,128)(2,1)} %slice.75.refs_1_, bf16[8,32,128]{2,1,0:T(8,128)(2,1)} %slice.76.refs_2_, bf16[8,2,4,128,256]{4,3,2,1,0:T(8,128)(2,1)} %bitcast.64, ...), custom_call_target="tpu_custom_call" | custom-call | tf_op jit(solution)/shard_map/attend/pallas_call | solution.py:408
  88.8 7.6 %attend.5 = (bf16[1328,128]{1,0:T(8,128)(2,1)}, bf16[1328,128]{1,0:T(8,128)(2,1)}) custom-call(s32[82]{0:T(128)} %pad_add_fusion.4.lists, bf16[8,160,128]{2,1,0:T(8,128)(2,1)} %copy-done.3, bf16[8,160,128]{2,1,0:T(8,128)(2,1)} %copy-done.9, bf16[8,32,128]{2,1,0:T(8,128)(2,1)} %slice.76.refs_2_, bf16[8,2,4,128,256]{4,3,2,1,0:T(8,128)(2,1)} %bitcast.65, ...), custom_call_target="tpu_custom_call" | custom-call | tf_op jit(solution)/shard_map/attend/pallas_call | solution.py:408
  97.1 7.6 %attend.6 = (bf16[1328,128]{1,0:T(8,128)(2,1)}, bf16[1328,128]{1,0:T(8,128)(2,1)}) custom-call(s32[82]{0:T(128)} %pad_add_fusion.4.lists, bf16[8,160,128]{2,1,0:T(8,128)(2,1)} %copy-done.2, bf16[8,160,128]{2,1,0:T(8,128)(2,1)} %copy-done.8, bf16[8,32,128]{2,1,0:T(8,128)(2,1)} %slice.76.refs_2_, bf16[8,2,4,128,256]{4,3,2,1,0:T(8,128)(2,1)} %bitcast.66, ...), custom_call_target="tpu_custom_call" | custom-call | tf_op jit(solution)/shard_map/attend/pallas_call | solution.py:408
  106.0 7.6 %attend.7 = (bf16[1328,128]{1,0:T(8,128)(2,1)}, bf16[1328,128]{1,0:T(8,128)(2,1)}) custom-call(s32[82]{0:T(128)} %pad_add_fusion.4.lists, bf16[8,160,128]{2,1,0:T(8,128)(2,1)} %copy-done.1, bf16[8,160,128]{2,1,0:T(8,128)(2,1)} %copy-done.10, bf16[8,32,128]{2,1,0:T(8,128)(2,1)} %slice.76.refs_2_, bf16[8,2,4,128,256]{4,3,2,1,0:T(8,128)(2,1)} %bitcast.67, ...), custom_call_target="tpu_custom_call" | custom-call | tf_op jit(solution)/shard_map/attend/pallas_call | solution.py:408
  115.1 2.8 %merge.8 = (bf16[672,128]{1,0:T(8,128)(2,1)}, bf16[672,128]{1,0:T(8,128)(2,1)}) custom-call(bf16[1328,128]{1,0:T(8,128)(2,1)} %get-tuple-element.39.refs_0_, bf16[1328,128]{1,0:T(8,128)(2,1)} %copy-done.7), custom_call_target="tpu_custom_call" | custom-call | tf_op jit(solution)/shard_map/merge/pallas_call | solution.py:432
  119.9 2.8 %merge.10 = (bf16[672,128]{1,0:T(8,128)(2,1)}, bf16[672,128]{1,0:T(8,128)(2,1)}) custom-call(bf16[1328,128]{1,0:T(8,128)(2,1)} %get-tuple-element.47.refs_0_, bf16[1328,128]{1,0:T(8,128)(2,1)} %copy-done.6), custom_call_target="tpu_custom_call" | custom-call | tf_op jit(solution)/shard_map/merge/pallas_call | solution.py:432
  125.0 2.8 %merge.12 = (bf16[672,128]{1,0:T(8,128)(2,1)}, bf16[672,128]{1,0:T(8,128)(2,1)}) custom-call(bf16[1328,128]{1,0:T(8,128)(2,1)} %get-tuple-element.55.refs_0_, bf16[1328,128]{1,0:T(8,128)(2,1)} %copy-done.4), custom_call_target="tpu_custom_call" | custom-call | tf_op jit(solution)/shard_map/merge/pallas_call | solution.py:432
  129.2 2.8 %merge.14 = (bf16[672,128]{1,0:T(8,128)(2,1)}, bf16[672,128]{1,0:T(8,128)(2,1)}) custom-call(bf16[1328,128]{1,0:T(8,128)(2,1)} %get-tuple-element.63.refs_0_, bf16[1328,128]{1,0:T(8,128)(2,1)} %copy-done.5), custom_call_target="tpu_custom_call" | custom-call | tf_op jit(solution)/shard_map/merge/pallas_call | solution.py:432
  133.2 1.9 %merge.9 = (bf16[176,128]{1,0:T(8,128)(2,1)}, bf16[176,128]{1,0:T(8,128)(2,1)}, bf16[176,128]{1,0:T(8,128)(2,1)}, bf16[176,128]{1,0:T(8,128)(2,1)}) custom-call(bf16[672,128]{1,0:T(8,128)(2,1)} %get-tuple-element.41.refs_0_, bf16[672,128]{1,0:T(8,128)(2,1)} %copy-done.14), custom_call_target="tpu_custom_call" | custom-call | tf_op jit(solution)/shard_map/merge/pallas_call | solution.py:432
  135.1 3.8 %collective-permute-start.9 = (bf16[176,128]{1,0:T(8,128)(2,1)}, bf16[176,128]{1,0:T(8,128)(2,1)S(1)}, u32[]{:S(2)}, u32[]{:S(2)}) collective-permute-start(bf16[176,128]{1,0:T(8,128)(2,1)} %get-tuple-element.44), channel_id=1, source_target_pairs={{0,24},{2,26},{4,28},{6,30},{8,0},{10,2},{12,4},{14,6},{16,8},{18,... | collective-permute-start | bytes 135176 | tf_op jit(solution)/shard_map/ppermute | solution.py:316
  138.9 3.5 %collective-permute-start.10 = (bf16[176,128]{1,0:T(8,128)(2,1)}, bf16[176,128]{1,0:T(8,128)(2,1)S(1)}, u32[]{:S(2)}, u32[]{:S(2)}) collective-permute-start(bf16[176,128]{1,0:T(8,128)(2,1)} %get-tuple-element.45), channel_id=1, source_target_pairs={{0,16},{2,18},{4,20},{6,22},{8,24},{10,26},{12,28},{14,30},{16,0},... | collective-permute-start | bytes 135176 | tf_op jit(solution)/shard_map/ppermute | solution.py:316
  142.4 2.0 %collective-permute-start.11 = (bf16[176,128]{1,0:T(8,128)(2,1)}, bf16[176,128]{1,0:T(8,128)(2,1)S(1)}, u32[]{:S(2)}, u32[]{:S(2)}) collective-permute-start(bf16[176,128]{1,0:T(8,128)(2,1)} %get-tuple-element.46), channel_id=1, source_target_pairs={{0,8},{2,10},{4,12},{6,14},{8,16},{10,18},{12,20},{14,22},{16,24},... | collective-permute-start | bytes 135176 | tf_op jit(solution)/shard_map/ppermute | solution.py:316
  144.4 1.9 %merge.11 = (bf16[176,128]{1,0:T(8,128)(2,1)}, bf16[176,128]{1,0:T(8,128)(2,1)}, bf16[176,128]{1,0:T(8,128)(2,1)}, bf16[176,128]{1,0:T(8,128)(2,1)}) custom-call(bf16[672,128]{1,0:T(8,128)(2,1)} %get-tuple-element.49.refs_0_, bf16[672,128]{1,0:T(8,128)(2,1)} %copy-done.13), custom_call_target="tpu_custom_call" | custom-call | tf_op jit(solution)/shard_map/merge/pallas_call | solution.py:432
  148.2 1.9 %merge.13 = (bf16[176,128]{1,0:T(8,128)(2,1)}, bf16[176,128]{1,0:T(8,128)(2,1)}, bf16[176,128]{1,0:T(8,128)(2,1)}, bf16[176,128]{1,0:T(8,128)(2,1)}) custom-call(bf16[672,128]{1,0:T(8,128)(2,1)} %get-tuple-element.57.refs_0_, bf16[672,128]{1,0:T(8,128)(2,1)} %copy-done.12), custom_call_target="tpu_custom_call" | custom-call | tf_op jit(solution)/shard_map/merge/pallas_call | solution.py:432
  151.3 3.0 %collective-permute-start.29 = (bf16[176,128]{1,0:T(8,128)(2,1)}, bf16[176,128]{1,0:T(8,128)(2,1)S(1)}, u32[]{:S(2)}, u32[]{:S(2)}) collective-permute-start(bf16[176,128]{1,0:T(8,128)(2,1)} %get-tuple-element.60), channel_id=1, source_target_pairs={{0,24},{2,26},{4,28},{6,30},{8,0},{10,2},{12,4},{14,6},{16,8},{18,... | collective-permute-start | bytes 135176 | tf_op jit(solution)/shard_map/ppermute | solution.py:316
  154.3 1.9 %merge.15 = (bf16[176,128]{1,0:T(8,128)(2,1)}, bf16[176,128]{1,0:T(8,128)(2,1)}, bf16[176,128]{1,0:T(8,128)(2,1)}, bf16[176,128]{1,0:T(8,128)(2,1)}) custom-call(bf16[672,128]{1,0:T(8,128)(2,1)} %get-tuple-element.65.refs_0_, bf16[672,128]{1,0:T(8,128)(2,1)} %copy-done.11), custom_call_target="tpu_custom_call" | custom-call | tf_op jit(solution)/shard_map/merge/pallas_call | solution.py:432
  157.3 3.6 %collective-permute-start.39 = (bf16[176,128]{1,0:T(8,128)(2,1)}, bf16[176,128]{1,0:T(8,128)(2,1)S(1)}, u32[]{:S(2)}, u32[]{:S(2)}) collective-permute-start(bf16[176,128]{1,0:T(8,128)(2,1)} %get-tuple-element.68), channel_id=1, source_target_pairs={{0,24},{2,26},{4,28},{6,30},{8,0},{10,2},{12,4},{14,6},{16,8},{18,... | collective-permute-start | bytes 135176 | tf_op jit(solution)/shard_map/ppermute | solution.py:316
  163.5 4.5 %resident.1 = (f32[4,160,128]{2,1,0:T(8,128)}, f32[8,128]{1,0:T(8,128)}) custom-call(bf16[4,160,128]{2,1,0:T(8,128)(2,1)} %bitcast.70, bf16[8,4,128,256]{3,2,1,0:T(8,128)(2,1)} %pages.1, bf16[4,32,256]{2,1,0:T(8,128)(2,1)} %bitcast.89, bf16[32,128]{1,0:T(8,128)(2,1)} %fusion.10.meta), custom_call_target="tpu_custom_call" | custom-call | tf_op jit(solution)/shard_map/resident/pallas_call | solution.py:381
  168.7 2.6 %final.1 = bf16[4,160,128]{2,1,0:T(8,128)(2,1)} custom-call(bf16[176,128]{1,0:T(8,128)(2,1)} %get-tuple-element.43.refs_0_, bf16[176,128]{1,0:T(8,128)(2,1)} %copy-done.16, bf16[176,128]{1,0:T(8,128)(2,1)} %copy-done.17, bf16[176,128]{1,0:T(8,128)(2,1)} %copy-done.18, bf16[176,128]{1,0:T(8,128)(2,1)} %get-tuple-element.51.refs_4_, ...), custom_call_target="tpu_custom_call" | custom-call | tf_op jit(solution)/shard_map/final/pallas_call | solution.py:458
  (188 shorter events, 45.9 us)
Async XLA Ops:
  3.8 55.7 %collective-permute-start.1 = (bf16[192,128]{1,0:T(8,128)(2,1)S(1)}, bf16[192,128]{1,0:T(8,128)(2,1)S(1)}, u32[]{:S(2)}, u32[]{:S(2)}) collective-permute-start(bf16[192,128]{1,0:T(8,128)(2,1)S(1)} %get-tuple-element.83), channel_id=1, source_target_pairs={{0,8},{2,10},{4,12},{6,14},{8,16},{10,18},{12,20},{14,22},{16,24},... | collective-permute-start | bytes 147464 | tf_op jit(solution)/shard_map/ppermute | solution.py:316
  6.9 54.2 %collective-permute-start.2 = (bf16[192,128]{1,0:T(8,128)(2,1)S(1)}, bf16[192,128]{1,0:T(8,128)(2,1)S(1)}, u32[]{:S(2)}, u32[]{:S(2)}) collective-permute-start(bf16[192,128]{1,0:T(8,128)(2,1)S(1)} %get-tuple-element.83), channel_id=1, source_target_pairs={{0,16},{2,18},{4,20},{6,22},{8,24},{10,26},{12,28},{14,30},{16,0},... | collective-permute-start | bytes 147464 | tf_op jit(solution)/shard_map/ppermute | solution.py:316
  9.5 52.1 %collective-permute-start.3 = (bf16[192,128]{1,0:T(8,128)(2,1)S(1)}, bf16[192,128]{1,0:T(8,128)(2,1)S(1)}, u32[]{:S(2)}, u32[]{:S(2)}) collective-permute-start(bf16[192,128]{1,0:T(8,128)(2,1)S(1)} %get-tuple-element.83), channel_id=1, source_target_pairs={{0,24},{2,26},{4,28},{6,30},{8,0},{10,2},{12,4},{14,6},{16,8},{18,... | collective-permute-start | bytes 147464 | tf_op jit(solution)/shard_map/ppermute | solution.py:316
  12.5 66.3 %collective-permute-start.6 = (bf16[8,8,128,256]{3,2,1,0:T(8,128)(2,1)}, bf16[8,8,128,256]{3,2,1,0:T(8,128)(2,1)}, u32[]{:S(2)}, u32[]{:S(2)}) collective-permute-start(bf16[8,8,128,256]{3,2,1,0:T(8,128)(2,1)} %param.7), channel_id=1, source_target_pairs={{0,2},{2,0},{4,6},{6,4},{8,10},{10,8},{12,14},{14,12},{16,18},{18,... | collective-permute-start | bytes 12582920 | tf_op jit(solution)/shard_map/ppermute | solution.py:316
  58.0 7.1 %collective-permute-start.15 = (bf16[4,160,128]{2,1,0:T(8,128)(2,1)S(1)}, bf16[4,160,128]{2,1,0:T(8,128)(2,1)S(1)}, u32[]{:S(2)}, u32[]{:S(2)}) collective-permute-start(bf16[4,160,128]{2,1,0:T(8,128)(2,1)S(1)} %pad_maximum_fusion.1), channel_id=1, source_target_pairs={{0,1},{1,0},{2,3},{3,2},{4,5},{5,4},{6,7},{7,6},{8,9},{9,8},{10,11... | collective-permute-start | bytes 491528 | tf_op jit(solution)/shard_map/ppermute | solution.py:305
  59.5 7.2 %collective-permute-start.25 = (bf16[4,160,128]{2,1,0:T(8,128)(2,1)S(1)}, bf16[4,160,128]{2,1,0:T(8,128)(2,1)S(1)}, u32[]{:S(2)}, u32[]{:S(2)}) collective-permute-start(bf16[4,160,128]{2,1,0:T(8,128)(2,1)S(1)} %pad_maximum_fusion.2), channel_id=1, source_target_pairs={{0,4},{2,6},{4,0},{6,2},{8,12},{10,14},{12,8},{14,10},{16,20},{18,... | collective-permute-start | bytes 491528 | tf_op jit(solution)/shard_map/ppermute | solution.py:316
  61.1 8.1 %collective-permute-start.35 = (bf16[4,160,128]{2,1,0:T(8,128)(2,1)S(1)}, bf16[4,160,128]{2,1,0:T(8,128)(2,1)S(1)}, u32[]{:S(2)}, u32[]{:S(2)}) collective-permute-start(bf16[4,160,128]{2,1,0:T(8,128)(2,1)S(1)} %pad_maximum_fusion.3), channel_id=1, source_target_pairs={{0,1},{1,0},{2,3},{3,2},{4,5},{5,4},{6,7},{7,6},{8,9},{9,8},{10,11... | collective-permute-start | bytes 491528 | tf_op jit(solution)/shard_map/ppermute | solution.py:305
  61.7 6.7 %collective-permute-start.4 = (bf16[4,192,128]{2,1,0:T(8,128)(2,1)S(1)}, bf16[4,192,128]{2,1,0:T(8,128)(2,1)S(1)}, u32[]{:S(2)}, u32[]{:S(2)}) collective-permute-start(bf16[4,192,128]{2,1,0:T(8,128)(2,1)S(1)} %pad_maximum_fusion), channel_id=1, source_target_pairs={{0,4},{2,6},{4,0},{6,2},{8,12},{10,14},{12,8},{14,10},{16,20},{18,... | collective-permute-start | bytes 589832 | tf_op jit(solution)/shard_map/ppermute | solution.py:316
  65.1 22.9 %collective-permute-start.16 = (bf16[8,160,128]{2,1,0:T(8,128)(2,1)S(1)}, bf16[8,160,128]{2,1,0:T(8,128)(2,1)S(1)}, u32[]{:S(2)}, u32[]{:S(2)}) collective-permute-start(bf16[8,160,128]{2,1,0:T(8,128)(2,1)S(1)} %constant_dynamic-update-slice_fusion.5.refs_0_), channel_id=1, source_target_pairs={{0,4},{2,6},{4,0},{6,2},{8,12},{10,14},{12,8},{14,10},{16,20},{18,... | collective-permute-start | bytes 983048 | tf_op jit(solution)/shard_map/ppermute | solution.py:316
  66.8 29.6 %collective-permute-start.26 = (bf16[8,160,128]{2,1,0:T(8,128)(2,1)S(1)}, bf16[8,160,128]{2,1,0:T(8,128)(2,1)S(1)}, u32[]{:S(2)}, u32[]{:S(2)}) collective-permute-start(bf16[8,160,128]{2,1,0:T(8,128)(2,1)S(1)} %constant_dynamic-update-slice_fusion.10.refs_0_), channel_id=1, source_target_pairs={{0,1},{1,0},{2,3},{3,2},{4,5},{5,4},{6,7},{7,6},{8,9},{9,8},{10,11... | collective-permute-start | bytes 983048 | tf_op jit(solution)/shard_map/ppermute | solution.py:305
  68.4 9.8 %collective-permute-start.5 = (bf16[8,192,128]{2,1,0:T(8,128)(2,1)S(1)}, bf16[8,192,128]{2,1,0:T(8,128)(2,1)S(1)}, u32[]{:S(2)}, u32[]{:S(2)}) collective-permute-start(bf16[8,192,128]{2,1,0:T(8,128)(2,1)S(1)} %constant_dynamic-update-slice_fusion), channel_id=1, source_target_pairs={{0,1},{1,0},{2,3},{3,2},{4,5},{5,4},{6,7},{7,6},{8,9},{9,8},{10,11... | collective-permute-start | bytes 1179656 | tf_op jit(solution)/shard_map/ppermute | solution.py:305
  69.2 36.0 %collective-permute-start.36 = (bf16[8,160,128]{2,1,0:T(8,128)(2,1)S(1)}, bf16[8,160,128]{2,1,0:T(8,128)(2,1)S(1)}, u32[]{:S(2)}, u32[]{:S(2)}) collective-permute-start(bf16[8,160,128]{2,1,0:T(8,128)(2,1)S(1)} %constant_dynamic-update-slice_fusion.15.refs_0_), channel_id=1, source_target_pairs={{0,4},{2,6},{4,0},{6,2},{8,12},{10,14},{12,8},{14,10},{16,20},{18,... | collective-permute-start | bytes 983048 | tf_op jit(solution)/shard_map/ppermute | solution.py:316
  86.5 27.9 %collective-permute-start.7 = (bf16[1328,128]{1,0:T(8,128)(2,1)}, bf16[1328,128]{1,0:T(8,128)(2,1)S(1)}, u32[]{:S(2)}, u32[]{:S(2)}) collective-permute-start(bf16[1328,128]{1,0:T(8,128)(2,1)} %get-tuple-element.40), channel_id=1, source_target_pairs={{0,1},{1,0},{2,3},{3,2},{4,5},{5,4},{6,7},{7,6},{8,9},{9,8},{10,11... | collective-permute-start | bytes 1019912 | tf_op jit(solution)/shard_map/ppermute | solution.py:305
  96.4 22.8 %collective-permute-start.17 = (bf16[1328,128]{1,0:T(8,128)(2,1)}, bf16[1328,128]{1,0:T(8,128)(2,1)S(1)}, u32[]{:S(2)}, u32[]{:S(2)}) collective-permute-start(bf16[1328,128]{1,0:T(8,128)(2,1)} %get-tuple-element.48), channel_id=1, source_target_pairs={{0,4},{2,6},{4,0},{6,2},{8,12},{10,14},{12,8},{14,10},{16,20},{18,... | collective-permute-start | bytes 1019912 | tf_op jit(solution)/shard_map/ppermute | solution.py:316
  104.7 19.5 %collective-permute-start.27 = (bf16[1328,128]{1,0:T(8,128)(2,1)}, bf16[1328,128]{1,0:T(8,128)(2,1)S(1)}, u32[]{:S(2)}, u32[]{:S(2)}) collective-permute-start(bf16[1328,128]{1,0:T(8,128)(2,1)} %get-tuple-element.56), channel_id=1, source_target_pairs={{0,1},{1,0},{2,3},{3,2},{4,5},{5,4},{6,7},{7,6},{8,9},{9,8},{10,11... | collective-permute-start | bytes 1019912 | tf_op jit(solution)/shard_map/ppermute | solution.py:305
  113.6 14.8 %collective-permute-start.37 = (bf16[1328,128]{1,0:T(8,128)(2,1)}, bf16[1328,128]{1,0:T(8,128)(2,1)S(1)}, u32[]{:S(2)}, u32[]{:S(2)}) collective-permute-start(bf16[1328,128]{1,0:T(8,128)(2,1)} %get-tuple-element.64), channel_id=1, source_target_pairs={{0,4},{2,6},{4,0},{6,2},{8,12},{10,14},{12,8},{14,10},{16,20},{18,... | collective-permute-start | bytes 1019912 | tf_op jit(solution)/shard_map/ppermute | solution.py:316
  117.9 14.6 %collective-permute-start.8 = (bf16[672,128]{1,0:T(8,128)(2,1)}, bf16[672,128]{1,0:T(8,128)(2,1)S(1)}, u32[]{:S(2)}, u32[]{:S(2)}) collective-permute-start(bf16[672,128]{1,0:T(8,128)(2,1)} %get-tuple-element.42), channel_id=1, source_target_pairs={{0,4},{2,6},{4,0},{6,2},{8,12},{10,14},{12,8},{14,10},{16,20},{18,... | collective-permute-start | bytes 516104 | tf_op jit(solution)/shard_map/ppermute | solution.py:316
  122.7 19.6 %collective-permute-start.18 = (bf16[672,128]{1,0:T(8,128)(2,1)}, bf16[672,128]{1,0:T(8,128)(2,1)S(1)}, u32[]{:S(2)}, u32[]{:S(2)}) collective-permute-start(bf16[672,128]{1,0:T(8,128)(2,1)} %get-tuple-element.50), channel_id=1, source_target_pairs={{0,1},{1,0},{2,3},{3,2},{4,5},{5,4},{6,7},{7,6},{8,9},{9,8},{10,11... | collective-permute-start | bytes 516104 | tf_op jit(solution)/shard_map/ppermute | solution.py:305
  127.8 18.6 %collective-permute-start.28 = (bf16[672,128]{1,0:T(8,128)(2,1)}, bf16[672,128]{1,0:T(8,128)(2,1)S(1)}, u32[]{:S(2)}, u32[]{:S(2)}) collective-permute-start(bf16[672,128]{1,0:T(8,128)(2,1)} %get-tuple-element.58), channel_id=1, source_target_pairs={{0,4},{2,6},{4,0},{6,2},{8,12},{10,14},{12,8},{14,10},{16,20},{18,... | collective-permute-start | bytes 516104 | tf_op jit(solution)/shard_map/ppermute | solution.py:316
  132.0 18.1 %collective-permute-start.38 = (bf16[672,128]{1,0:T(8,128)(2,1)}, bf16[672,128]{1,0:T(8,128)(2,1)S(1)}, u32[]{:S(2)}, u32[]{:S(2)}) collective-permute-start(bf16[672,128]{1,0:T(8,128)(2,1)} %get-tuple-element.66), channel_id=1, source_target_pairs={{0,1},{1,0},{2,3},{3,2},{4,5},{5,4},{6,7},{7,6},{8,9},{9,8},{10,11... | collective-permute-start | bytes 516104 | tf_op jit(solution)/shard_map/ppermute | solution.py:305
  135.1 15.4 %collective-permute-start.9 = (bf16[176,128]{1,0:T(8,128)(2,1)}, bf16[176,128]{1,0:T(8,128)(2,1)S(1)}, u32[]{:S(2)}, u32[]{:S(2)}) collective-permute-start(bf16[176,128]{1,0:T(8,128)(2,1)} %get-tuple-element.44), channel_id=1, source_target_pairs={{0,24},{2,26},{4,28},{6,30},{8,0},{10,2},{12,4},{14,6},{16,8},{18,... | collective-permute-start | bytes 135176 | tf_op jit(solution)/shard_map/ppermute | solution.py:316
  138.9 12.4 %collective-permute-start.10 = (bf16[176,128]{1,0:T(8,128)(2,1)}, bf16[176,128]{1,0:T(8,128)(2,1)S(1)}, u32[]{:S(2)}, u32[]{:S(2)}) collective-permute-start(bf16[176,128]{1,0:T(8,128)(2,1)} %get-tuple-element.45), channel_id=1, source_target_pairs={{0,16},{2,18},{4,20},{6,22},{8,24},{10,26},{12,28},{14,30},{16,0},... | collective-permute-start | bytes 135176 | tf_op jit(solution)/shard_map/ppermute | solution.py:316
  142.4 13.8 %collective-permute-start.11 = (bf16[176,128]{1,0:T(8,128)(2,1)}, bf16[176,128]{1,0:T(8,128)(2,1)S(1)}, u32[]{:S(2)}, u32[]{:S(2)}) collective-permute-start(bf16[176,128]{1,0:T(8,128)(2,1)} %get-tuple-element.46), channel_id=1, source_target_pairs={{0,8},{2,10},{4,12},{6,14},{8,16},{10,18},{12,20},{14,22},{16,24},... | collective-permute-start | bytes 135176 | tf_op jit(solution)/shard_map/ppermute | solution.py:316
  146.3 10.7 %collective-permute-start.19 = (bf16[176,128]{1,0:T(8,128)(2,1)}, bf16[176,128]{1,0:T(8,128)(2,1)S(1)}, u32[]{:S(2)}, u32[]{:S(2)}) collective-permute-start(bf16[176,128]{1,0:T(8,128)(2,1)} %get-tuple-element.52), channel_id=1, source_target_pairs={{0,24},{2,26},{4,28},{6,30},{8,0},{10,2},{12,4},{14,6},{16,8},{18,... | collective-permute-start | bytes 135176 | tf_op jit(solution)/shard_map/ppermute | solution.py:316
  150.1 7.2 %collective-permute-start.20 = (bf16[176,128]{1,0:T(8,128)(2,1)}, bf16[176,128]{1,0:T(8,128)(2,1)S(1)}, u32[]{:S(2)}, u32[]{:S(2)}) collective-permute-start(bf16[176,128]{1,0:T(8,128)(2,1)} %get-tuple-element.53), channel_id=1, source_target_pairs={{0,16},{2,18},{4,20},{6,22},{8,24},{10,26},{12,28},{14,30},{16,0},... | collective-permute-start | bytes 135176 | tf_op jit(solution)/shard_map/ppermute | solution.py:316
  150.4 10.4 %collective-permute-start.21 = (bf16[176,128]{1,0:T(8,128)(2,1)}, bf16[176,128]{1,0:T(8,128)(2,1)S(1)}, u32[]{:S(2)}, u32[]{:S(2)}) collective-permute-start(bf16[176,128]{1,0:T(8,128)(2,1)} %get-tuple-element.54), channel_id=1, source_target_pairs={{0,8},{2,10},{4,12},{6,14},{8,16},{10,18},{12,20},{14,22},{16,24},... | collective-permute-start | bytes 135176 | tf_op jit(solution)/shard_map/ppermute | solution.py:316
  151.3 9.9 %collective-permute-start.29 = (bf16[176,128]{1,0:T(8,128)(2,1)}, bf16[176,128]{1,0:T(8,128)(2,1)S(1)}, u32[]{:S(2)}, u32[]{:S(2)}) collective-permute-start(bf16[176,128]{1,0:T(8,128)(2,1)} %get-tuple-element.60), channel_id=1, source_target_pairs={{0,24},{2,26},{4,28},{6,30},{8,0},{10,2},{12,4},{14,6},{16,8},{18,... | collective-permute-start | bytes 135176 | tf_op jit(solution)/shard_map/ppermute | solution.py:316
  156.2 11.9 %collective-permute-start.30 = (bf16[176,128]{1,0:T(8,128)(2,1)}, bf16[176,128]{1,0:T(8,128)(2,1)S(1)}, u32[]{:S(2)}, u32[]{:S(2)}) collective-permute-start(bf16[176,128]{1,0:T(8,128)(2,1)} %get-tuple-element.61), channel_id=1, source_target_pairs={{0,16},{2,18},{4,20},{6,22},{8,24},{10,26},{12,28},{14,30},{16,0},... | collective-permute-start | bytes 135176 | tf_op jit(solution)/shard_map/ppermute | solution.py:316
  157.0 11.0 %collective-permute-start.31 = (bf16[176,128]{1,0:T(8,128)(2,1)}, bf16[176,128]{1,0:T(8,128)(2,1)S(1)}, u32[]{:S(2)}, u32[]{:S(2)}) collective-permute-start(bf16[176,128]{1,0:T(8,128)(2,1)} %get-tuple-element.62), channel_id=1, source_target_pairs={{0,8},{2,10},{4,12},{6,14},{8,16},{10,18},{12,20},{14,22},{16,24},... | collective-permute-start | bytes 135176 | tf_op jit(solution)/shard_map/ppermute | solution.py:316
  157.3 10.8 %collective-permute-start.39 = (bf16[176,128]{1,0:T(8,128)(2,1)}, bf16[176,128]{1,0:T(8,128)(2,1)S(1)}, u32[]{:S(2)}, u32[]{:S(2)}) collective-permute-start(bf16[176,128]{1,0:T(8,128)(2,1)} %get-tuple-element.68), channel_id=1, source_target_pairs={{0,24},{2,26},{4,28},{6,30},{8,0},{10,2},{12,4},{14,6},{16,8},{18,... | collective-permute-start | bytes 135176 | tf_op jit(solution)/shard_map/ppermute | solution.py:316
  160.9 7.2 %collective-permute-start.40 = (bf16[176,128]{1,0:T(8,128)(2,1)}, bf16[176,128]{1,0:T(8,128)(2,1)S(1)}, u32[]{:S(2)}, u32[]{:S(2)}) collective-permute-start(bf16[176,128]{1,0:T(8,128)(2,1)} %get-tuple-element.69), channel_id=1, source_target_pairs={{0,16},{2,18},{4,20},{6,22},{8,24},{10,26},{12,28},{14,30},{16,0},... | collective-permute-start | bytes 135176 | tf_op jit(solution)/shard_map/ppermute | solution.py:316
  161.2 6.9 %collective-permute-start.41 = (bf16[176,128]{1,0:T(8,128)(2,1)}, bf16[176,128]{1,0:T(8,128)(2,1)S(1)}, u32[]{:S(2)}, u32[]{:S(2)}) collective-permute-start(bf16[176,128]{1,0:T(8,128)(2,1)} %get-tuple-element.70), channel_id=1, source_target_pairs={{0,8},{2,10},{4,12},{6,14},{8,16},{10,18},{12,20},{14,22},{16,24},... | collective-permute-start | bytes 135176 | tf_op jit(solution)/shard_map/ppermute | solution.py:316
  (38 other events, 301.4 us)

commit v2 on v0

v2 whole, which is shorter than its diff:
```python
import functools
import math

import jax
import jax.numpy as jnp
from jax import lax
from jax.experimental import pallas as pl
from jax.experimental.pallas import tpu as pltpu
from jax.sharding import PartitionSpec as P

CAP = 2
Z_WAIT, R_WAIT, A_WAIT, B_WAIT = 2, 3, 3, 2
DIRECT_OUT = (1, 1, 1, 1)
DIRECT_BACK = (1, 1, 1, 1)
LANES = 128
NEG = -1e30
VMEM_LIMIT = 62 * 1024 * 1024


class Layout:
    def __init__(self, heads, groups, requests, head_dim, width):
        self.heads, self.groups, self.requests, self.head_dim = heads, groups, requests, head_dim
        self.per = LANES // requests
        whole = groups - groups % self.per
        runs = [(h, g) for h in range(heads) for g in range(whole)]
        runs += [(h, g) for h in range(heads) for g in range(whole, groups)]
        self.runs = [runs[i : i + self.per] for i in range(0, len(runs), self.per)]
        self.tiles = len(self.runs)
        self.tiles_of = [
            [i for i, tile in enumerate(self.runs) if any(h == head for h, _ in tile)] for head in range(heads)
        ]
        self.width = width
        self.counts = -(-width // self.per)
        self.data = self.tiles * head_dim
        self.count_rows = -(-2 * self.counts // 16) * 16
        self.tail_rows = -(-3 * self.tiles // 16) * 16
        self.query_rows = self.data + self.count_rows
        self.result_rows = self.data + self.tail_rows

    def mine(self, tile, head):
        owners = [h for h, _ in self.runs[tile]]
        if all(h == head for h in owners) and len(owners) == self.per:
            return None
        run = lax.broadcasted_iota(jnp.int32, (1, LANES), 1) // self.requests
        hits = [run == i for i, h in enumerate(owners) if h == head]
        return functools.reduce(jnp.logical_or, hits)


def rows_of(start, count):
    return pl.ds(start if isinstance(start, int) else pl.multiple_of(start, 16), count)


def store_tail(out, start, lse, tail):
    count = lse.shape[0]
    tail[...] = jnp.zeros_like(tail)
    high = lse.astype(jnp.bfloat16).astype(jnp.float32)
    middle = (lse - high).astype(jnp.bfloat16).astype(jnp.float32)
    tail[0:count] = high
    tail[count : 2 * count] = middle
    tail[2 * count : 3 * count] = lse - high - middle
    out[rows_of(start, tail.shape[0])] = tail[...].astype(jnp.bfloat16)


def load_tail(ref, start, count, tail):
    tail[...] = ref[rows_of(start, tail.shape[0])].astype(jnp.float32)
    return tail[0:count] + tail[count : 2 * count] + tail[2 * count : 3 * count]


def weighted(times):
    return jnp.where(times > 0, jnp.log2(jnp.maximum(times, 1.0)), NEG)


def attend_tiles(lay, count, query_tile, keys, values, bias, scores, extra=None):
    unit = math.log2(math.e) * lay.head_dim ** (-0.5)
    shared = {}
    for j in range(count):
        for head in range(lay.heads):
            mine = lay.tiles_of[head]
            got = jnp.dot(
                keys(j, head),
                jnp.concatenate([query_tile(i) for i in mine], axis=1),
                preferred_element_type=jnp.float32,
            )
            for n, i in enumerate(mine):
                part = got[:, n * LANES : (n + 1) * LANES]
                mask = lay.mine(i, head)
                if mask is None:
                    scores[j, i] = part * unit + bias(j)
                elif (j, i) in shared:
                    shared[j, i] = jnp.where(mask, part, shared[j, i])
                else:
                    shared[j, i] = part
        for i in range(lay.tiles):
            if (j, i) in shared:
                scores[j, i] = shared.pop((j, i)) * unit + bias(j)
    weights, totals, highests = {}, [], []
    for i in range(lay.tiles):
        highest = functools.reduce(jnp.maximum, [scores[j, i] for j in range(count)])
        highest = jnp.max(highest, axis=0, keepdims=True)
        if extra is not None:
            highest = jnp.maximum(highest, extra[i])
        total = None
        for j in range(count):
            value = jnp.exp2(scores[j, i] - highest)
            total = value if total is None else total + value
            weights[j, i] = value.astype(jnp.bfloat16)
        totals.append(jnp.sum(total, axis=0, keepdims=True))
        highests.append(highest)
    mixed = [None] * lay.tiles
    for head in range(lay.heads):
        mine = lay.tiles_of[head]
        got = None
        for j in range(count):
            term = lax.dot_general(
                values(j, head),
                jnp.concatenate([weights[j, i] for i in mine], axis=1),
                (((0,), (0,)), ((), ())),
                preferred_element_type=jnp.float32,
            )
            got = term if got is None else got + term
        for n, i in enumerate(mine):
            part = got[:, n * LANES : (n + 1) * LANES]
            mask = lay.mine(i, head)
            mixed[i] = part if mask is None or mixed[i] is None else jnp.where(mask, part, mixed[i])
    return mixed, totals, highests


def prepare_kernel(lay, first_page, page, q_ref, tables, lengths, out, local, wide, table, line):
    per, requests, dim = lay.per, lay.requests, lay.head_dim
    wide[...] = q_ref[...].astype(jnp.float32)
    for i, runs in enumerate(lay.runs):
        parts = [wide[:, g, h, :] for h, g in runs]
        parts += [jnp.zeros((requests, dim), jnp.float32)] * (per - len(runs))
        out[i * dim : (i + 1) * dim] = jnp.concatenate(parts, axis=0).T.astype(jnp.bfloat16)

    def repeat(ref, value):
        ref[...] = jnp.zeros_like(ref)
        ref[:, 0:requests] = value
        value = ref[...]
        step = requests
        while step < LANES:
            value = value + pltpu.roll(value, step, 1)
            step *= 2
        return value

    slots = tables.shape[0]
    turned, length = repeat(table, tables[...]), repeat(line, lengths[...])
    whole, rest = length // page, length % page

    def count(names):
        full = jnp.zeros(names.shape, jnp.float32)
        part = jnp.zeros(names.shape, jnp.float32)
        for m in range(slots):
            named = turned[m : m + 1] == names
            full = full + jnp.where(named & (whole > m), 1.0, 0.0)
            part = part + jnp.where(named & (whole == m), rest, 0).astype(jnp.float32)
        return full, part

    shape = (lay.count_rows // 2, LANES)
    row = lax.broadcasted_iota(jnp.int32, shape, 0)
    run = lax.broadcasted_iota(jnp.int32, shape, 1) // requests
    full, part = count(first_page + row * per + run)
    out[lay.data :] = jnp.concatenate([full, part], axis=0).astype(jnp.bfloat16)
    shape = (local.shape[0] // 2, LANES)
    full, part = count(lax.broadcasted_iota(jnp.int32, shape, 0))
    local[...] = jnp.concatenate([full, part], axis=0)


def attend_kernel(lay, nb, nt, query_at, result_at, lists, *refs):
    n_in, n_out = (1 + max(which for which, _ in at.values()) for at in (query_at, result_at))
    q_refs, refs = refs[:n_in], refs[n_in:]
    own_pages, other_pages = refs[:2]
    outs, refs = refs[2 : 2 + n_out], refs[2 + n_out :]
    query, result, held, q_sems, out_sems, sems, scores, bias, tail = refs
    most = 2 * CAP
    dim = lay.head_dim
    dests = nb
    heads_at = 5 * 2 * dests
    every = list(query_at)

    def query_copy(sb, st):
        which, block = query_at[sb, st]
        source = q_refs[which].at[pl.ds(block * lay.query_rows, lay.query_rows)]
        return pltpu.make_async_copy(source, query.at[sb, st], q_sems.at[sb, st])

    def result_copy(sb, st):
        which, block = result_at[sb, st]
        goal = outs[which].at[pl.ds(block * lay.result_rows, lay.result_rows)]
        return pltpu.make_async_copy(result.at[sb, st], goal, out_sems.at[sb, st])

    def page_copy(dest, source, j):
        base = (source * dests + dest) * 5
        index = lists[base + 1 + j]
        goal = j if source == 0 else lists[dest * 5] + j
        pages = (own_pages, other_pages)[source]
        return pltpu.make_async_copy(pages.at[index], held.at[dest, goal], sems.at[dest, source, j])

    def each_page(dest, what):
        for source in range(2):
            for j in range(CAP):

                @pl.when(j < lists[(source * dests + dest) * 5])
                def _(source=source, j=j):
                    what(page_copy(dest, source, j))

    def start_pages(dest, carry):
        each_page(dest, lambda copy: copy.start())
        return carry

    for at in every:
        query_copy(*at).start()
    lax.fori_loop(0, dests, start_pages, 0)
    for at in every:
        query_copy(*at).wait()

    position = lax.broadcasted_iota(jnp.int32, (held.shape[-2], LANES), 0).astype(jnp.float32)
    run = lax.broadcasted_iota(jnp.int32, (lay.count_rows, LANES), 1) // lay.requests
    row = lax.broadcasted_iota(jnp.int32, (lay.count_rows, LANES), 0)

    def spread(counts, column, kind):
        here = (row == kind * (lay.count_rows // 2) + column // lay.per) & (run == column % lay.per)
        line = jnp.sum(jnp.where(here, counts, 0.0), axis=0, keepdims=True)
        step = lay.requests
        while step < LANES:
            line = line + pltpu.roll(line, step, 1)
            step *= 2
        return line

    def one_dest(dest, carry):
        count_own, count_other = lists[dest * 5], lists[(dests + dest) * 5]
        count = count_own + count_other
        each_page(dest, lambda copy: copy.wait())

        @pl.when(count == 0)
        def _():
            for st in range(nt):
                result[dest, st, 0 : lay.data] = jnp.zeros((lay.data, LANES), jnp.bfloat16)
                store_tail(
                    result.at[dest, st], lay.data, jnp.full((lay.tiles, LANES), NEG, jnp.float32), tail
                )

        for n in range(1, most + 1):

            @pl.when(count == n)
            def _(n=n):
                counts = query[dest, 0, lay.data :].astype(jnp.float32)
                for j in range(n):
                    from_other = (j >= count_own).astype(jnp.int32)
                    column = lists[(from_other * dests + dest) * 5 + 3 + j - from_other * count_own]
                    full = spread(counts, column, 0)
                    part = spread(counts, column, 1)
                    bias[j] = weighted(full + jnp.where(position < part, 1.0, 0.0))
                for st in range(nt):
                    head_at = lists[heads_at + st]
                    mixed, totals, highests = attend_tiles(
                        lay,
                        n,
                        lambda i: query[dest, st, i * dim : (i + 1) * dim],
                        lambda j, h: held[dest, j, head_at, h, :, :dim],
                        lambda j, h: held[dest, j, head_at, h, :, dim:],
                        lambda j: bias[j],
                        scores.at[st % 2],
                    )
                    lse = []
                    for i in range(lay.tiles):
                        result[dest, st, i * dim : (i + 1) * dim] = (mixed[i] * (1.0 / totals[i])).astype(
                            jnp.bfloat16
                        )
                        lse.append(highests[i] + jnp.log2(totals[i]))
                    store_tail(result.at[dest, st], lay.data, jnp.concatenate(lse, axis=0), tail)

        return carry

    lax.fori_loop(0, dests, one_dest, 0)
    for at in every:
        result_copy(*at).start()
    for at in every:
        result_copy(*at).wait()


def mix(lses):
    highest = functools.reduce(jnp.maximum, lses)
    exps = [jnp.exp2(value - highest) for value in lses]
    total = functools.reduce(jnp.add, exps)
    scale = 1.0 / total
    return [value * scale for value in exps], highest + jnp.log2(total)


def merge_kernel(lay, jobs, *refs):
    ins, refs = refs[: sum(n for n, _ in jobs)], refs[sum(n for n, _ in jobs) :]
    outs, tail = refs[: sum(blocks for _, blocks in jobs)], refs[-1]
    dim = lay.head_dim
    for n, blocks in jobs:
        for b in range(blocks):
            start = b * lay.result_rows
            lses = [load_tail(ref, start + lay.data, lay.tiles, tail) for ref in ins[:n]]
            weights, lse = mix(lses)
            for i in range(lay.tiles):
                terms = [
                    weights[k][i : i + 1] * ins[k][start + i * dim : start + (i + 1) * dim].astype(jnp.float32)
                    for k in range(n)
                ]
                outs[b][i * dim : (i + 1) * dim] = functools.reduce(jnp.add, terms).astype(jnp.bfloat16)
            store_tail(outs[b], lay.data, lse, tail)
        ins, outs = ins[n:], outs[blocks:]


def resident_kernel(lay, q_ref, pages, own, counts, out, lse, scores, wide):
    count, page, dim = pages.shape[0], pages.shape[2], lay.head_dim
    unit = math.log2(math.e) * dim ** (-0.5)
    position = lax.broadcasted_iota(jnp.int32, (page, LANES), 0).astype(jnp.float32)
    offset = counts.shape[0] // 2
    biases = [
        weighted(counts[p : p + 1] + jnp.where(position < counts[offset + p : offset + p + 1], 1.0, 0.0))
        for p in range(count)
    ]

    wide[...] = own[...].astype(jnp.float32)

    def own_tile(i, half):
        parts = [wide[:, h, half * dim : (half + 1) * dim] for h, _ in lay.runs[i]]
        parts += [jnp.zeros((lay.requests, dim), jnp.float32)] * (lay.per - len(parts))
        return jnp.concatenate(parts, axis=0).T

    def query_tile(i):
        return q_ref[i * dim : (i + 1) * dim]

    own_scores = [
        jnp.sum(query_tile(i).astype(jnp.float32) * own_tile(i, 0), axis=0, keepdims=True) * unit
        for i in range(lay.tiles)
    ]
    mixed, totals, highests = attend_tiles(
        lay,
        count,
        query_tile,
        lambda j, h: pages[j, h, :, :dim],
        lambda j, h: pages[j, h, :, dim:],
        lambda j: biases[j],
        scores,
        own_scores,
    )
    lse[...] = jnp.zeros_like(lse)
    for i in range(lay.tiles):
        own_weights = jnp.exp2(own_scores[i] - highests[i])
        total = totals[i] + own_weights
        out[i * dim : (i + 1) * dim] = (mixed[i] + own_weights * own_tile(i, 1)) * (1.0 / total)
        lse[i : i + 1] = highests[i] + jnp.log2(total)


def final_kernel(lay, n, *refs):
    ins, refs = refs[:n], refs[n:]
    local, local_lse, out, tail, wide = refs
    dim, requests = lay.head_dim, lay.requests
    lses = [load_tail(ref, lay.data, lay.tiles, tail) for ref in ins]
    lses.append(local_lse[0 : lay.tiles])
    weights, _ = mix(lses)
    for i, runs in enumerate(lay.runs):
        span = slice(i * dim, (i + 1) * dim)
        total = weights[n][i : i + 1] * local[span]
        for k in range(n):
            total = total + weights[k][i : i + 1] * ins[k][span].astype(jnp.float32)
        turned = total.T
        for r, (h, g) in enumerate(runs):
            wide[:, g, h, :] = turned[r * requests : (r + 1) * requests]
    out[...] = wide[...].astype(out.dtype)


def vmem(count):
    return [pl.BlockSpec(memory_space=pltpu.VMEM)] * count


def params():
    return pltpu.CompilerParams(vmem_limit_bytes=VMEM_LIMIT)


def on_device(new_pages, routes, resident, queries, own_kv, tables, lengths):
    n_inst, nt = lax.axis_size("inst"), lax.axis_size("tp")
    half = n_inst // 2
    nb = max(b for b in range(1, half + 1) if half % b == 0 and b * b <= half)
    na = half // nb
    requests, heads, groups, head_dim = queries.shape
    resident_count, page = resident.shape[0], resident.shape[2]
    width = n_inst * CAP
    lay = Layout(heads, groups, requests, head_dim, width)
    me, tp = lax.axis_index("inst"), lax.axis_index("tp")
    core, b_at, a_at = me % 2, me // 2 % nb, me // (2 * nb)

    def shift(x, axis, by):
        if axis == "t":
            return lax.ppermute(x, "tp", [(i, (i + by) % nt) for i in range(nt)])
        pairs = []
        for i in range(n_inst):
            c, b, a = i % 2, i // 2 % nb, i // (2 * nb)
            if axis == "a":
                a = (a + by) % na
            elif axis == "b":
                b = (b + by) % nb
            else:
                c = (c + by) % 2
            pairs.append((i, (a * nb + b) * 2 + c))
        return lax.ppermute(x, "inst", pairs)

    def shift_both(x, by_b, by_t):
        pairs = []
        for i in range(n_inst):
            b = (i // 2 % nb + by_b) % nb
            goal = (i // (2 * nb) * nb + b) * 2 + i % 2
            pairs += [(i * nt + j, goal * nt + (j + by_t) % nt) for j in range(nt)]
        return lax.ppermute(x, ("inst", "tp"), pairs)

    sizes = {"a": na, "b": nb, "t": nt}
    others = [(sb, st) for sb in range(nb) for st in range(nt)][1:]

    def gather(x, axis):
        return [x] + [shift(x, axis, by) for by in range(1, sizes[axis])]

    local_rows = -(-2 * resident_count // 16) * 16
    block, local_counts = pl.pallas_call(
        functools.partial(prepare_kernel, lay, resident_count, page),
        out_shape=(
            jax.ShapeDtypeStruct((lay.query_rows, LANES), jnp.bfloat16),
            jax.ShapeDtypeStruct((local_rows, LANES), jnp.float32),
        ),
        scratch_shapes=[
            pltpu.VMEM((requests, groups, heads, head_dim), jnp.float32),
            pltpu.VMEM((tables.shape[1], LANES), jnp.int32),
            pltpu.VMEM((1, LANES), jnp.int32),
        ],
        compiler_params=params(),
        name="prepare",
    )(queries.transpose(0, 2, 1, 3), tables.T, lengths[None])

    turns = [0] + sorted(range(1, na), key=lambda s: (min(s, na - s), s))
    small = nb * nt <= 4
    ways, back = {}, {}
    for turn, s in enumerate(turns):
        ways[s] = "bt" if small and DIRECT_OUT[turn] else "bt"[turn % 2]
        back[s] = "bt" if small and DIRECT_BACK[turn] else "bt"[turn % 2]
    other = {"b": "t", "t": "b"}

    def tie(x, *after):
        return lax.optimization_barrier((x, *after))[0]

    other_pages = shift(new_pages, "c", 1)
    def gather_first(x, way):
        if way == "bt":
            return [x] + [shift_both(x, sb, st) for sb, st in others]
        return [jnp.concatenate(gather(x, way), axis=0)]

    def gather_second(got, way):
        return got if way == "bt" else gather(got[0], other[way])

    half_way = {0: gather_first(block, ways[0])}
    direct_first = ways[0] == "bt"
    slots = {}
    for turn, s in enumerate(turns[1:]):
        slots[s] = shift(tie(block, half_way[0][1]) if turn >= Z_WAIT and direct_first else block, "a", s)

    local, local_lse = pl.pallas_call(
        functools.partial(resident_kernel, lay),
        out_shape=(
            jax.ShapeDtypeStruct((lay.data, LANES), jnp.float32),
            jax.ShapeDtypeStruct((-(-lay.tiles // 8) * 8, LANES), jnp.float32),
        ),
        scratch_shapes=[
            pltpu.VMEM((resident_count, lay.tiles, page, LANES), jnp.float32),
            pltpu.VMEM(own_kv.shape, jnp.float32),
        ],
        compiler_params=params(),
        name="resident",
    )(block, resident, own_kv, tie(local_counts, other_pages))

    page_count = new_pages.shape[0]
    same = routes[:, None] == routes[None, :]
    total_pages = routes.shape[0]
    earlier = lax.broadcasted_iota(jnp.int32, (total_pages, total_pages), 1) < lax.broadcasted_iota(
        jnp.int32, (total_pages, total_pages), 0
    )
    rank = jnp.sum(jnp.where(same & earlier, 1, 0), axis=1).astype(jnp.int32)
    mine = jnp.stack([routes, me * CAP + rank])
    mine = lax.dynamic_slice_in_dim(mine, tp * page_count, page_count, axis=1)
    mine = tie(mine, other_pages)
    both = jnp.stack([mine, shift(mine, "c", 1)])
    dest_a = (a_at - jnp.arange(na, dtype=jnp.int32)) % na
    dest_b = (b_at - jnp.arange(nb, dtype=jnp.int32)) % nb
    dest = (dest_a[:, None] * nb + dest_b[None, :]) * 2 + core
    hit = both[None, :, 0, None, :] == dest[:, None, :, None]
    place = lax.broadcasted_iota(jnp.int32, hit.shape, 3)
    count = jnp.sum(jnp.where(hit, 1, 0), axis=3)
    index = jnp.stack(
        [jnp.min(jnp.where(hit, place, page_count - 1), axis=3), jnp.max(jnp.where(hit, place, 0), axis=3)], axis=3
    )
    chosen = index[..., None] == lax.broadcasted_iota(jnp.int32, index.shape + (page_count,), 4)
    column = jnp.sum(jnp.where(chosen, both[None, :, 1, None, None, :], 0), axis=4)
    lists = jnp.concatenate([count[..., None], index, column], axis=3).transpose(1, 0, 2, 3).astype(jnp.int32)
    tp_of_slot = (tp - jnp.arange(nt, dtype=jnp.int32)) % nt

    own_split = new_pages.reshape(page_count, nt, heads, page, 2 * head_dim)
    other_split = other_pages.reshape(page_count, nt, heads, page, 2 * head_dim)

    def places(way):
        every = [(sb, st) for sb in range(nb) for st in range(nt)]
        if way == "bt":
            return {(sb, st): (sb * nt + st, 0) for sb, st in every}
        return {(sb, st): (st, sb) if way == "b" else (sb, st) for sb, st in every}

    def attend(s):
        query_at, result_at = places(ways[s]), places(back[s])
        counts = [0] * (1 + max(which for which, _ in result_at.values()))
        for which, _ in result_at.values():
            counts[which] += 1
        return list(
            pl.pallas_call(
                functools.partial(attend_kernel, lay, nb, nt, query_at, result_at),
                out_shape=tuple(
                    jax.ShapeDtypeStruct((count * lay.result_rows, LANES), jnp.bfloat16) for count in counts
                ),
                in_specs=[pl.BlockSpec(memory_space=pltpu.SMEM)]
                + [pl.BlockSpec(memory_space=pl.ANY)] * (len(gathered[s]) + 2),
                out_specs=(pl.BlockSpec(memory_space=pl.ANY),) * len(counts),
                scratch_shapes=[
                    pltpu.VMEM((nb, nt, lay.query_rows, LANES), jnp.bfloat16),
                    pltpu.VMEM((nb, nt, lay.result_rows, LANES), jnp.bfloat16),
                    pltpu.VMEM((nb, 2 * CAP, nt, heads, page, 2 * head_dim), jnp.bfloat16),
                    pltpu.SemaphoreType.DMA((nb, nt)),
                    pltpu.SemaphoreType.DMA((nb, nt)),
                    pltpu.SemaphoreType.DMA((nb, 2, CAP)),
                    pltpu.VMEM((2, 2 * CAP, lay.tiles, page, LANES), jnp.float32),
                    pltpu.VMEM((2 * CAP, page, LANES), jnp.float32),
                    pltpu.VMEM((lay.tail_rows, LANES), jnp.float32),
                ],
                compiler_params=params(),
                cost_estimate=pl.CostEstimate(flops=0, bytes_accessed=16 << 20, transcendentals=0),
                name="attend",
            )(jnp.concatenate([lists[:, s].reshape(-1), tp_of_slot]), *gathered[s], own_split, other_split)
        )

    def merge(arrays, blocks):
        out = jax.ShapeDtypeStruct((lay.result_rows, LANES), jnp.bfloat16)
        jobs = [(len(x), count) for x, count in zip(arrays, blocks)]
        got = pl.pallas_call(
            functools.partial(merge_kernel, lay, jobs),
            out_shape=(out,) * sum(blocks),
            scratch_shapes=[pltpu.VMEM((lay.tail_rows, LANES), jnp.float32)],
            compiler_params=params(),
            name="merge",
        )(*[x for each in arrays for x in each])
        parts = []
        for count in blocks:
            parts.append(list(got[:count]))
            got = got[count:]
        return parts

    def send_back(arrays, axis):
        return [arrays[0]] + [shift(arrays[by], axis, -by) for by in range(1, len(arrays))]

    def go_back(s):
        parts, way = first_back[s], back[s]
        if way == "bt":
            return [parts[0]] + [shift_both(parts[sb * nt + st], -sb, -st) for sb, st in others]
        parts = merge([send_back(parts, other[way])], [sizes[way]])[0]
        return send_back(parts, way)

    gathered, first_back, returned = {0: gather_second(half_way[0], ways[0])}, {}, {}
    first_back[0] = attend(0)
    for turn, s in enumerate(turns):
        if turn > 0:
            start = slots[s] if turn < R_WAIT else tie(slots[s], local_lse)
            start = start if turn < A_WAIT else tie(start, first_back[0][0])
            gathered[s] = gather_second(gather_first(start, ways[s]), ways[s])
    returned[0] = go_back(0)
    for turn, s in enumerate(turns):
        if turn > 0:
            gathered[s][0] = tie(gathered[s][0], first_back[turns[turn - 1]][0])
            if turn == B_WAIT:
                gathered[s][0] = tie(gathered[s][0], *returned[0][1:])
            first_back[s] = attend(s)
    arrived = list(returned[0])
    for s in turns[1:]:
        arrived.append(shift(merge([go_back(s)], [1])[0][0], "a", -s))

    return pl.pallas_call(
        functools.partial(final_kernel, lay, len(arrived)),
        out_shape=jax.ShapeDtypeStruct((requests, groups, heads, head_dim), queries.dtype),
        scratch_shapes=[
            pltpu.VMEM((lay.tail_rows, LANES), jnp.float32),
            pltpu.VMEM((requests, groups, heads, head_dim), jnp.float32),
        ],
        compiler_params=params(),
        name="final",
    )(*arrived, local, local_lse).transpose(0, 2, 1, 3)


def solution(mesh):
    return jax.shard_map(
        on_device,
        mesh=mesh,
        in_specs=(
            P(("inst", "tp"), None, None, None),
            P("inst"),
            P("inst", "tp", None, None),
            P("inst", "tp", None, None),
            P("inst", "tp", None),
            P("inst", None),
            P("inst"),
        ),
        out_specs=P("inst", "tp", None, None),
        check_vma=False,
    )
```

time: 504 us -> 90.1 us (0.18)
  the two profiles are of different devices: /device:TPU:13 before, /device:TPU:0 now
where the time goes in v2:
time: 90.1 us
  starting transfers between devices  41.7 us (46%)
  Pallas kernels  33.3 us (37%)
  waiting for transfers between devices  8.64 us (10%)
  local copies, waits for them, and re-layouts  3.12 us (3%)
  other arithmetic  3.05 us (3%)
    ppermute x24, starting transfers between devices, shift_both(): return lax.ppermute(x, ('inst', 'tp'), pairs)  30 us
    pallas_call x4, Pallas kernels, attend(): pl.pallas_call(functools.partial(attend_kernel, lay, nb, nt, query_at, re...  18.5 us
    ppermute x8, starting transfers between devices, shift(): return lax.ppermute(x, 'inst', pairs)  11.7 us
    ppermute x8, waiting for transfers between devices, shift(): return lax.ppermute(x, 'inst', pairs)  8.18 us
    pallas_call x3, Pallas kernels, merge(): pl.pallas_call(functools.partial(merge_kernel, lay, jobs), out_shape=(out...  6.05 us
    pallas_call x1, Pallas kernels, on_device(): pl.pallas_call(functools.partial(resident_kernel, lay), out_shape=(jax.Sh...  4.25 us
    pallas_call x1, Pallas kernels, on_device(): pl.pallas_call(functools.partial(final_kernel, lay, len(arrived)), out_sh...  2.62 us
    unnamed x62, local copies, waits for them, and re-layouts  2.27 us
  transfers between devices with their start and end apart: 32, of which 4 were waited for; matrix products, arithmetic and copies ran while one was open for 4% of the time, Pallas kernels for 34%

profile of v2, /device:TPU:0, one launch (start us, length us, event | category | flops | bytes accessed | tf_op | source)
XLA Modules:
  0.0 90.1 jit_solution(9439374808653092733)
XLA Ops:
  0.5 1.9 %prepare.1 = (bf16[656,128]{1,0:T(8,128)(2,1)}, f32[16,128]{1,0:T(8,128)}) custom-call(bf16[32,5,4,128]{3,2,1,0:T(4,128)(2,1)} %bitcast.28, s32[16,32]{1,0:T(8,128)} %bitcast.34, s32[1,32]{1,0:T(1,128)} %bitcast.39), custom_call_target="tpu_custom_call" | custom-call | tf_op jit(solution)/shard_map/prepare/pallas_call | solution.py:418
  2.4 2.5 %collective-permute-start.2 = (bf16[656,128]{1,0:T(8,128)(2,1)}, bf16[656,128]{1,0:T(8,128)(2,1)S(1)}, u32[]{:S(2)}, u32[]{:S(2)}) collective-permute-start(bf16[656,128]{1,0:T(8,128)(2,1)} %get-tuple-element.51.refs_0_.q_ref), channel_id=1, source_target_pairs={{0,1},{1,0},{2,3},{3,2},{4,5},{5,4},{6,7},{7,6},{8,9},{9,8},{10,11... | collective-permute-start | bytes 503816 | tf_op jit(solution)/shard_map/ppermute | solution.py:409
  4.8 1.5 %collective-permute-start.3 = (bf16[656,128]{1,0:T(8,128)(2,1)}, bf16[656,128]{1,0:T(8,128)(2,1)S(1)}, u32[]{:S(2)}, u32[]{:S(2)}) collective-permute-start(bf16[656,128]{1,0:T(8,128)(2,1)} %get-tuple-element.51.refs_0_.q_ref), channel_id=1, source_target_pairs={{0,4},{1,5},{2,6},{3,7},{4,0},{5,1},{6,2},{7,3},{8,12},{9,13},{10,... | collective-permute-start | bytes 503816 | tf_op jit(solution)/shard_map/ppermute | solution.py:409
  6.4 2.1 %collective-permute-start.8 = (bf16[656,128]{1,0:T(8,128)(2,1)}, bf16[656,128]{1,0:T(8,128)(2,1)S(1)}, u32[]{:S(2)}, u32[]{:S(2)}) collective-permute-start(bf16[656,128]{1,0:T(8,128)(2,1)} %get-tuple-element.51.refs_0_.q_ref), channel_id=1, source_target_pairs={{0,8},{2,10},{4,12},{6,14},{8,16},{10,18},{12,20},{14,22},{16,24},... | collective-permute-start | bytes 503816 | tf_op jit(solution)/shard_map/ppermute | solution.py:401
  10.2 4.1 %collective-permute-start.16 = (bf16[656,128]{1,0:T(8,128)(2,1)}, bf16[656,128]{1,0:T(8,128)(2,1)S(1)}, u32[]{:S(2)}, u32[]{:S(2)}) collective-permute-start(bf16[656,128]{1,0:T(8,128)(2,1)} %get-tuple-element.51.refs_0_.q_ref), channel_id=1, source_target_pairs={{0,24},{2,26},{4,28},{6,30},{8,0},{10,2},{12,4},{14,6},{16,8},{18,... | collective-permute-start | bytes 503816 | tf_op jit(solution)/shard_map/ppermute | solution.py:401
  15.5 1.5 %collective-permute-start.9 = (bf16[656,128]{1,0:T(8,128)(2,1)S(1)}, bf16[656,128]{1,0:T(8,128)(2,1)S(1)}, u32[]{:S(2)}, u32[]{:S(2)}) collective-permute-start(bf16[656,128]{1,0:T(8,128)(2,1)S(1)} %collective-permute-done.8.refs_0_), channel_id=1, source_target_pairs={{0,1},{1,0},{2,3},{3,2},{4,5},{5,4},{6,7},{7,6},{8,9},{9,8},{10,11... | collective-permute-start | bytes 503816 | tf_op jit(solution)/shard_map/ppermute | solution.py:409
  19.2 1.6 %collective-permute-start.10 = (bf16[656,128]{1,0:T(8,128)(2,1)S(1)}, bf16[656,128]{1,0:T(8,128)(2,1)S(1)}, u32[]{:S(2)}, u32[]{:S(2)}) collective-permute-start(bf16[656,128]{1,0:T(8,128)(2,1)S(1)} %collective-permute-done.8.refs_0_), channel_id=1, source_target_pairs={{0,4},{1,5},{2,6},{3,7},{4,0},{5,1},{6,2},{7,3},{8,12},{9,13},{10,... | collective-permute-start | bytes 503816 | tf_op jit(solution)/shard_map/ppermute | solution.py:409
  21.4 4.8 %attend.4 = (bf16[656,128]{1,0:T(8,128)(2,1)}, bf16[656,128]{1,0:T(8,128)(2,1)}, bf16[656,128]{1,0:T(8,128)(2,1)}, bf16[656,128]{1,0:T(8,128)(2,1)}) custom-call(s32[22]{0:T(128)} %get-tuple-element.75.lists, bf16[656,128]{1,0:T(8,128)(2,1)} %get-tuple-element.51.refs_0_.q_ref, bf16[656,128]{1,0:T(8,128)(2,1)} %copy-done.16, bf16[656,128]{1,0:T(8,128)(2,1)} %copy-done.17, ...), custom_call_target="tpu_custom_call" | custom-call | bytes 16777216 | tf_op jit(solution)/shard_map/attend/pallas_call | solution.py:513
  26.8 2.0 %collective-permute-start.6 = (bf16[656,128]{1,0:T(8,128)(2,1)}, bf16[656,128]{1,0:T(8,128)(2,1)S(1)}, u32[]{:S(2)}, u32[]{:S(2)}) collective-permute-start(bf16[656,128]{1,0:T(8,128)(2,1)} %get-tuple-element.38), channel_id=1, source_target_pairs={{0,4},{1,5},{2,6},{3,7},{4,0},{5,1},{6,2},{7,3},{8,12},{9,13},{10,... | collective-permute-start | bytes 503816 | tf_op jit(solution)/shard_map/ppermute | solution.py:409
  28.8 1.0 %collective-permute-start.7 = (bf16[656,128]{1,0:T(8,128)(2,1)}, bf16[656,128]{1,0:T(8,128)(2,1)S(1)}, u32[]{:S(2)}, u32[]{:S(2)}) collective-permute-start(bf16[656,128]{1,0:T(8,128)(2,1)} %get-tuple-element.39), channel_id=1, source_target_pairs={{0,5},{1,4},{2,7},{3,6},{4,1},{5,0},{6,3},{7,2},{8,13},{9,12},{10,... | collective-permute-start | bytes 503816 | tf_op jit(solution)/shard_map/ppermute | solution.py:409
  29.8 4.3 %resident.1 = (f32[640,128]{1,0:T(8,128)}, f32[8,128]{1,0:T(8,128)}) custom-call(bf16[656,128]{1,0:T(8,128)(2,1)} %get-tuple-element.51.refs_0_.q_ref, bf16[8,4,128,256]{3,2,1,0:T(8,128)(2,1)} %pages.1, bf16[32,4,256]{2,1,0:T(4,128)(2,1)} %own.1, f32[16,128]{1,0:T(8,128)} %get-tuple-element.53.counts), custom_call_target="tpu_custom_call" | custom-call | tf_op jit(solution)/shard_map/resident/pallas_call | solution.py:459
  34.7 1.9 %collective-permute-start.18 = (bf16[656,128]{1,0:T(8,128)(2,1)S(1)}, bf16[656,128]{1,0:T(8,128)(2,1)S(1)}, u32[]{:S(2)}, u32[]{:S(2)}) collective-permute-start(bf16[656,128]{1,0:T(8,128)(2,1)S(1)} %collective-permute-done.16.refs_0_), channel_id=1, source_target_pairs={{0,4},{1,5},{2,6},{3,7},{4,0},{5,1},{6,2},{7,3},{8,12},{9,13},{10,... | collective-permute-start | bytes 503816 | tf_op jit(solution)/shard_map/ppermute | solution.py:409
  37.7 1.1 %collective-permute-start.25 = (bf16[656,128]{1,0:T(8,128)(2,1)S(1)}, bf16[656,128]{1,0:T(8,128)(2,1)S(1)}, u32[]{:S(2)}, u32[]{:S(2)}) collective-permute-start(bf16[656,128]{1,0:T(8,128)(2,1)S(1)} %collective-permute-done.24.refs_0_), channel_id=1, source_target_pairs={{0,1},{1,0},{2,3},{3,2},{4,5},{5,4},{6,7},{7,6},{8,9},{9,8},{10,11... | collective-permute-start | bytes 503816 | tf_op jit(solution)/shard_map/ppermute | solution.py:409
  38.8 1.4 %collective-permute-start.26 = (bf16[656,128]{1,0:T(8,128)(2,1)S(1)}, bf16[656,128]{1,0:T(8,128)(2,1)S(1)}, u32[]{:S(2)}, u32[]{:S(2)}) collective-permute-start(bf16[656,128]{1,0:T(8,128)(2,1)S(1)} %collective-permute-done.24.refs_0_), channel_id=1, source_target_pairs={{0,4},{1,5},{2,6},{3,7},{4,0},{5,1},{6,2},{7,3},{8,12},{9,13},{10,... | collective-permute-start | bytes 503816 | tf_op jit(solution)/shard_map/ppermute | solution.py:409
  40.1 4.8 %attend.5 = (bf16[656,128]{1,0:T(8,128)(2,1)}, bf16[656,128]{1,0:T(8,128)(2,1)}, bf16[656,128]{1,0:T(8,128)(2,1)}, bf16[656,128]{1,0:T(8,128)(2,1)}) custom-call(s32[22]{0:T(128)} %get-tuple-element.73.lists, bf16[656,128]{1,0:T(8,128)(2,1)} %copy-done.15, bf16[656,128]{1,0:T(8,128)(2,1)} %copy-done.21, bf16[656,128]{1,0:T(8,128)(2,1)} %copy-done.22, ...), custom_call_target="tpu_custom_call" | custom-call | bytes 16777216 | tf_op jit(solution)/shard_map/attend/pallas_call | solution.py:513
  45.0 1.6 %collective-permute-start.27 = (bf16[656,128]{1,0:T(8,128)(2,1)S(1)}, bf16[656,128]{1,0:T(8,128)(2,1)S(1)}, u32[]{:S(2)}, u32[]{:S(2)}) collective-permute-start(bf16[656,128]{1,0:T(8,128)(2,1)S(1)} %collective-permute-done.24.refs_0_), channel_id=1, source_target_pairs={{0,5},{1,4},{2,7},{3,6},{4,1},{5,0},{6,3},{7,2},{8,13},{9,12},{10,... | collective-permute-start | bytes 503816 | tf_op jit(solution)/shard_map/ppermute | solution.py:409
  46.7 1.8 %collective-permute-start.13 = (bf16[656,128]{1,0:T(8,128)(2,1)}, bf16[656,128]{1,0:T(8,128)(2,1)S(1)}, u32[]{:S(2)}, u32[]{:S(2)}) collective-permute-start(bf16[656,128]{1,0:T(8,128)(2,1)} %get-tuple-element.43), channel_id=1, source_target_pairs={{0,4},{1,5},{2,6},{3,7},{4,0},{5,1},{6,2},{7,3},{8,12},{9,13},{10,... | collective-permute-start | bytes 503816 | tf_op jit(solution)/shard_map/ppermute | solution.py:409
  48.5 4.1 %attend.6 = (bf16[656,128]{1,0:T(8,128)(2,1)}, bf16[656,128]{1,0:T(8,128)(2,1)}, bf16[656,128]{1,0:T(8,128)(2,1)}, bf16[656,128]{1,0:T(8,128)(2,1)}) custom-call(s32[22]{0:T(128)} %get-tuple-element.74.lists, bf16[656,128]{1,0:T(8,128)(2,1)} %copy-done.20, bf16[656,128]{1,0:T(8,128)(2,1)} %copy-done.26, bf16[656,128]{1,0:T(8,128)(2,1)} %copy-done.27, ...), custom_call_target="tpu_custom_call" | custom-call | bytes 16777216 | tf_op jit(solution)/shard_map/attend/pallas_call | solution.py:513
  52.6 2.2 %collective-permute-start.14 = (bf16[656,128]{1,0:T(8,128)(2,1)S(1)}, bf16[656,128]{1,0:T(8,128)(2,1)S(1)}, u32[]{:S(2)}, u32[]{:S(2)}) collective-permute-start(bf16[656,128]{1,0:T(8,128)(2,1)S(1)} %copy-done.29), channel_id=1, source_target_pairs={{0,5},{1,4},{2,7},{3,6},{4,1},{5,0},{6,3},{7,2},{8,13},{9,12},{10,... | collective-permute-start | bytes 503816 | tf_op jit(solution)/shard_map/ppermute | solution.py:409
  54.9 1.5 %collective-permute-start.21 = (bf16[656,128]{1,0:T(8,128)(2,1)}, bf16[656,128]{1,0:T(8,128)(2,1)S(1)}, u32[]{:S(2)}, u32[]{:S(2)}) collective-permute-start(bf16[656,128]{1,0:T(8,128)(2,1)} %get-tuple-element.49), channel_id=1, source_target_pairs={{0,4},{1,5},{2,6},{3,7},{4,0},{5,1},{6,2},{7,3},{8,12},{9,13},{10,... | collective-permute-start | bytes 503816 | tf_op jit(solution)/shard_map/ppermute | solution.py:409
  56.4 4.9 %attend.7 = (bf16[656,128]{1,0:T(8,128)(2,1)}, bf16[656,128]{1,0:T(8,128)(2,1)}, bf16[656,128]{1,0:T(8,128)(2,1)}, bf16[656,128]{1,0:T(8,128)(2,1)}) custom-call(s32[22]{0:T(128)} %get-tuple-element.72.lists, bf16[656,128]{1,0:T(8,128)(2,1)} %copy-done.19, bf16[656,128]{1,0:T(8,128)(2,1)} %copy-done.24, bf16[656,128]{1,0:T(8,128)(2,1)} %copy-done.25, ...), custom_call_target="tpu_custom_call" | custom-call | bytes 16777216 | tf_op jit(solution)/shard_map/attend/pallas_call | solution.py:513
  61.3 2.1 %collective-permute-start.22 = (bf16[656,128]{1,0:T(8,128)(2,1)S(1)}, bf16[656,128]{1,0:T(8,128)(2,1)S(1)}, u32[]{:S(2)}, u32[]{:S(2)}) collective-permute-start(bf16[656,128]{1,0:T(8,128)(2,1)S(1)} %copy-done.30), channel_id=1, source_target_pairs={{0,5},{1,4},{2,7},{3,6},{4,1},{5,0},{6,3},{7,2},{8,13},{9,12},{10,... | collective-permute-start | bytes 503816 | tf_op jit(solution)/shard_map/ppermute | solution.py:409
  63.5 1.4 %collective-permute-start.29 = (bf16[656,128]{1,0:T(8,128)(2,1)}, bf16[656,128]{1,0:T(8,128)(2,1)S(1)}, u32[]{:S(2)}, u32[]{:S(2)}) collective-permute-start(bf16[656,128]{1,0:T(8,128)(2,1)} %get-tuple-element.60), channel_id=1, source_target_pairs={{0,4},{1,5},{2,6},{3,7},{4,0},{5,1},{6,2},{7,3},{8,12},{9,13},{10,... | collective-permute-start | bytes 503816 | tf_op jit(solution)/shard_map/ppermute | solution.py:409
  64.9 2.0 %collective-permute-start.30 = (bf16[656,128]{1,0:T(8,128)(2,1)}, bf16[656,128]{1,0:T(8,128)(2,1)S(1)}, u32[]{:S(2)}, u32[]{:S(2)}) collective-permute-start(bf16[656,128]{1,0:T(8,128)(2,1)} %get-tuple-element.61), channel_id=1, source_target_pairs={{0,5},{1,4},{2,7},{3,6},{4,1},{5,0},{6,3},{7,2},{8,13},{9,12},{10,... | collective-permute-start | bytes 503816 | tf_op jit(solution)/shard_map/ppermute | solution.py:409
  66.9 2.0 %merge.3 = bf16[656,128]{1,0:T(8,128)(2,1)} custom-call(bf16[656,128]{1,0:T(8,128)(2,1)} %get-tuple-element.41.refs_0_, bf16[656,128]{1,0:T(8,128)(2,1)} %copy-done.3, bf16[656,128]{1,0:T(8,128)(2,1)} %copy-done.4, bf16[656,128]{1,0:T(8,128)(2,1)} %copy-done.7), custom_call_target="tpu_custom_call" | custom-call | tf_op jit(solution)/shard_map/merge/pallas_call | solution.py:541
  69.0 1.4 %collective-permute-start.15 = (bf16[656,128]{1,0:T(8,128)(2,1)}, bf16[656,128]{1,0:T(8,128)(2,1)S(1)}, u32[]{:S(2)}, u32[]{:S(2)}) collective-permute-start(bf16[656,128]{1,0:T(8,128)(2,1)} %merge.3), channel_id=1, source_target_pairs={{0,24},{2,26},{4,28},{6,30},{8,0},{10,2},{12,4},{14,6},{16,8},{18,... | collective-permute-start | bytes 503816 | tf_op jit(solution)/shard_map/ppermute | solution.py:401
  71.1 2.0 %merge.4 = bf16[656,128]{1,0:T(8,128)(2,1)} custom-call(bf16[656,128]{1,0:T(8,128)(2,1)} %get-tuple-element.47.refs_0_, bf16[656,128]{1,0:T(8,128)(2,1)} %copy-done.5, bf16[656,128]{1,0:T(8,128)(2,1)} %copy-done.6, bf16[656,128]{1,0:T(8,128)(2,1)} %copy-done.11), custom_call_target="tpu_custom_call" | custom-call | tf_op jit(solution)/shard_map/merge/pallas_call | solution.py:541
  74.8 2.0 %merge.5 = bf16[656,128]{1,0:T(8,128)(2,1)} custom-call(bf16[656,128]{1,0:T(8,128)(2,1)} %get-tuple-element.58.refs_0_, bf16[656,128]{1,0:T(8,128)(2,1)} %copy-done.8, bf16[656,128]{1,0:T(8,128)(2,1)} %copy-done.10, bf16[656,128]{1,0:T(8,128)(2,1)} %copy-done.12), custom_call_target="tpu_custom_call" | custom-call | tf_op jit(solution)/shard_map/merge/pallas_call | solution.py:541
  76.8 2.6 %collective-permute-start.31 = (bf16[656,128]{1,0:T(8,128)(2,1)}, bf16[656,128]{1,0:T(8,128)(2,1)S(1)}, u32[]{:S(2)}, u32[]{:S(2)}) collective-permute-start(bf16[656,128]{1,0:T(8,128)(2,1)} %merge.5), channel_id=1, source_target_pairs={{0,16},{2,18},{4,20},{6,22},{8,24},{10,26},{12,28},{14,30},{16,0},... | collective-permute-start | bytes 503816 | tf_op jit(solution)/shard_map/ppermute | solution.py:401
  79.4 2.5 %collective-permute-done.23.refs_5_ = bf16[656,128]{1,0:T(8,128)(2,1)S(1)} collective-permute-done((bf16[656,128]{1,0:T(8,128)(2,1)}, bf16[656,128]{1,0:T(8,128)(2,1)S(1)}, u32[]{:S(2)}, u32[]{:S(2)}) %collective-permute-start.23) | collective-permute-done | bytes 167968 | tf_op jit(solution)/shard_map/ppermute | solution.py:401
  81.9 4.9 %collective-permute-done.31.refs_6_ = bf16[656,128]{1,0:T(8,128)(2,1)S(1)} collective-permute-done((bf16[656,128]{1,0:T(8,128)(2,1)}, bf16[656,128]{1,0:T(8,128)(2,1)S(1)}, u32[]{:S(2)}, u32[]{:S(2)}) %collective-permute-start.31) | collective-permute-done | bytes 167968 | tf_op jit(solution)/shard_map/ppermute | solution.py:401
  87.5 2.6 %final.1 = bf16[32,5,4,128]{3,2,1,0:T(4,128)(2,1)} custom-call(bf16[656,128]{1,0:T(8,128)(2,1)} %get-tuple-element.36.refs_0_, bf16[656,128]{1,0:T(8,128)(2,1)} %copy-done, bf16[656,128]{1,0:T(8,128)(2,1)} %copy-done.1, bf16[656,128]{1,0:T(8,128)(2,1)} %copy-done.2, bf16[656,128]{1,0:T(8,128)(2,1)} %copy-done.9, bf16[656,128]{1,0:T(8,128)(2,1)} %copy-done.13, ...), custom_call_target="tpu_custom_call" | custom-call | tf_op jit(solution)/shard_map/final/pallas_call | solution.py:582
  (124 shorter events, 11.8 us)
Async XLA Ops:
  0.0 14.3 %collective-permute-start = (bf16[8,8,128,256]{3,2,1,0:T(8,128)(2,1)}, bf16[8,8,128,256]{3,2,1,0:T(8,128)(2,1)}, u32[]{:S(2)}, u32[]{:S(2)}) collective-permute-start(bf16[8,8,128,256]{3,2,1,0:T(8,128)(2,1)} %param.7), channel_id=1, source_target_pairs={{0,2},{2,0},{4,6},{6,4},{8,10},{10,8},{12,14},{14,12},{16,18},{18,... | collective-permute-start | bytes 12582920 | tf_op jit(solution)/shard_map/ppermute | solution.py:401
  2.4 7.8 %collective-permute-start.2 = (bf16[656,128]{1,0:T(8,128)(2,1)}, bf16[656,128]{1,0:T(8,128)(2,1)S(1)}, u32[]{:S(2)}, u32[]{:S(2)}) collective-permute-start(bf16[656,128]{1,0:T(8,128)(2,1)} %get-tuple-element.51.refs_0_.q_ref), channel_id=1, source_target_pairs={{0,1},{1,0},{2,3},{3,2},{4,5},{5,4},{6,7},{7,6},{8,9},{9,8},{10,11... | collective-permute-start | bytes 503816 | tf_op jit(solution)/shard_map/ppermute | solution.py:409
  4.8 14.3 %collective-permute-start.3 = (bf16[656,128]{1,0:T(8,128)(2,1)}, bf16[656,128]{1,0:T(8,128)(2,1)S(1)}, u32[]{:S(2)}, u32[]{:S(2)}) collective-permute-start(bf16[656,128]{1,0:T(8,128)(2,1)} %get-tuple-element.51.refs_0_.q_ref), channel_id=1, source_target_pairs={{0,4},{1,5},{2,6},{3,7},{4,0},{5,1},{6,2},{7,3},{8,12},{9,13},{10,... | collective-permute-start | bytes 503816 | tf_op jit(solution)/shard_map/ppermute | solution.py:409
  6.4 14.4 %collective-permute-start.4 = (bf16[656,128]{1,0:T(8,128)(2,1)}, bf16[656,128]{1,0:T(8,128)(2,1)S(1)}, u32[]{:S(2)}, u32[]{:S(2)}) collective-permute-start(bf16[656,128]{1,0:T(8,128)(2,1)} %get-tuple-element.51.refs_0_.q_ref), channel_id=1, source_target_pairs={{0,5},{1,4},{2,7},{3,6},{4,1},{5,0},{6,3},{7,2},{8,13},{9,12},{10,... | collective-permute-start | bytes 503816 | tf_op jit(solution)/shard_map/ppermute | solution.py:409
  6.4 8.6 %collective-permute-start.8 = (bf16[656,128]{1,0:T(8,128)(2,1)}, bf16[656,128]{1,0:T(8,128)(2,1)S(1)}, u32[]{:S(2)}, u32[]{:S(2)}) collective-permute-start(bf16[656,128]{1,0:T(8,128)(2,1)} %get-tuple-element.51.refs_0_.q_ref), channel_id=1, source_target_pairs={{0,8},{2,10},{4,12},{6,14},{8,16},{10,18},{12,20},{14,22},{16,24},... | collective-permute-start | bytes 503816 | tf_op jit(solution)/shard_map/ppermute | solution.py:401
  10.2 16.0 %collective-permute-start.16 = (bf16[656,128]{1,0:T(8,128)(2,1)}, bf16[656,128]{1,0:T(8,128)(2,1)S(1)}, u32[]{:S(2)}, u32[]{:S(2)}) collective-permute-start(bf16[656,128]{1,0:T(8,128)(2,1)} %get-tuple-element.51.refs_0_.q_ref), channel_id=1, source_target_pairs={{0,24},{2,26},{4,28},{6,30},{8,0},{10,2},{12,4},{14,6},{16,8},{18,... | collective-permute-start | bytes 503816 | tf_op jit(solution)/shard_map/ppermute | solution.py:401
  14.3 1.3 %collective-permute-start.1 = (s32[2,8]{1,0:T(2,128)S(1)}, s32[2,8]{1,0:T(2,128)S(1)}, u32[]{:S(2)}, u32[]{:S(2)}) collective-permute-start(s32[2,8]{1,0:T(2,128)S(1)} %constant_dynamic-slice_fusion), channel_id=1, source_target_pairs={{0,2},{2,0},{4,6},{6,4},{8,10},{10,8},{12,14},{14,12},{16,18},{18,... | collective-permute-start | bytes 200 | tf_op jit(solution)/shard_map/ppermute | solution.py:401
  15.0 13.8 %collective-permute-start.24 = (bf16[656,128]{1,0:T(8,128)(2,1)}, bf16[656,128]{1,0:T(8,128)(2,1)S(1)}, u32[]{:S(2)}, u32[]{:S(2)}) collective-permute-start(bf16[656,128]{1,0:T(8,128)(2,1)} %get-tuple-element.51.refs_0_.q_ref), channel_id=1, source_target_pairs={{0,16},{2,18},{4,20},{6,22},{8,24},{10,26},{12,28},{14,30},{16,0},... | collective-permute-start | bytes 503816 | tf_op jit(solution)/shard_map/ppermute | solution.py:401
  15.5 11.2 %collective-permute-start.9 = (bf16[656,128]{1,0:T(8,128)(2,1)S(1)}, bf16[656,128]{1,0:T(8,128)(2,1)S(1)}, u32[]{:S(2)}, u32[]{:S(2)}) collective-permute-start(bf16[656,128]{1,0:T(8,128)(2,1)S(1)} %collective-permute-done.8.refs_0_), channel_id=1, source_target_pairs={{0,1},{1,0},{2,3},{3,2},{4,5},{5,4},{6,7},{7,6},{8,9},{9,8},{10,11... | collective-permute-start | bytes 503816 | tf_op jit(solution)/shard_map/ppermute | solution.py:409
  19.2 14.9 %collective-permute-start.10 = (bf16[656,128]{1,0:T(8,128)(2,1)S(1)}, bf16[656,128]{1,0:T(8,128)(2,1)S(1)}, u32[]{:S(2)}, u32[]{:S(2)}) collective-permute-start(bf16[656,128]{1,0:T(8,128)(2,1)S(1)} %collective-permute-done.8.refs_0_), channel_id=1, source_target_pairs={{0,4},{1,5},{2,6},{3,7},{4,0},{5,1},{6,2},{7,3},{8,12},{9,13},{10,... | collective-permute-start | bytes 503816 | tf_op jit(solution)/shard_map/ppermute | solution.py:409
  20.7 13.9 %collective-permute-start.11 = (bf16[656,128]{1,0:T(8,128)(2,1)S(1)}, bf16[656,128]{1,0:T(8,128)(2,1)S(1)}, u32[]{:S(2)}, u32[]{:S(2)}) collective-permute-start(bf16[656,128]{1,0:T(8,128)(2,1)S(1)} %collective-permute-done.8.refs_0_), channel_id=1, source_target_pairs={{0,5},{1,4},{2,7},{3,6},{4,1},{5,0},{6,3},{7,2},{8,13},{9,12},{10,... | collective-permute-start | bytes 503816 | tf_op jit(solution)/shard_map/ppermute | solution.py:409
  26.2 10.4 %collective-permute-start.5 = (bf16[656,128]{1,0:T(8,128)(2,1)}, bf16[656,128]{1,0:T(8,128)(2,1)S(1)}, u32[]{:S(2)}, u32[]{:S(2)}) collective-permute-start(bf16[656,128]{1,0:T(8,128)(2,1)} %get-tuple-element.37), channel_id=1, source_target_pairs={{0,1},{1,0},{2,3},{3,2},{4,5},{5,4},{6,7},{7,6},{8,9},{9,8},{10,11... | collective-permute-start | bytes 503816 | tf_op jit(solution)/shard_map/ppermute | solution.py:409
  26.8 10.9 %collective-permute-start.6 = (bf16[656,128]{1,0:T(8,128)(2,1)}, bf16[656,128]{1,0:T(8,128)(2,1)S(1)}, u32[]{:S(2)}, u32[]{:S(2)}) collective-permute-start(bf16[656,128]{1,0:T(8,128)(2,1)} %get-tuple-element.38), channel_id=1, source_target_pairs={{0,4},{1,5},{2,6},{3,7},{4,0},{5,1},{6,2},{7,3},{8,12},{9,13},{10,... | collective-permute-start | bytes 503816 | tf_op jit(solution)/shard_map/ppermute | solution.py:409
  28.8 10.0 %collective-permute-start.7 = (bf16[656,128]{1,0:T(8,128)(2,1)}, bf16[656,128]{1,0:T(8,128)(2,1)S(1)}, u32[]{:S(2)}, u32[]{:S(2)}) collective-permute-start(bf16[656,128]{1,0:T(8,128)(2,1)} %get-tuple-element.39), channel_id=1, source_target_pairs={{0,5},{1,4},{2,7},{3,6},{4,1},{5,0},{6,3},{7,2},{8,13},{9,12},{10,... | collective-permute-start | bytes 503816 | tf_op jit(solution)/shard_map/ppermute | solution.py:409
  34.1 10.8 %collective-permute-start.17 = (bf16[656,128]{1,0:T(8,128)(2,1)S(1)}, bf16[656,128]{1,0:T(8,128)(2,1)S(1)}, u32[]{:S(2)}, u32[]{:S(2)}) collective-permute-start(bf16[656,128]{1,0:T(8,128)(2,1)S(1)} %collective-permute-done.16.refs_0_), channel_id=1, source_target_pairs={{0,1},{1,0},{2,3},{3,2},{4,5},{5,4},{6,7},{7,6},{8,9},{9,8},{10,11... | collective-permute-start | bytes 503816 | tf_op jit(solution)/shard_map/ppermute | solution.py:409
  34.7 11.9 %collective-permute-start.18 = (bf16[656,128]{1,0:T(8,128)(2,1)S(1)}, bf16[656,128]{1,0:T(8,128)(2,1)S(1)}, u32[]{:S(2)}, u32[]{:S(2)}) collective-permute-start(bf16[656,128]{1,0:T(8,128)(2,1)S(1)} %collective-permute-done.16.refs_0_), channel_id=1, source_target_pairs={{0,4},{1,5},{2,6},{3,7},{4,0},{5,1},{6,2},{7,3},{8,12},{9,13},{10,... | collective-permute-start | bytes 503816 | tf_op jit(solution)/shard_map/ppermute | solution.py:409
  36.6 10.1 %collective-permute-start.19 = (bf16[656,128]{1,0:T(8,128)(2,1)S(1)}, bf16[656,128]{1,0:T(8,128)(2,1)}, u32[]{:S(2)}, u32[]{:S(2)}) collective-permute-start(bf16[656,128]{1,0:T(8,128)(2,1)S(1)} %collective-permute-done.16.refs_0_), channel_id=1, source_target_pairs={{0,5},{1,4},{2,7},{3,6},{4,1},{5,0},{6,3},{7,2},{8,13},{9,12},{10,... | collective-permute-start | bytes 503816 | tf_op jit(solution)/shard_map/ppermute | solution.py:409
  37.7 15.0 %collective-permute-start.25 = (bf16[656,128]{1,0:T(8,128)(2,1)S(1)}, bf16[656,128]{1,0:T(8,128)(2,1)S(1)}, u32[]{:S(2)}, u32[]{:S(2)}) collective-permute-start(bf16[656,128]{1,0:T(8,128)(2,1)S(1)} %collective-permute-done.24.refs_0_), channel_id=1, source_target_pairs={{0,1},{1,0},{2,3},{3,2},{4,5},{5,4},{6,7},{7,6},{8,9},{9,8},{10,11... | collective-permute-start | bytes 503816 | tf_op jit(solution)/shard_map/ppermute | solution.py:409
  38.8 16.1 %collective-permute-start.26 = (bf16[656,128]{1,0:T(8,128)(2,1)S(1)}, bf16[656,128]{1,0:T(8,128)(2,1)S(1)}, u32[]{:S(2)}, u32[]{:S(2)}) collective-permute-start(bf16[656,128]{1,0:T(8,128)(2,1)S(1)} %collective-permute-done.24.refs_0_), channel_id=1, source_target_pairs={{0,4},{1,5},{2,6},{3,7},{4,0},{5,1},{6,2},{7,3},{8,12},{9,13},{10,... | collective-permute-start | bytes 503816 | tf_op jit(solution)/shard_map/ppermute | solution.py:409
  45.0 10.0 %collective-permute-start.27 = (bf16[656,128]{1,0:T(8,128)(2,1)S(1)}, bf16[656,128]{1,0:T(8,128)(2,1)S(1)}, u32[]{:S(2)}, u32[]{:S(2)}) collective-permute-start(bf16[656,128]{1,0:T(8,128)(2,1)S(1)} %collective-permute-done.24.refs_0_), channel_id=1, source_target_pairs={{0,5},{1,4},{2,7},{3,6},{4,1},{5,0},{6,3},{7,2},{8,13},{9,12},{10,... | collective-permute-start | bytes 503816 | tf_op jit(solution)/shard_map/ppermute | solution.py:409
  46.6 14.8 %collective-permute-start.12 = (bf16[656,128]{1,0:T(8,128)(2,1)}, bf16[656,128]{1,0:T(8,128)(2,1)S(1)}, u32[]{:S(2)}, u32[]{:S(2)}) collective-permute-start(bf16[656,128]{1,0:T(8,128)(2,1)} %get-tuple-element.42), channel_id=1, source_target_pairs={{0,1},{1,0},{2,3},{3,2},{4,5},{5,4},{6,7},{7,6},{8,9},{9,8},{10,11... | collective-permute-start | bytes 503816 | tf_op jit(solution)/shard_map/ppermute | solution.py:409
  46.7 16.7 %collective-permute-start.13 = (bf16[656,128]{1,0:T(8,128)(2,1)}, bf16[656,128]{1,0:T(8,128)(2,1)S(1)}, u32[]{:S(2)}, u32[]{:S(2)}) collective-permute-start(bf16[656,128]{1,0:T(8,128)(2,1)} %get-tuple-element.43), channel_id=1, source_target_pairs={{0,4},{1,5},{2,6},{3,7},{4,0},{5,1},{6,2},{7,3},{8,12},{9,13},{10,... | collective-permute-start | bytes 503816 | tf_op jit(solution)/shard_map/ppermute | solution.py:409
  52.6 10.8 %collective-permute-start.14 = (bf16[656,128]{1,0:T(8,128)(2,1)S(1)}, bf16[656,128]{1,0:T(8,128)(2,1)S(1)}, u32[]{:S(2)}, u32[]{:S(2)}) collective-permute-start(bf16[656,128]{1,0:T(8,128)(2,1)S(1)} %copy-done.29), channel_id=1, source_target_pairs={{0,5},{1,4},{2,7},{3,6},{4,1},{5,0},{6,3},{7,2},{8,13},{9,12},{10,... | collective-permute-start | bytes 503816 | tf_op jit(solution)/shard_map/ppermute | solution.py:409
  54.8 10.1 %collective-permute-start.20 = (bf16[656,128]{1,0:T(8,128)(2,1)}, bf16[656,128]{1,0:T(8,128)(2,1)S(1)}, u32[]{:S(2)}, u32[]{:S(2)}) collective-permute-start(bf16[656,128]{1,0:T(8,128)(2,1)} %get-tuple-element.48), channel_id=1, source_target_pairs={{0,1},{1,0},{2,3},{3,2},{4,5},{5,4},{6,7},{7,6},{8,9},{9,8},{10,11... | collective-permute-start | bytes 503816 | tf_op jit(solution)/shard_map/ppermute | solution.py:409
  54.9 14.0 %collective-permute-start.21 = (bf16[656,128]{1,0:T(8,128)(2,1)}, bf16[656,128]{1,0:T(8,128)(2,1)S(1)}, u32[]{:S(2)}, u32[]{:S(2)}) collective-permute-start(bf16[656,128]{1,0:T(8,128)(2,1)} %get-tuple-element.49), channel_id=1, source_target_pairs={{0,4},{1,5},{2,6},{3,7},{4,0},{5,1},{6,2},{7,3},{8,12},{9,13},{10,... | collective-permute-start | bytes 503816 | tf_op jit(solution)/shard_map/ppermute | solution.py:409
  61.3 9.1 %collective-permute-start.22 = (bf16[656,128]{1,0:T(8,128)(2,1)S(1)}, bf16[656,128]{1,0:T(8,128)(2,1)S(1)}, u32[]{:S(2)}, u32[]{:S(2)}) collective-permute-start(bf16[656,128]{1,0:T(8,128)(2,1)S(1)} %copy-done.30), channel_id=1, source_target_pairs={{0,5},{1,4},{2,7},{3,6},{4,1},{5,0},{6,3},{7,2},{8,13},{9,12},{10,... | collective-permute-start | bytes 503816 | tf_op jit(solution)/shard_map/ppermute | solution.py:409
  63.4 10.2 %collective-permute-start.28 = (bf16[656,128]{1,0:T(8,128)(2,1)}, bf16[656,128]{1,0:T(8,128)(2,1)S(1)}, u32[]{:S(2)}, u32[]{:S(2)}) collective-permute-start(bf16[656,128]{1,0:T(8,128)(2,1)} %get-tuple-element.59), channel_id=1, source_target_pairs={{0,1},{1,0},{2,3},{3,2},{4,5},{5,4},{6,7},{7,6},{8,9},{9,8},{10,11... | collective-permute-start | bytes 503816 | tf_op jit(solution)/shard_map/ppermute | solution.py:409
  63.5 10.2 %collective-permute-start.29 = (bf16[656,128]{1,0:T(8,128)(2,1)}, bf16[656,128]{1,0:T(8,128)(2,1)S(1)}, u32[]{:S(2)}, u32[]{:S(2)}) collective-permute-start(bf16[656,128]{1,0:T(8,128)(2,1)} %get-tuple-element.60), channel_id=1, source_target_pairs={{0,4},{1,5},{2,6},{3,7},{4,0},{5,1},{6,2},{7,3},{8,12},{9,13},{10,... | collective-permute-start | bytes 503816 | tf_op jit(solution)/shard_map/ppermute | solution.py:409
  64.9 9.2 %collective-permute-start.30 = (bf16[656,128]{1,0:T(8,128)(2,1)}, bf16[656,128]{1,0:T(8,128)(2,1)S(1)}, u32[]{:S(2)}, u32[]{:S(2)}) collective-permute-start(bf16[656,128]{1,0:T(8,128)(2,1)} %get-tuple-element.61), channel_id=1, source_target_pairs={{0,5},{1,4},{2,7},{3,6},{4,1},{5,0},{6,3},{7,2},{8,13},{9,12},{10,... | collective-permute-start | bytes 503816 | tf_op jit(solution)/shard_map/ppermute | solution.py:409
  69.0 10.4 %collective-permute-start.15 = (bf16[656,128]{1,0:T(8,128)(2,1)}, bf16[656,128]{1,0:T(8,128)(2,1)S(1)}, u32[]{:S(2)}, u32[]{:S(2)}) collective-permute-start(bf16[656,128]{1,0:T(8,128)(2,1)} %merge.3), channel_id=1, source_target_pairs={{0,24},{2,26},{4,28},{6,30},{8,0},{10,2},{12,4},{14,6},{16,8},{18,... | collective-permute-start | bytes 503816 | tf_op jit(solution)/shard_map/ppermute | solution.py:401
  73.1 8.8 %collective-permute-start.23 = (bf16[656,128]{1,0:T(8,128)(2,1)}, bf16[656,128]{1,0:T(8,128)(2,1)S(1)}, u32[]{:S(2)}, u32[]{:S(2)}) collective-permute-start(bf16[656,128]{1,0:T(8,128)(2,1)} %merge.4), channel_id=1, source_target_pairs={{0,8},{2,10},{4,12},{6,14},{8,16},{10,18},{12,20},{14,22},{16,24},... | collective-permute-start | bytes 503816 | tf_op jit(solution)/shard_map/ppermute | solution.py:401
  76.8 10.0 %collective-permute-start.31 = (bf16[656,128]{1,0:T(8,128)(2,1)}, bf16[656,128]{1,0:T(8,128)(2,1)S(1)}, u32[]{:S(2)}, u32[]{:S(2)}) collective-permute-start(bf16[656,128]{1,0:T(8,128)(2,1)} %merge.5), channel_id=1, source_target_pairs={{0,16},{2,18},{4,20},{6,22},{8,24},{10,26},{12,28},{14,30},{16,0},... | collective-permute-start | bytes 503816 | tf_op jit(solution)/shard_map/ppermute | solution.py:401
  (31 other events, 163.3 us)

commit v3 on v2

--- a/solution.py
+++ b/solution.py
@@ -10,11 +10,9 @@
 
 CAP = 2
 Z_WAIT, R_WAIT, A_WAIT, B_WAIT = 2, 3, 3, 2
-DIRECT_OUT = (1, 1, 1, 1)
-DIRECT_BACK = (1, 1, 1, 1)
 LANES = 128
 NEG = -1e30
-VMEM_LIMIT = 62 * 1024 * 1024
+VMEM_LIMIT = 64 * 1024 * 1024 - 512 * 1024
 
 
 class Layout:
@@ -430,12 +428,11 @@
         name="prepare",
     )(queries.transpose(0, 2, 1, 3), tables.T, lengths[None])
 
-    turns = [0] + sorted(range(1, na), key=lambda s: (min(s, na - s), s))
+    turns = [0, *range(1, na)]
     small = nb * nt <= 4
     ways, back = {}, {}
     for turn, s in enumerate(turns):
-        ways[s] = "bt" if small and DIRECT_OUT[turn] else "bt"[turn % 2]
-        back[s] = "bt" if small and DIRECT_BACK[turn] else "bt"[turn % 2]
+        ways[s] = back[s] = "bt" if small else "bt"[turn % 2]
     other = {"b": "t", "t": "b"}
 
     def tie(x, *after):

time: 90.1 us -> 87.8 us (0.974); the launches traced: 90.1 us -> 86.8 us
  waiting for transfers between devices: 8.64 us -> 11.1 us
  local copies, waits for them, and re-layouts: 3.12 us -> 0.87 us
  Pallas kernels: 33.3 us -> 31.1 us
  starting transfers between devices: 41.7 us -> 40.5 us
    ppermute x8, starting transfers between devices: 11.7 us -> 9.39 us  [shift(): return lax.ppermute(x, 'inst', pairs)]
    unnamed x62 -> x16, local copies, waits for them, and re-layouts: 2.27 us -> 0.03 us
    pallas_call x4, Pallas kernels: 18.5 us -> 16.3 us  [attend(): pl.pallas_call(functools.partial(attend_kernel, lay, nb, nt, query_at, re...]
    ppermute x24, waiting for transfers between devices: 0.46 us -> 1.84 us  [shift_both(): return lax.ppermute(x, ('inst', 'tp'), pairs)]
    ppermute x24, starting transfers between devices: 30 us -> 31.1 us  [shift_both(): return lax.ppermute(x, ('inst', 'tp'), pairs)]
    ppermute x8, waiting for transfers between devices: 8.18 us -> 9.26 us  [shift(): return lax.ppermute(x, 'inst', pairs)]
  transfers between devices with their start and end apart: 32 -> 32, of which waited for: 4 -> 4; matrix products, arithmetic and copies ran while one was open for 4% -> 4% of each run, Pallas kernels for 34% -> 33%
where the time goes in v3:
time: 87.8 us; the launch traced here: 86.8 us
  starting transfers between devices  40.5 us (46%)
  Pallas kernels  31.1 us (35%)
  waiting for transfers between devices  11.1 us (13%)
  other arithmetic  3.05 us (3%)
    ppermute x24, starting transfers between devices, shift_both(): return lax.ppermute(x, ('inst', 'tp'), pairs)  31.1 us
    pallas_call x4, Pallas kernels, attend(): pl.pallas_call(functools.partial(attend_kernel, lay, nb, nt, query_at, re...  16.3 us
    ppermute x8, starting transfers between devices, shift(): return lax.ppermute(x, 'inst', pairs)  9.39 us
    ppermute x8, waiting for transfers between devices, shift(): return lax.ppermute(x, 'inst', pairs)  9.26 us
    pallas_call x3, Pallas kernels, merge(): pl.pallas_call(functools.partial(merge_kernel, lay, jobs), out_shape=(out...  6.03 us
    pallas_call x1, Pallas kernels, on_device(): pl.pallas_call(functools.partial(resident_kernel, lay), out_shape=(jax.Sh...  4.25 us
    pallas_call x1, Pallas kernels, on_device(): pl.pallas_call(functools.partial(final_kernel, lay, len(arrived)), out_sh...  2.63 us
    pallas_call x1, Pallas kernels, on_device(): pl.pallas_call(functools.partial(prepare_kernel, lay, resident_count, pag...  1.9 us
  transfers between devices with their start and end apart: 32, of which 4 were waited for; matrix products, arithmetic and copies ran while one was open for 4% of the time, Pallas kernels for 33%

profile of v3, /device:TPU:0, one launch (start us, length us, event | category | flops | bytes accessed | tf_op | source)
XLA Modules:
  0.0 86.8 jit_solution(17811939404074592611)
XLA Ops:
  0.5 1.9 %prepare.1 = (bf16[656,128]{1,0:T(8,128)(2,1)}, f32[16,128]{1,0:T(8,128)}) custom-call(bf16[32,5,4,128]{3,2,1,0:T(4,128)(2,1)} %bitcast.28, s32[16,32]{1,0:T(8,128)} %bitcast.34, s32[1,32]{1,0:T(1,128)} %bitcast.39), custom_call_target="tpu_custom_call" | custom-call | tf_op jit(solution)/shard_map/prepare/pallas_call | solution.py:416
  2.4 2.5 %collective-permute-start.2 = (bf16[656,128]{1,0:T(8,128)(2,1)}, bf16[656,128]{1,0:T(8,128)(2,1)S(1)}, u32[]{:S(2)}, u32[]{:S(2)}) collective-permute-start(bf16[656,128]{1,0:T(8,128)(2,1)} %get-tuple-element.51.refs_0_.q_ref), channel_id=1, source_target_pairs={{0,1},{1,0},{2,3},{3,2},{4,5},{5,4},{6,7},{7,6},{8,9},{9,8},{10,11... | collective-permute-start | bytes 503816 | tf_op jit(solution)/shard_map/ppermute | solution.py:407
  4.8 1.5 %collective-permute-start.3 = (bf16[656,128]{1,0:T(8,128)(2,1)}, bf16[656,128]{1,0:T(8,128)(2,1)S(1)}, u32[]{:S(2)}, u32[]{:S(2)}) collective-permute-start(bf16[656,128]{1,0:T(8,128)(2,1)} %get-tuple-element.51.refs_0_.q_ref), channel_id=1, source_target_pairs={{0,4},{1,5},{2,6},{3,7},{4,0},{5,1},{6,2},{7,3},{8,12},{9,13},{10,... | collective-permute-start | bytes 503816 | tf_op jit(solution)/shard_map/ppermute | solution.py:407
  6.4 2.1 %collective-permute-start.8 = (bf16[656,128]{1,0:T(8,128)(2,1)}, bf16[656,128]{1,0:T(8,128)(2,1)}, u32[]{:S(2)}, u32[]{:S(2)}) collective-permute-start(bf16[656,128]{1,0:T(8,128)(2,1)} %get-tuple-element.51.refs_0_.q_ref), channel_id=1, source_target_pairs={{0,8},{2,10},{4,12},{6,14},{8,16},{10,18},{12,20},{14,22},{16,24},... | collective-permute-start | bytes 503816 | tf_op jit(solution)/shard_map/ppermute | solution.py:399
  10.2 3.0 %collective-permute-start.16 = (bf16[656,128]{1,0:T(8,128)(2,1)}, bf16[656,128]{1,0:T(8,128)(2,1)}, u32[]{:S(2)}, u32[]{:S(2)}) collective-permute-start(bf16[656,128]{1,0:T(8,128)(2,1)} %get-tuple-element.51.refs_0_.q_ref), channel_id=1, source_target_pairs={{0,16},{2,18},{4,20},{6,22},{8,24},{10,26},{12,28},{14,30},{16,0},... | collective-permute-start | bytes 503816 | tf_op jit(solution)/shard_map/ppermute | solution.py:399
  13.2 1.8 %collective-permute-done.8.refs_0_ = bf16[656,128]{1,0:T(8,128)(2,1)} collective-permute-done((bf16[656,128]{1,0:T(8,128)(2,1)}, bf16[656,128]{1,0:T(8,128)(2,1)}, u32[]{:S(2)}, u32[]{:S(2)}) %collective-permute-start.8) | collective-permute-done | bytes 167968 | tf_op jit(solution)/shard_map/ppermute | solution.py:399
  15.0 1.6 %collective-permute-start.24 = (bf16[656,128]{1,0:T(8,128)(2,1)}, bf16[656,128]{1,0:T(8,128)(2,1)}, u32[]{:S(2)}, u32[]{:S(2)}) collective-permute-start(bf16[656,128]{1,0:T(8,128)(2,1)} %get-tuple-element.51.refs_0_.q_ref), channel_id=1, source_target_pairs={{0,24},{2,26},{4,28},{6,30},{8,0},{10,2},{12,4},{14,6},{16,8},{18,... | collective-permute-start | bytes 503816 | tf_op jit(solution)/shard_map/ppermute | solution.py:399
  16.6 1.5 %collective-permute-start.9 = (bf16[656,128]{1,0:T(8,128)(2,1)}, bf16[656,128]{1,0:T(8,128)(2,1)}, u32[]{:S(2)}, u32[]{:S(2)}) collective-permute-start(bf16[656,128]{1,0:T(8,128)(2,1)} %collective-permute-done.8.refs_0_), channel_id=1, source_target_pairs={{0,1},{1,0},{2,3},{3,2},{4,5},{5,4},{6,7},{7,6},{8,9},{9,8},{10,11... | collective-permute-start | bytes 503816 | tf_op jit(solution)/shard_map/ppermute | solution.py:407
  20.3 1.6 %collective-permute-start.10 = (bf16[656,128]{1,0:T(8,128)(2,1)}, bf16[656,128]{1,0:T(8,128)(2,1)}, u32[]{:S(2)}, u32[]{:S(2)}) collective-permute-start(bf16[656,128]{1,0:T(8,128)(2,1)} %collective-permute-done.8.refs_0_), channel_id=1, source_target_pairs={{0,4},{1,5},{2,6},{3,7},{4,0},{5,1},{6,2},{7,3},{8,12},{9,13},{10,... | collective-permute-start | bytes 503816 | tf_op jit(solution)/shard_map/ppermute | solution.py:407
  22.3 4.8 %attend.4 = (bf16[656,128]{1,0:T(8,128)(2,1)}, bf16[656,128]{1,0:T(8,128)(2,1)}, bf16[656,128]{1,0:T(8,128)(2,1)}, bf16[656,128]{1,0:T(8,128)(2,1)}) custom-call(s32[22]{0:T(128)} %get-tuple-element.75.lists, bf16[656,128]{1,0:T(8,128)(2,1)} %get-tuple-element.51.refs_0_.q_ref, bf16[656,128]{1,0:T(8,128)(2,1)} %copy-done.6, bf16[656,128]{1,0:T(8,128)(2,1)} %copy-done.7, ...), custom_call_target="tpu_custom_call" | custom-call | bytes 16777216 | tf_op jit(solution)/shard_map/attend/pallas_call | solution.py:510
  27.1 1.6 %collective-permute-start.5 = (bf16[656,128]{1,0:T(8,128)(2,1)}, bf16[656,128]{1,0:T(8,128)(2,1)S(1)}, u32[]{:S(2)}, u32[]{:S(2)}) collective-permute-start(bf16[656,128]{1,0:T(8,128)(2,1)} %get-tuple-element.37), channel_id=1, source_target_pairs={{0,1},{1,0},{2,3},{3,2},{4,5},{5,4},{6,7},{7,6},{8,9},{9,8},{10,11... | collective-permute-start | bytes 503816 | tf_op jit(solution)/shard_map/ppermute | solution.py:407
  28.7 2.0 %collective-permute-start.6 = (bf16[656,128]{1,0:T(8,128)(2,1)}, bf16[656,128]{1,0:T(8,128)(2,1)S(1)}, u32[]{:S(2)}, u32[]{:S(2)}) collective-permute-start(bf16[656,128]{1,0:T(8,128)(2,1)} %get-tuple-element.38), channel_id=1, source_target_pairs={{0,4},{1,5},{2,6},{3,7},{4,0},{5,1},{6,2},{7,3},{8,12},{9,13},{10,... | collective-permute-start | bytes 503816 | tf_op jit(solution)/shard_map/ppermute | solution.py:407
  30.7 4.2 %resident.1 = (f32[640,128]{1,0:T(8,128)}, f32[8,128]{1,0:T(8,128)}) custom-call(bf16[656,128]{1,0:T(8,128)(2,1)} %get-tuple-element.51.refs_0_.q_ref, bf16[8,4,128,256]{3,2,1,0:T(8,128)(2,1)} %pages.1, bf16[32,4,256]{2,1,0:T(4,128)(2,1)} %own.1, f32[16,128]{1,0:T(8,128)} %get-tuple-element.53.counts), custom_call_target="tpu_custom_call" | custom-call | tf_op jit(solution)/shard_map/resident/pallas_call | solution.py:456
  35.0 1.5 %collective-permute-start.17 = (bf16[656,128]{1,0:T(8,128)(2,1)}, bf16[656,128]{1,0:T(8,128)(2,1)}, u32[]{:S(2)}, u32[]{:S(2)}) collective-permute-start(bf16[656,128]{1,0:T(8,128)(2,1)} %collective-permute-done.16.refs_0_), channel_id=1, source_target_pairs={{0,1},{1,0},{2,3},{3,2},{4,5},{5,4},{6,7},{7,6},{8,9},{9,8},{10,11... | collective-permute-start | bytes 503816 | tf_op jit(solution)/shard_map/ppermute | solution.py:407
  36.5 2.0 %collective-permute-start.18 = (bf16[656,128]{1,0:T(8,128)(2,1)}, bf16[656,128]{1,0:T(8,128)(2,1)}, u32[]{:S(2)}, u32[]{:S(2)}) collective-permute-start(bf16[656,128]{1,0:T(8,128)(2,1)} %collective-permute-done.16.refs_0_), channel_id=1, source_target_pairs={{0,4},{1,5},{2,6},{3,7},{4,0},{5,1},{6,2},{7,3},{8,12},{9,13},{10,... | collective-permute-start | bytes 503816 | tf_op jit(solution)/shard_map/ppermute | solution.py:407
  38.5 1.5 %collective-permute-start.25 = (bf16[656,128]{1,0:T(8,128)(2,1)}, bf16[656,128]{1,0:T(8,128)(2,1)}, u32[]{:S(2)}, u32[]{:S(2)}) collective-permute-start(bf16[656,128]{1,0:T(8,128)(2,1)} %collective-permute-done.24.refs_0_), channel_id=1, source_target_pairs={{0,1},{1,0},{2,3},{3,2},{4,5},{5,4},{6,7},{7,6},{8,9},{9,8},{10,11... | collective-permute-start | bytes 503816 | tf_op jit(solution)/shard_map/ppermute | solution.py:407
  40.0 1.9 %collective-permute-start.26 = (bf16[656,128]{1,0:T(8,128)(2,1)}, bf16[656,128]{1,0:T(8,128)(2,1)}, u32[]{:S(2)}, u32[]{:S(2)}) collective-permute-start(bf16[656,128]{1,0:T(8,128)(2,1)} %collective-permute-done.24.refs_0_), channel_id=1, source_target_pairs={{0,4},{1,5},{2,6},{3,7},{4,0},{5,1},{6,2},{7,3},{8,12},{9,13},{10,... | collective-permute-start | bytes 503816 | tf_op jit(solution)/shard_map/ppermute | solution.py:407
  42.0 3.0 %attend.5 = (bf16[656,128]{1,0:T(8,128)(2,1)}, bf16[656,128]{1,0:T(8,128)(2,1)}, bf16[656,128]{1,0:T(8,128)(2,1)}, bf16[656,128]{1,0:T(8,128)(2,1)}) custom-call(s32[22]{0:T(128)} %get-tuple-element.73.lists, bf16[656,128]{1,0:T(8,128)(2,1)} %collective-permute-done.8.refs_0_, bf16[656,128]{1,0:T(8,128)(2,1)} %collective-permute-done.9.refs_1_, ...), custom_call_target="tpu_custom_call" | custom-call | bytes 16777216 | tf_op jit(solution)/shard_map/attend/pallas_call | solution.py:510
  45.2 1.8 %collective-permute-done.18.refs_2_ = bf16[656,128]{1,0:T(8,128)(2,1)} collective-permute-done((bf16[656,128]{1,0:T(8,128)(2,1)}, bf16[656,128]{1,0:T(8,128)(2,1)}, u32[]{:S(2)}, u32[]{:S(2)}) %collective-permute-start.18) | collective-permute-done | bytes 167968 | tf_op jit(solution)/shard_map/ppermute | solution.py:407
  47.5 2.1 %collective-permute-start.13 = (bf16[656,128]{1,0:T(8,128)(2,1)}, bf16[656,128]{1,0:T(8,128)(2,1)S(1)}, u32[]{:S(2)}, u32[]{:S(2)}) collective-permute-start(bf16[656,128]{1,0:T(8,128)(2,1)} %get-tuple-element.43), channel_id=1, source_target_pairs={{0,4},{1,5},{2,6},{3,7},{4,0},{5,1},{6,2},{7,3},{8,12},{9,13},{10,... | collective-permute-start | bytes 503816 | tf_op jit(solution)/shard_map/ppermute | solution.py:407
  49.6 4.5 %attend.6 = (bf16[656,128]{1,0:T(8,128)(2,1)}, bf16[656,128]{1,0:T(8,128)(2,1)}, bf16[656,128]{1,0:T(8,128)(2,1)}, bf16[656,128]{1,0:T(8,128)(2,1)}) custom-call(s32[22]{0:T(128)} %get-tuple-element.74.lists, bf16[656,128]{1,0:T(8,128)(2,1)} %collective-permute-done.16.refs_0_, bf16[656,128]{1,0:T(8,128)(2,1)} %collective-permute-done.17.refs_1_, ...), custom_call_target="tpu_custom_call" | custom-call | bytes 16777216 | tf_op jit(solution)/shard_map/attend/pallas_call | solution.py:510
  54.2 2.2 %collective-permute-start.14 = (bf16[656,128]{1,0:T(8,128)(2,1)}, bf16[656,128]{1,0:T(8,128)(2,1)}, u32[]{:S(2)}, u32[]{:S(2)}) collective-permute-start(bf16[656,128]{1,0:T(8,128)(2,1)} %get-tuple-element.44), channel_id=1, source_target_pairs={{0,5},{1,4},{2,7},{3,6},{4,1},{5,0},{6,3},{7,2},{8,13},{9,12},{10,... | collective-permute-start | bytes 503816 | tf_op jit(solution)/shard_map/ppermute | solution.py:407
  58.1 4.0 %attend.7 = (bf16[656,128]{1,0:T(8,128)(2,1)}, bf16[656,128]{1,0:T(8,128)(2,1)}, bf16[656,128]{1,0:T(8,128)(2,1)}, bf16[656,128]{1,0:T(8,128)(2,1)}) custom-call(s32[22]{0:T(128)} %get-tuple-element.72.lists, bf16[656,128]{1,0:T(8,128)(2,1)} %collective-permute-done.24.refs_0_, bf16[656,128]{1,0:T(8,128)(2,1)} %collective-permute-done.25.refs_1_, ...), custom_call_target="tpu_custom_call" | custom-call | bytes 16777216 | tf_op jit(solution)/shard_map/attend/pallas_call | solution.py:510
  62.1 2.9 %collective-permute-start.22 = (bf16[656,128]{1,0:T(8,128)(2,1)}, bf16[656,128]{1,0:T(8,128)(2,1)}, u32[]{:S(2)}, u32[]{:S(2)}) collective-permute-start(bf16[656,128]{1,0:T(8,128)(2,1)} %get-tuple-element.50), channel_id=1, source_target_pairs={{0,5},{1,4},{2,7},{3,6},{4,1},{5,0},{6,3},{7,2},{8,13},{9,12},{10,... | collective-permute-start | bytes 503816 | tf_op jit(solution)/shard_map/ppermute | solution.py:407
  65.6 2.8 %collective-permute-start.30 = (bf16[656,128]{1,0:T(8,128)(2,1)}, bf16[656,128]{1,0:T(8,128)(2,1)}, u32[]{:S(2)}, u32[]{:S(2)}) collective-permute-start(bf16[656,128]{1,0:T(8,128)(2,1)} %get-tuple-element.61), channel_id=1, source_target_pairs={{0,5},{1,4},{2,7},{3,6},{4,1},{5,0},{6,3},{7,2},{8,13},{9,12},{10,... | collective-permute-start | bytes 503816 | tf_op jit(solution)/shard_map/ppermute | solution.py:407
  68.4 2.0 %merge.3 = bf16[656,128]{1,0:T(8,128)(2,1)} custom-call(bf16[656,128]{1,0:T(8,128)(2,1)} %get-tuple-element.41.refs_0_, bf16[656,128]{1,0:T(8,128)(2,1)} %copy-done.2, bf16[656,128]{1,0:T(8,128)(2,1)} %copy-done.3, bf16[656,128]{1,0:T(8,128)(2,1)} %collective-permute-done.14.refs_3_), custom_call_target="tpu_custom_call" | custom-call | tf_op jit(solution)/shard_map/merge/pallas_call | solution.py:538
  70.5 2.0 %merge.4 = bf16[656,128]{1,0:T(8,128)(2,1)} custom-call(bf16[656,128]{1,0:T(8,128)(2,1)} %get-tuple-element.47.refs_0_, bf16[656,128]{1,0:T(8,128)(2,1)} %collective-permute-done.20.refs_1_, bf16[656,128]{1,0:T(8,128)(2,1)} %collective-permute-done.21.refs_2_, bf16[656,128]{1,0:T(8,128)(2,1)} %collective-permute-done.22.refs_3_), custom_call_target="tpu_custom_call" | custom-call | tf_op jit(solution)/shard_map/merge/pallas_call | solution.py:538
  72.5 2.2 %collective-permute-start.23 = (bf16[656,128]{1,0:T(8,128)(2,1)}, bf16[656,128]{1,0:T(8,128)(2,1)S(1)}, u32[]{:S(2)}, u32[]{:S(2)}) collective-permute-start(bf16[656,128]{1,0:T(8,128)(2,1)} %merge.4), channel_id=1, source_target_pairs={{0,16},{2,18},{4,20},{6,22},{8,24},{10,26},{12,28},{14,30},{16,0},... | collective-permute-start | bytes 503816 | tf_op jit(solution)/shard_map/ppermute | solution.py:399
  74.7 2.0 %merge.5 = bf16[656,128]{1,0:T(8,128)(2,1)} custom-call(bf16[656,128]{1,0:T(8,128)(2,1)} %get-tuple-element.58.refs_0_, bf16[656,128]{1,0:T(8,128)(2,1)} %collective-permute-done.28.refs_1_, bf16[656,128]{1,0:T(8,128)(2,1)} %collective-permute-done.29.refs_2_, bf16[656,128]{1,0:T(8,128)(2,1)} %collective-permute-done.30.refs_3_), custom_call_target="tpu_custom_call" | custom-call | tf_op jit(solution)/shard_map/merge/pallas_call | solution.py:538
  76.7 5.4 %collective-permute-done.23.refs_5_ = bf16[656,128]{1,0:T(8,128)(2,1)S(1)} collective-permute-done((bf16[656,128]{1,0:T(8,128)(2,1)}, bf16[656,128]{1,0:T(8,128)(2,1)S(1)}, u32[]{:S(2)}, u32[]{:S(2)}) %collective-permute-start.23) | collective-permute-done | bytes 167968 | tf_op jit(solution)/shard_map/ppermute | solution.py:399
  82.2 2.1 %collective-permute-done.31.refs_6_ = bf16[656,128]{1,0:T(8,128)(2,1)} collective-permute-done((bf16[656,128]{1,0:T(8,128)(2,1)}, bf16[656,128]{1,0:T(8,128)(2,1)}, u32[]{:S(2)}, u32[]{:S(2)}) %collective-permute-start.31) | collective-permute-done | bytes 167968 | tf_op jit(solution)/shard_map/ppermute | solution.py:399
  84.2 2.6 %final.1 = bf16[32,5,4,128]{3,2,1,0:T(4,128)(2,1)} custom-call(bf16[656,128]{1,0:T(8,128)(2,1)} %get-tuple-element.36.refs_0_, bf16[656,128]{1,0:T(8,128)(2,1)} %copy-done, bf16[656,128]{1,0:T(8,128)(2,1)} %copy-done.1, bf16[656,128]{1,0:T(8,128)(2,1)} %collective-permute-done.7.refs_3_, bf16[656,128]{1,0:T(8,128)(2,1)} %copy-done.4, ...), custom_call_target="tpu_custom_call" | custom-call | tf_op jit(solution)/shard_map/final/pallas_call | solution.py:579
  (78 shorter events, 8.1 us)
Async XLA Ops:
  0.0 13.2 %collective-permute-start = (bf16[8,8,128,256]{3,2,1,0:T(8,128)(2,1)}, bf16[8,8,128,256]{3,2,1,0:T(8,128)(2,1)}, u32[]{:S(2)}, u32[]{:S(2)}) collective-permute-start(bf16[8,8,128,256]{3,2,1,0:T(8,128)(2,1)} %param.7), channel_id=1, source_target_pairs={{0,2},{2,0},{4,6},{6,4},{8,10},{10,8},{12,14},{14,12},{16,18},{18,... | collective-permute-start | bytes 12582920 | tf_op jit(solution)/shard_map/ppermute | solution.py:399
  2.4 7.8 %collective-permute-start.2 = (bf16[656,128]{1,0:T(8,128)(2,1)}, bf16[656,128]{1,0:T(8,128)(2,1)S(1)}, u32[]{:S(2)}, u32[]{:S(2)}) collective-permute-start(bf16[656,128]{1,0:T(8,128)(2,1)} %get-tuple-element.51.refs_0_.q_ref), channel_id=1, source_target_pairs={{0,1},{1,0},{2,3},{3,2},{4,5},{5,4},{6,7},{7,6},{8,9},{9,8},{10,11... | collective-permute-start | bytes 503816 | tf_op jit(solution)/shard_map/ppermute | solution.py:407
  4.8 15.4 %collective-permute-start.3 = (bf16[656,128]{1,0:T(8,128)(2,1)}, bf16[656,128]{1,0:T(8,128)(2,1)S(1)}, u32[]{:S(2)}, u32[]{:S(2)}) collective-permute-start(bf16[656,128]{1,0:T(8,128)(2,1)} %get-tuple-element.51.refs_0_.q_ref), channel_id=1, source_target_pairs={{0,4},{1,5},{2,6},{3,7},{4,0},{5,1},{6,2},{7,3},{8,12},{9,13},{10,... | collective-permute-start | bytes 503816 | tf_op jit(solution)/shard_map/ppermute | solution.py:407
  6.4 15.5 %collective-permute-start.4 = (bf16[656,128]{1,0:T(8,128)(2,1)}, bf16[656,128]{1,0:T(8,128)(2,1)}, u32[]{:S(2)}, u32[]{:S(2)}) collective-permute-start(bf16[656,128]{1,0:T(8,128)(2,1)} %get-tuple-element.51.refs_0_.q_ref), channel_id=1, source_target_pairs={{0,5},{1,4},{2,7},{3,6},{4,1},{5,0},{6,3},{7,2},{8,13},{9,12},{10,... | collective-permute-start | bytes 503816 | tf_op jit(solution)/shard_map/ppermute | solution.py:407
  6.4 8.7 %collective-permute-start.8 = (bf16[656,128]{1,0:T(8,128)(2,1)}, bf16[656,128]{1,0:T(8,128)(2,1)}, u32[]{:S(2)}, u32[]{:S(2)}) collective-permute-start(bf16[656,128]{1,0:T(8,128)(2,1)} %get-tuple-element.51.refs_0_.q_ref), channel_id=1, source_target_pairs={{0,8},{2,10},{4,12},{6,14},{8,16},{10,18},{12,20},{14,22},{16,24},... | collective-permute-start | bytes 503816 | tf_op jit(solution)/shard_map/ppermute | solution.py:399
  10.2 16.9 %collective-permute-start.16 = (bf16[656,128]{1,0:T(8,128)(2,1)}, bf16[656,128]{1,0:T(8,128)(2,1)}, u32[]{:S(2)}, u32[]{:S(2)}) collective-permute-start(bf16[656,128]{1,0:T(8,128)(2,1)} %get-tuple-element.51.refs_0_.q_ref), channel_id=1, source_target_pairs={{0,16},{2,18},{4,20},{6,22},{8,24},{10,26},{12,28},{14,30},{16,0},... | collective-permute-start | bytes 503816 | tf_op jit(solution)/shard_map/ppermute | solution.py:399
  13.2 3.4 %collective-permute-start.1 = (s32[2,8]{1,0:T(2,128)S(1)}, s32[2,8]{1,0:T(2,128)S(1)}, u32[]{:S(2)}, u32[]{:S(2)}) collective-permute-start(s32[2,8]{1,0:T(2,128)S(1)} %constant_dynamic-slice_fusion), channel_id=1, source_target_pairs={{0,2},{2,0},{4,6},{6,4},{8,10},{10,8},{12,14},{14,12},{16,18},{18,... | collective-permute-start | bytes 200 | tf_op jit(solution)/shard_map/ppermute | solution.py:399
  15.0 15.7 %collective-permute-start.24 = (bf16[656,128]{1,0:T(8,128)(2,1)}, bf16[656,128]{1,0:T(8,128)(2,1)}, u32[]{:S(2)}, u32[]{:S(2)}) collective-permute-start(bf16[656,128]{1,0:T(8,128)(2,1)} %get-tuple-element.51.refs_0_.q_ref), channel_id=1, source_target_pairs={{0,24},{2,26},{4,28},{6,30},{8,0},{10,2},{12,4},{14,6},{16,8},{18,... | collective-permute-start | bytes 503816 | tf_op jit(solution)/shard_map/ppermute | solution.py:399
  16.6 12.1 %collective-permute-start.9 = (bf16[656,128]{1,0:T(8,128)(2,1)}, bf16[656,128]{1,0:T(8,128)(2,1)}, u32[]{:S(2)}, u32[]{:S(2)}) collective-permute-start(bf16[656,128]{1,0:T(8,128)(2,1)} %collective-permute-done.8.refs_0_), channel_id=1, source_target_pairs={{0,1},{1,0},{2,3},{3,2},{4,5},{5,4},{6,7},{7,6},{8,9},{9,8},{10,11... | collective-permute-start | bytes 503816 | tf_op jit(solution)/shard_map/ppermute | solution.py:407
  20.3 14.7 %collective-permute-start.10 = (bf16[656,128]{1,0:T(8,128)(2,1)}, bf16[656,128]{1,0:T(8,128)(2,1)}, u32[]{:S(2)}, u32[]{:S(2)}) collective-permute-start(bf16[656,128]{1,0:T(8,128)(2,1)} %collective-permute-done.8.refs_0_), channel_id=1, source_target_pairs={{0,4},{1,5},{2,6},{3,7},{4,0},{5,1},{6,2},{7,3},{8,12},{9,13},{10,... | collective-permute-start | bytes 503816 | tf_op jit(solution)/shard_map/ppermute | solution.py:407
  21.8 14.7 %collective-permute-start.11 = (bf16[656,128]{1,0:T(8,128)(2,1)}, bf16[656,128]{1,0:T(8,128)(2,1)}, u32[]{:S(2)}, u32[]{:S(2)}) collective-permute-start(bf16[656,128]{1,0:T(8,128)(2,1)} %collective-permute-done.8.refs_0_), channel_id=1, source_target_pairs={{0,5},{1,4},{2,7},{3,6},{4,1},{5,0},{6,3},{7,2},{8,13},{9,12},{10,... | collective-permute-start | bytes 503816 | tf_op jit(solution)/shard_map/ppermute | solution.py:407
  27.1 11.4 %collective-permute-start.5 = (bf16[656,128]{1,0:T(8,128)(2,1)}, bf16[656,128]{1,0:T(8,128)(2,1)S(1)}, u32[]{:S(2)}, u32[]{:S(2)}) collective-permute-start(bf16[656,128]{1,0:T(8,128)(2,1)} %get-tuple-element.37), channel_id=1, source_target_pairs={{0,1},{1,0},{2,3},{3,2},{4,5},{5,4},{6,7},{7,6},{8,9},{9,8},{10,11... | collective-permute-start | bytes 503816 | tf_op jit(solution)/shard_map/ppermute | solution.py:407
  28.7 9.8 %collective-permute-start.6 = (bf16[656,128]{1,0:T(8,128)(2,1)}, bf16[656,128]{1,0:T(8,128)(2,1)S(1)}, u32[]{:S(2)}, u32[]{:S(2)}) collective-permute-start(bf16[656,128]{1,0:T(8,128)(2,1)} %get-tuple-element.38), channel_id=1, source_target_pairs={{0,4},{1,5},{2,6},{3,7},{4,0},{5,1},{6,2},{7,3},{8,12},{9,13},{10,... | collective-permute-start | bytes 503816 | tf_op jit(solution)/shard_map/ppermute | solution.py:407
  30.7 9.3 %collective-permute-start.7 = (bf16[656,128]{1,0:T(8,128)(2,1)}, bf16[656,128]{1,0:T(8,128)(2,1)}, u32[]{:S(2)}, u32[]{:S(2)}) collective-permute-start(bf16[656,128]{1,0:T(8,128)(2,1)} %get-tuple-element.39), channel_id=1, source_target_pairs={{0,5},{1,4},{2,7},{3,6},{4,1},{5,0},{6,3},{7,2},{8,13},{9,12},{10,... | collective-permute-start | bytes 503816 | tf_op jit(solution)/shard_map/ppermute | solution.py:407
  35.0 10.0 %collective-permute-start.17 = (bf16[656,128]{1,0:T(8,128)(2,1)}, bf16[656,128]{1,0:T(8,128)(2,1)}, u32[]{:S(2)}, u32[]{:S(2)}) collective-permute-start(bf16[656,128]{1,0:T(8,128)(2,1)} %collective-permute-done.16.refs_0_), channel_id=1, source_target_pairs={{0,1},{1,0},{2,3},{3,2},{4,5},{5,4},{6,7},{7,6},{8,9},{9,8},{10,11... | collective-permute-start | bytes 503816 | tf_op jit(solution)/shard_map/ppermute | solution.py:407
  36.5 10.4 %collective-permute-start.18 = (bf16[656,128]{1,0:T(8,128)(2,1)}, bf16[656,128]{1,0:T(8,128)(2,1)}, u32[]{:S(2)}, u32[]{:S(2)}) collective-permute-start(bf16[656,128]{1,0:T(8,128)(2,1)} %collective-permute-done.16.refs_0_), channel_id=1, source_target_pairs={{0,4},{1,5},{2,6},{3,7},{4,0},{5,1},{6,2},{7,3},{8,12},{9,13},{10,... | collective-permute-start | bytes 503816 | tf_op jit(solution)/shard_map/ppermute | solution.py:407
  38.5 9.1 %collective-permute-start.19 = (bf16[656,128]{1,0:T(8,128)(2,1)}, bf16[656,128]{1,0:T(8,128)(2,1)}, u32[]{:S(2)}, u32[]{:S(2)}) collective-permute-start(bf16[656,128]{1,0:T(8,128)(2,1)} %collective-permute-done.16.refs_0_), channel_id=1, source_target_pairs={{0,5},{1,4},{2,7},{3,6},{4,1},{5,0},{6,3},{7,2},{8,13},{9,12},{10,... | collective-permute-start | bytes 503816 | tf_op jit(solution)/shard_map/ppermute | solution.py:407
  38.5 15.6 %collective-permute-start.25 = (bf16[656,128]{1,0:T(8,128)(2,1)}, bf16[656,128]{1,0:T(8,128)(2,1)}, u32[]{:S(2)}, u32[]{:S(2)}) collective-permute-start(bf16[656,128]{1,0:T(8,128)(2,1)} %collective-permute-done.24.refs_0_), channel_id=1, source_target_pairs={{0,1},{1,0},{2,3},{3,2},{4,5},{5,4},{6,7},{7,6},{8,9},{9,8},{10,11... | collective-permute-start | bytes 503816 | tf_op jit(solution)/shard_map/ppermute | solution.py:407
  40.0 16.3 %collective-permute-start.26 = (bf16[656,128]{1,0:T(8,128)(2,1)}, bf16[656,128]{1,0:T(8,128)(2,1)}, u32[]{:S(2)}, u32[]{:S(2)}) collective-permute-start(bf16[656,128]{1,0:T(8,128)(2,1)} %collective-permute-done.24.refs_0_), channel_id=1, source_target_pairs={{0,4},{1,5},{2,6},{3,7},{4,0},{5,1},{6,2},{7,3},{8,12},{9,13},{10,... | collective-permute-start | bytes 503816 | tf_op jit(solution)/shard_map/ppermute | solution.py:407
  45.0 11.6 %collective-permute-start.27 = (bf16[656,128]{1,0:T(8,128)(2,1)}, bf16[656,128]{1,0:T(8,128)(2,1)}, u32[]{:S(2)}, u32[]{:S(2)}) collective-permute-start(bf16[656,128]{1,0:T(8,128)(2,1)} %collective-permute-done.24.refs_0_), channel_id=1, source_target_pairs={{0,5},{1,4},{2,7},{3,6},{4,1},{5,0},{6,3},{7,2},{8,13},{9,12},{10,... | collective-permute-start | bytes 503816 | tf_op jit(solution)/shard_map/ppermute | solution.py:407
  47.0 15.1 %collective-permute-start.12 = (bf16[656,128]{1,0:T(8,128)(2,1)}, bf16[656,128]{1,0:T(8,128)(2,1)S(1)}, u32[]{:S(2)}, u32[]{:S(2)}) collective-permute-start(bf16[656,128]{1,0:T(8,128)(2,1)} %get-tuple-element.42), channel_id=1, source_target_pairs={{0,1},{1,0},{2,3},{3,2},{4,5},{5,4},{6,7},{7,6},{8,9},{9,8},{10,11... | collective-permute-start | bytes 503816 | tf_op jit(solution)/shard_map/ppermute | solution.py:407
  47.5 17.4 %collective-permute-start.13 = (bf16[656,128]{1,0:T(8,128)(2,1)}, bf16[656,128]{1,0:T(8,128)(2,1)S(1)}, u32[]{:S(2)}, u32[]{:S(2)}) collective-permute-start(bf16[656,128]{1,0:T(8,128)(2,1)} %get-tuple-element.43), channel_id=1, source_target_pairs={{0,4},{1,5},{2,6},{3,7},{4,0},{5,1},{6,2},{7,3},{8,12},{9,13},{10,... | collective-permute-start | bytes 503816 | tf_op jit(solution)/shard_map/ppermute | solution.py:407
  54.2 10.8 %collective-permute-start.14 = (bf16[656,128]{1,0:T(8,128)(2,1)}, bf16[656,128]{1,0:T(8,128)(2,1)}, u32[]{:S(2)}, u32[]{:S(2)}) collective-permute-start(bf16[656,128]{1,0:T(8,128)(2,1)} %get-tuple-element.44), channel_id=1, source_target_pairs={{0,5},{1,4},{2,7},{3,6},{4,1},{5,0},{6,3},{7,2},{8,13},{9,12},{10,... | collective-permute-start | bytes 503816 | tf_op jit(solution)/shard_map/ppermute | solution.py:407
  56.3 9.3 %collective-permute-start.20 = (bf16[656,128]{1,0:T(8,128)(2,1)}, bf16[656,128]{1,0:T(8,128)(2,1)}, u32[]{:S(2)}, u32[]{:S(2)}) collective-permute-start(bf16[656,128]{1,0:T(8,128)(2,1)} %get-tuple-element.48), channel_id=1, source_target_pairs={{0,1},{1,0},{2,3},{3,2},{4,5},{5,4},{6,7},{7,6},{8,9},{9,8},{10,11... | collective-permute-start | bytes 503816 | tf_op jit(solution)/shard_map/ppermute | solution.py:407
  56.6 13.8 %collective-permute-start.21 = (bf16[656,128]{1,0:T(8,128)(2,1)}, bf16[656,128]{1,0:T(8,128)(2,1)}, u32[]{:S(2)}, u32[]{:S(2)}) collective-permute-start(bf16[656,128]{1,0:T(8,128)(2,1)} %get-tuple-element.49), channel_id=1, source_target_pairs={{0,4},{1,5},{2,6},{3,7},{4,0},{5,1},{6,2},{7,3},{8,12},{9,13},{10,... | collective-permute-start | bytes 503816 | tf_op jit(solution)/shard_map/ppermute | solution.py:407
  62.1 8.4 %collective-permute-start.22 = (bf16[656,128]{1,0:T(8,128)(2,1)}, bf16[656,128]{1,0:T(8,128)(2,1)}, u32[]{:S(2)}, u32[]{:S(2)}) collective-permute-start(bf16[656,128]{1,0:T(8,128)(2,1)} %get-tuple-element.50), channel_id=1, source_target_pairs={{0,5},{1,4},{2,7},{3,6},{4,1},{5,0},{6,3},{7,2},{8,13},{9,12},{10,... | collective-permute-start | bytes 503816 | tf_op jit(solution)/shard_map/ppermute | solution.py:407
  64.9 9.8 %collective-permute-start.28 = (bf16[656,128]{1,0:T(8,128)(2,1)}, bf16[656,128]{1,0:T(8,128)(2,1)}, u32[]{:S(2)}, u32[]{:S(2)}) collective-permute-start(bf16[656,128]{1,0:T(8,128)(2,1)} %get-tuple-element.59), channel_id=1, source_target_pairs={{0,1},{1,0},{2,3},{3,2},{4,5},{5,4},{6,7},{7,6},{8,9},{9,8},{10,11... | collective-permute-start | bytes 503816 | tf_op jit(solution)/shard_map/ppermute | solution.py:407
  64.9 9.8 %collective-permute-start.29 = (bf16[656,128]{1,0:T(8,128)(2,1)}, bf16[656,128]{1,0:T(8,128)(2,1)}, u32[]{:S(2)}, u32[]{:S(2)}) collective-permute-start(bf16[656,128]{1,0:T(8,128)(2,1)} %get-tuple-element.60), channel_id=1, source_target_pairs={{0,4},{1,5},{2,6},{3,7},{4,0},{5,1},{6,2},{7,3},{8,12},{9,13},{10,... | collective-permute-start | bytes 503816 | tf_op jit(solution)/shard_map/ppermute | solution.py:407
  65.6 9.1 %collective-permute-start.30 = (bf16[656,128]{1,0:T(8,128)(2,1)}, bf16[656,128]{1,0:T(8,128)(2,1)}, u32[]{:S(2)}, u32[]{:S(2)}) collective-permute-start(bf16[656,128]{1,0:T(8,128)(2,1)} %get-tuple-element.61), channel_id=1, source_target_pairs={{0,5},{1,4},{2,7},{3,6},{4,1},{5,0},{6,3},{7,2},{8,13},{9,12},{10,... | collective-permute-start | bytes 503816 | tf_op jit(solution)/shard_map/ppermute | solution.py:407
  70.4 6.3 %collective-permute-start.15 = (bf16[656,128]{1,0:T(8,128)(2,1)}, bf16[656,128]{1,0:T(8,128)(2,1)S(1)}, u32[]{:S(2)}, u32[]{:S(2)}) collective-permute-start(bf16[656,128]{1,0:T(8,128)(2,1)} %merge.3), channel_id=1, source_target_pairs={{0,24},{2,26},{4,28},{6,30},{8,0},{10,2},{12,4},{14,6},{16,8},{18,... | collective-permute-start | bytes 503816 | tf_op jit(solution)/shard_map/ppermute | solution.py:399
  72.5 9.7 %collective-permute-start.23 = (bf16[656,128]{1,0:T(8,128)(2,1)}, bf16[656,128]{1,0:T(8,128)(2,1)S(1)}, u32[]{:S(2)}, u32[]{:S(2)}) collective-permute-start(bf16[656,128]{1,0:T(8,128)(2,1)} %merge.4), channel_id=1, source_target_pairs={{0,16},{2,18},{4,20},{6,22},{8,24},{10,26},{12,28},{14,30},{16,0},... | collective-permute-start | bytes 503816 | tf_op jit(solution)/shard_map/ppermute | solution.py:399
  76.7 7.5 %collective-permute-start.31 = (bf16[656,128]{1,0:T(8,128)(2,1)}, bf16[656,128]{1,0:T(8,128)(2,1)}, u32[]{:S(2)}, u32[]{:S(2)}) collective-permute-start(bf16[656,128]{1,0:T(8,128)(2,1)} %merge.5), channel_id=1, source_target_pairs={{0,8},{2,10},{4,12},{6,14},{8,16},{10,18},{12,20},{14,22},{16,24},... | collective-permute-start | bytes 503816 | tf_op jit(solution)/shard_map/ppermute | solution.py:399
  (8 other events, 46.6 us)

commit v4 on v3

--- a/solution.py
+++ b/solution.py
@@ -568,7 +568,6 @@
     returned[0] = go_back(0)
     for turn, s in enumerate(turns):
         if turn > 0:
-            gathered[s][0] = tie(gathered[s][0], first_back[turns[turn - 1]][0])
             if turn == B_WAIT:
                 gathered[s][0] = tie(gathered[s][0], *returned[0][1:])
             first_back[s] = attend(s)

time: 87.8 us -> 87.9 us (level)
  Pallas kernels: 31.1 us -> 32.9 us
  starting transfers between devices: 40.5 us -> 39 us
    pallas_call x4, Pallas kernels: 16.3 us -> 18.2 us  [attend(): pl.pallas_call(functools.partial(attend_kernel, lay, nb, nt, query_at, re...]
    ppermute x24, starting transfers between devices: 31.1 us -> 29.3 us  [shift_both(): return lax.ppermute(x, ('inst', 'tp'), pairs)]
  transfers between devices with their start and end apart: 32 -> 32, of which waited for: 4 -> 4; matrix products, arithmetic and copies ran while one was open for 4% -> 4% of each run, Pallas kernels for 33% -> 35%
where the time goes in v4:
time: 87.9 us; the launch traced here: 86.5 us
  starting transfers between devices  39 us (44%)
  Pallas kernels  32.9 us (37%)
  waiting for transfers between devices  10.4 us (12%)
  other arithmetic  3.05 us (3%)
    ppermute x24, starting transfers between devices, shift_both(): return lax.ppermute(x, ('inst', 'tp'), pairs)  29.3 us
    pallas_call x4, Pallas kernels, attend(): pl.pallas_call(functools.partial(attend_kernel, lay, nb, nt, query_at, re...  18.2 us
    ppermute x8, starting transfers between devices, shift(): return lax.ppermute(x, 'inst', pairs)  9.68 us
    ppermute x8, waiting for transfers between devices, shift(): return lax.ppermute(x, 'inst', pairs)  9.26 us
    pallas_call x3, Pallas kernels, merge(): pl.pallas_call(functools.partial(merge_kernel, lay, jobs), out_shape=(out...  6.02 us
    pallas_call x1, Pallas kernels, on_device(): pl.pallas_call(functools.partial(resident_kernel, lay), out_shape=(jax.Sh...  4.25 us
    pallas_call x1, Pallas kernels, on_device(): pl.pallas_call(functools.partial(final_kernel, lay, len(arrived)), out_sh...  2.63 us
    pallas_call x1, Pallas kernels, on_device(): pl.pallas_call(functools.partial(prepare_kernel, lay, resident_count, pag...  1.9 us
  transfers between devices with their start and end apart: 32, of which 4 were waited for; matrix products, arithmetic and copies ran while one was open for 4% of the time, Pallas kernels for 35%

profile of v4, /device:TPU:0, one launch (start us, length us, event | category | flops | bytes accessed | tf_op | source)
XLA Modules:
  0.0 86.5 jit_solution(17811939404074592611)
XLA Ops:
  0.5 1.9 %prepare.1 = (bf16[656,128]{1,0:T(8,128)(2,1)}, f32[16,128]{1,0:T(8,128)}) custom-call(bf16[32,5,4,128]{3,2,1,0:T(4,128)(2,1)} %bitcast.28, s32[16,32]{1,0:T(8,128)} %bitcast.34, s32[1,32]{1,0:T(1,128)} %bitcast.39), custom_call_target="tpu_custom_call" | custom-call | tf_op jit(solution)/shard_map/prepare/pallas_call | solution.py:416
  2.4 2.5 %collective-permute-start.2 = (bf16[656,128]{1,0:T(8,128)(2,1)}, bf16[656,128]{1,0:T(8,128)(2,1)S(1)}, u32[]{:S(2)}, u32[]{:S(2)}) collective-permute-start(bf16[656,128]{1,0:T(8,128)(2,1)} %get-tuple-element.46.refs_0_.q_ref), channel_id=1, source_target_pairs={{0,1},{1,0},{2,3},{3,2},{4,5},{5,4},{6,7},{7,6},{8,9},{9,8},{10,11... | collective-permute-start | bytes 503816 | tf_op jit(solution)/shard_map/ppermute | solution.py:407
  4.8 1.5 %collective-permute-start.3 = (bf16[656,128]{1,0:T(8,128)(2,1)}, bf16[656,128]{1,0:T(8,128)(2,1)S(1)}, u32[]{:S(2)}, u32[]{:S(2)}) collective-permute-start(bf16[656,128]{1,0:T(8,128)(2,1)} %get-tuple-element.46.refs_0_.q_ref), channel_id=1, source_target_pairs={{0,4},{1,5},{2,6},{3,7},{4,0},{5,1},{6,2},{7,3},{8,12},{9,13},{10,... | collective-permute-start | bytes 503816 | tf_op jit(solution)/shard_map/ppermute | solution.py:407
  6.4 2.1 %collective-permute-start.8 = (bf16[656,128]{1,0:T(8,128)(2,1)}, bf16[656,128]{1,0:T(8,128)(2,1)}, u32[]{:S(2)}, u32[]{:S(2)}) collective-permute-start(bf16[656,128]{1,0:T(8,128)(2,1)} %get-tuple-element.46.refs_0_.q_ref), channel_id=1, source_target_pairs={{0,8},{2,10},{4,12},{6,14},{8,16},{10,18},{12,20},{14,22},{16,24},... | collective-permute-start | bytes 503816 | tf_op jit(solution)/shard_map/ppermute | solution.py:399
  10.2 3.0 %collective-permute-start.16 = (bf16[656,128]{1,0:T(8,128)(2,1)}, bf16[656,128]{1,0:T(8,128)(2,1)}, u32[]{:S(2)}, u32[]{:S(2)}) collective-permute-start(bf16[656,128]{1,0:T(8,128)(2,1)} %get-tuple-element.46.refs_0_.q_ref), channel_id=1, source_target_pairs={{0,16},{2,18},{4,20},{6,22},{8,24},{10,26},{12,28},{14,30},{16,0},... | collective-permute-start | bytes 503816 | tf_op jit(solution)/shard_map/ppermute | solution.py:399
  13.2 1.8 %collective-permute-done.8.refs_0_ = bf16[656,128]{1,0:T(8,128)(2,1)} collective-permute-done((bf16[656,128]{1,0:T(8,128)(2,1)}, bf16[656,128]{1,0:T(8,128)(2,1)}, u32[]{:S(2)}, u32[]{:S(2)}) %collective-permute-start.8) | collective-permute-done | bytes 167968 | tf_op jit(solution)/shard_map/ppermute | solution.py:399
  15.0 1.6 %collective-permute-start.24 = (bf16[656,128]{1,0:T(8,128)(2,1)}, bf16[656,128]{1,0:T(8,128)(2,1)}, u32[]{:S(2)}, u32[]{:S(2)}) collective-permute-start(bf16[656,128]{1,0:T(8,128)(2,1)} %get-tuple-element.46.refs_0_.q_ref), channel_id=1, source_target_pairs={{0,24},{2,26},{4,28},{6,30},{8,0},{10,2},{12,4},{14,6},{16,8},{18,... | collective-permute-start | bytes 503816 | tf_op jit(solution)/shard_map/ppermute | solution.py:399
  16.6 1.5 %collective-permute-start.9 = (bf16[656,128]{1,0:T(8,128)(2,1)}, bf16[656,128]{1,0:T(8,128)(2,1)}, u32[]{:S(2)}, u32[]{:S(2)}) collective-permute-start(bf16[656,128]{1,0:T(8,128)(2,1)} %collective-permute-done.8.refs_0_), channel_id=1, source_target_pairs={{0,1},{1,0},{2,3},{3,2},{4,5},{5,4},{6,7},{7,6},{8,9},{9,8},{10,11... | collective-permute-start | bytes 503816 | tf_op jit(solution)/shard_map/ppermute | solution.py:407
  20.3 1.6 %collective-permute-start.10 = (bf16[656,128]{1,0:T(8,128)(2,1)}, bf16[656,128]{1,0:T(8,128)(2,1)}, u32[]{:S(2)}, u32[]{:S(2)}) collective-permute-start(bf16[656,128]{1,0:T(8,128)(2,1)} %collective-permute-done.8.refs_0_), channel_id=1, source_target_pairs={{0,4},{1,5},{2,6},{3,7},{4,0},{5,1},{6,2},{7,3},{8,12},{9,13},{10,... | collective-permute-start | bytes 503816 | tf_op jit(solution)/shard_map/ppermute | solution.py:407
  22.3 4.4 %attend.4 = (bf16[656,128]{1,0:T(8,128)(2,1)}, bf16[656,128]{1,0:T(8,128)(2,1)}, bf16[656,128]{1,0:T(8,128)(2,1)}, bf16[656,128]{1,0:T(8,128)(2,1)}) custom-call(s32[22]{0:T(128)} %get-tuple-element.69.lists, bf16[656,128]{1,0:T(8,128)(2,1)} %get-tuple-element.46.refs_0_.q_ref, bf16[656,128]{1,0:T(8,128)(2,1)} %copy-done.6, bf16[656,128]{1,0:T(8,128)(2,1)} %copy-done.7, ...), custom_call_target="tpu_custom_call" | custom-call | bytes 16777216 | tf_op jit(solution)/shard_map/attend/pallas_call | solution.py:510
  26.8 1.9 %collective-permute-start.5 = (bf16[656,128]{1,0:T(8,128)(2,1)}, bf16[656,128]{1,0:T(8,128)(2,1)S(1)}, u32[]{:S(2)}, u32[]{:S(2)}) collective-permute-start(bf16[656,128]{1,0:T(8,128)(2,1)} %get-tuple-element.34), channel_id=1, source_target_pairs={{0,1},{1,0},{2,3},{3,2},{4,5},{5,4},{6,7},{7,6},{8,9},{9,8},{10,11... | collective-permute-start | bytes 503816 | tf_op jit(solution)/shard_map/ppermute | solution.py:407
  28.7 2.0 %collective-permute-start.6 = (bf16[656,128]{1,0:T(8,128)(2,1)}, bf16[656,128]{1,0:T(8,128)(2,1)S(1)}, u32[]{:S(2)}, u32[]{:S(2)}) collective-permute-start(bf16[656,128]{1,0:T(8,128)(2,1)} %get-tuple-element.35), channel_id=1, source_target_pairs={{0,4},{1,5},{2,6},{3,7},{4,0},{5,1},{6,2},{7,3},{8,12},{9,13},{10,... | collective-permute-start | bytes 503816 | tf_op jit(solution)/shard_map/ppermute | solution.py:407
  30.7 4.2 %resident.1 = (f32[640,128]{1,0:T(8,128)}, f32[8,128]{1,0:T(8,128)}) custom-call(bf16[656,128]{1,0:T(8,128)(2,1)} %get-tuple-element.46.refs_0_.q_ref, bf16[8,4,128,256]{3,2,1,0:T(8,128)(2,1)} %pages.1, bf16[32,4,256]{2,1,0:T(4,128)(2,1)} %own.1, f32[16,128]{1,0:T(8,128)} %get-tuple-element.48.counts), custom_call_target="tpu_custom_call" | custom-call | tf_op jit(solution)/shard_map/resident/pallas_call | solution.py:456
  35.0 1.5 %collective-permute-start.17 = (bf16[656,128]{1,0:T(8,128)(2,1)}, bf16[656,128]{1,0:T(8,128)(2,1)}, u32[]{:S(2)}, u32[]{:S(2)}) collective-permute-start(bf16[656,128]{1,0:T(8,128)(2,1)} %collective-permute-done.16.refs_0_), channel_id=1, source_target_pairs={{0,1},{1,0},{2,3},{3,2},{4,5},{5,4},{6,7},{7,6},{8,9},{9,8},{10,11... | collective-permute-start | bytes 503816 | tf_op jit(solution)/shard_map/ppermute | solution.py:407
  36.5 2.0 %collective-permute-start.18 = (bf16[656,128]{1,0:T(8,128)(2,1)}, bf16[656,128]{1,0:T(8,128)(2,1)}, u32[]{:S(2)}, u32[]{:S(2)}) collective-permute-start(bf16[656,128]{1,0:T(8,128)(2,1)} %collective-permute-done.16.refs_0_), channel_id=1, source_target_pairs={{0,4},{1,5},{2,6},{3,7},{4,0},{5,1},{6,2},{7,3},{8,12},{9,13},{10,... | collective-permute-start | bytes 503816 | tf_op jit(solution)/shard_map/ppermute | solution.py:407
  38.5 1.5 %collective-permute-start.25 = (bf16[656,128]{1,0:T(8,128)(2,1)}, bf16[656,128]{1,0:T(8,128)(2,1)}, u32[]{:S(2)}, u32[]{:S(2)}) collective-permute-start(bf16[656,128]{1,0:T(8,128)(2,1)} %collective-permute-done.24.refs_0_), channel_id=1, source_target_pairs={{0,1},{1,0},{2,3},{3,2},{4,5},{5,4},{6,7},{7,6},{8,9},{9,8},{10,11... | collective-permute-start | bytes 503816 | tf_op jit(solution)/shard_map/ppermute | solution.py:407
  40.0 1.9 %collective-permute-start.26 = (bf16[656,128]{1,0:T(8,128)(2,1)}, bf16[656,128]{1,0:T(8,128)(2,1)}, u32[]{:S(2)}, u32[]{:S(2)}) collective-permute-start(bf16[656,128]{1,0:T(8,128)(2,1)} %collective-permute-done.24.refs_0_), channel_id=1, source_target_pairs={{0,4},{1,5},{2,6},{3,7},{4,0},{5,1},{6,2},{7,3},{8,12},{9,13},{10,... | collective-permute-start | bytes 503816 | tf_op jit(solution)/shard_map/ppermute | solution.py:407
  42.0 4.8 %attend.5 = (bf16[656,128]{1,0:T(8,128)(2,1)}, bf16[656,128]{1,0:T(8,128)(2,1)}, bf16[656,128]{1,0:T(8,128)(2,1)}, bf16[656,128]{1,0:T(8,128)(2,1)}) custom-call(s32[22]{0:T(128)} %get-tuple-element.67.lists, bf16[656,128]{1,0:T(8,128)(2,1)} %collective-permute-done.8.refs_0_, bf16[656,128]{1,0:T(8,128)(2,1)} %collective-permute-done.9.refs_1_, ...), custom_call_target="tpu_custom_call" | custom-call | bytes 16777216 | tf_op jit(solution)/shard_map/attend/pallas_call | solution.py:510
  48.4 1.9 %collective-permute-start.13 = (bf16[656,128]{1,0:T(8,128)(2,1)}, bf16[656,128]{1,0:T(8,128)(2,1)S(1)}, u32[]{:S(2)}, u32[]{:S(2)}) collective-permute-start(bf16[656,128]{1,0:T(8,128)(2,1)} %get-tuple-element.39), channel_id=1, source_target_pairs={{0,4},{1,5},{2,6},{3,7},{4,0},{5,1},{6,2},{7,3},{8,12},{9,13},{10,... | collective-permute-start | bytes 503816 | tf_op jit(solution)/shard_map/ppermute | solution.py:407
  50.4 4.5 %attend.6 = (bf16[656,128]{1,0:T(8,128)(2,1)}, bf16[656,128]{1,0:T(8,128)(2,1)}, bf16[656,128]{1,0:T(8,128)(2,1)}, bf16[656,128]{1,0:T(8,128)(2,1)}) custom-call(s32[22]{0:T(128)} %get-tuple-element.68.lists, bf16[656,128]{1,0:T(8,128)(2,1)} %collective-permute-done.16.refs_0_, bf16[656,128]{1,0:T(8,128)(2,1)} %collective-permute-done.17.refs_1_, ...), custom_call_target="tpu_custom_call" | custom-call | bytes 16777216 | tf_op jit(solution)/shard_map/attend/pallas_call | solution.py:510
  54.9 1.3 %collective-permute-start.14 = (bf16[656,128]{1,0:T(8,128)(2,1)}, bf16[656,128]{1,0:T(8,128)(2,1)}, u32[]{:S(2)}, u32[]{:S(2)}) collective-permute-start(bf16[656,128]{1,0:T(8,128)(2,1)} %get-tuple-element.40), channel_id=1, source_target_pairs={{0,5},{1,4},{2,7},{3,6},{4,1},{5,0},{6,3},{7,2},{8,13},{9,12},{10,... | collective-permute-start | bytes 503816 | tf_op jit(solution)/shard_map/ppermute | solution.py:407
  56.2 2.2 %collective-permute-start.21 = (bf16[656,128]{1,0:T(8,128)(2,1)}, bf16[656,128]{1,0:T(8,128)(2,1)}, u32[]{:S(2)}, u32[]{:S(2)}) collective-permute-start(bf16[656,128]{1,0:T(8,128)(2,1)} %get-tuple-element.44), channel_id=1, source_target_pairs={{0,4},{1,5},{2,6},{3,7},{4,0},{5,1},{6,2},{7,3},{8,12},{9,13},{10,... | collective-permute-start | bytes 503816 | tf_op jit(solution)/shard_map/ppermute | solution.py:407
  58.5 4.4 %attend.7 = (bf16[656,128]{1,0:T(8,128)(2,1)}, bf16[656,128]{1,0:T(8,128)(2,1)}, bf16[656,128]{1,0:T(8,128)(2,1)}, bf16[656,128]{1,0:T(8,128)(2,1)}) custom-call(s32[22]{0:T(128)} %get-tuple-element.66.lists, bf16[656,128]{1,0:T(8,128)(2,1)} %collective-permute-done.24.refs_0_, bf16[656,128]{1,0:T(8,128)(2,1)} %collective-permute-done.25.refs_1_, ...), custom_call_target="tpu_custom_call" | custom-call | bytes 16777216 | tf_op jit(solution)/shard_map/attend/pallas_call | solution.py:510
  63.0 2.2 %collective-permute-start.28 = (bf16[656,128]{1,0:T(8,128)(2,1)}, bf16[656,128]{1,0:T(8,128)(2,1)}, u32[]{:S(2)}, u32[]{:S(2)}) collective-permute-start(bf16[656,128]{1,0:T(8,128)(2,1)} %get-tuple-element.53), channel_id=1, source_target_pairs={{0,1},{1,0},{2,3},{3,2},{4,5},{5,4},{6,7},{7,6},{8,9},{9,8},{10,11... | collective-permute-start | bytes 503816 | tf_op jit(solution)/shard_map/ppermute | solution.py:407
  65.2 1.3 %collective-permute-start.29 = (bf16[656,128]{1,0:T(8,128)(2,1)}, bf16[656,128]{1,0:T(8,128)(2,1)}, u32[]{:S(2)}, u32[]{:S(2)}) collective-permute-start(bf16[656,128]{1,0:T(8,128)(2,1)} %get-tuple-element.54), channel_id=1, source_target_pairs={{0,4},{1,5},{2,6},{3,7},{4,0},{5,1},{6,2},{7,3},{8,12},{9,13},{10,... | collective-permute-start | bytes 503816 | tf_op jit(solution)/shard_map/ppermute | solution.py:407
  66.7 2.0 %merge.3 = bf16[656,128]{1,0:T(8,128)(2,1)} custom-call(bf16[656,128]{1,0:T(8,128)(2,1)} %get-tuple-element.37.refs_0_, bf16[656,128]{1,0:T(8,128)(2,1)} %copy-done.2, bf16[656,128]{1,0:T(8,128)(2,1)} %copy-done.3, bf16[656,128]{1,0:T(8,128)(2,1)} %collective-permute-done.14.refs_3_), custom_call_target="tpu_custom_call" | custom-call | tf_op jit(solution)/shard_map/merge/pallas_call | solution.py:538
  70.6 2.0 %merge.4 = bf16[656,128]{1,0:T(8,128)(2,1)} custom-call(bf16[656,128]{1,0:T(8,128)(2,1)} %get-tuple-element.42.refs_0_, bf16[656,128]{1,0:T(8,128)(2,1)} %collective-permute-done.20.refs_1_, bf16[656,128]{1,0:T(8,128)(2,1)} %collective-permute-done.21.refs_2_, bf16[656,128]{1,0:T(8,128)(2,1)} %collective-permute-done.22.refs_3_), custom_call_target="tpu_custom_call" | custom-call | tf_op jit(solution)/shard_map/merge/pallas_call | solution.py:538
  72.6 1.8 %collective-permute-start.23 = (bf16[656,128]{1,0:T(8,128)(2,1)}, bf16[656,128]{1,0:T(8,128)(2,1)S(1)}, u32[]{:S(2)}, u32[]{:S(2)}) collective-permute-start(bf16[656,128]{1,0:T(8,128)(2,1)} %merge.4), channel_id=1, source_target_pairs={{0,16},{2,18},{4,20},{6,22},{8,24},{10,26},{12,28},{14,30},{16,0},... | collective-permute-start | bytes 503816 | tf_op jit(solution)/shard_map/ppermute | solution.py:399
  74.4 2.0 %merge.5 = bf16[656,128]{1,0:T(8,128)(2,1)} custom-call(bf16[656,128]{1,0:T(8,128)(2,1)} %get-tuple-element.52.refs_0_, bf16[656,128]{1,0:T(8,128)(2,1)} %collective-permute-done.28.refs_1_, bf16[656,128]{1,0:T(8,128)(2,1)} %collective-permute-done.29.refs_2_, bf16[656,128]{1,0:T(8,128)(2,1)} %collective-permute-done.30.refs_3_), custom_call_target="tpu_custom_call" | custom-call | tf_op jit(solution)/shard_map/merge/pallas_call | solution.py:538
  76.4 5.3 %collective-permute-done.23.refs_5_ = bf16[656,128]{1,0:T(8,128)(2,1)S(1)} collective-permute-done((bf16[656,128]{1,0:T(8,128)(2,1)}, bf16[656,128]{1,0:T(8,128)(2,1)S(1)}, u32[]{:S(2)}, u32[]{:S(2)}) %collective-permute-start.23) | collective-permute-done | bytes 167968 | tf_op jit(solution)/shard_map/ppermute | solution.py:399
  81.7 2.2 %collective-permute-done.31.refs_6_ = bf16[656,128]{1,0:T(8,128)(2,1)} collective-permute-done((bf16[656,128]{1,0:T(8,128)(2,1)}, bf16[656,128]{1,0:T(8,128)(2,1)}, u32[]{:S(2)}, u32[]{:S(2)}) %collective-permute-start.31) | collective-permute-done | bytes 167968 | tf_op jit(solution)/shard_map/ppermute | solution.py:399
  83.9 2.6 %final.1 = bf16[32,5,4,128]{3,2,1,0:T(4,128)(2,1)} custom-call(bf16[656,128]{1,0:T(8,128)(2,1)} %get-tuple-element.33.refs_0_, bf16[656,128]{1,0:T(8,128)(2,1)} %copy-done, bf16[656,128]{1,0:T(8,128)(2,1)} %copy-done.1, bf16[656,128]{1,0:T(8,128)(2,1)} %collective-permute-done.7.refs_3_, bf16[656,128]{1,0:T(8,128)(2,1)} %copy-done.4, ...), custom_call_target="tpu_custom_call" | custom-call | tf_op jit(solution)/shard_map/final/pallas_call | solution.py:578
  (78 shorter events, 8.7 us)
Async XLA Ops:
  0.0 13.2 %collective-permute-start = (bf16[8,8,128,256]{3,2,1,0:T(8,128)(2,1)}, bf16[8,8,128,256]{3,2,1,0:T(8,128)(2,1)}, u32[]{:S(2)}, u32[]{:S(2)}) collective-permute-start(bf16[8,8,128,256]{3,2,1,0:T(8,128)(2,1)} %param.7), channel_id=1, source_target_pairs={{0,2},{2,0},{4,6},{6,4},{8,10},{10,8},{12,14},{14,12},{16,18},{18,... | collective-permute-start | bytes 12582920 | tf_op jit(solution)/shard_map/ppermute | solution.py:399
  2.4 7.8 %collective-permute-start.2 = (bf16[656,128]{1,0:T(8,128)(2,1)}, bf16[656,128]{1,0:T(8,128)(2,1)S(1)}, u32[]{:S(2)}, u32[]{:S(2)}) collective-permute-start(bf16[656,128]{1,0:T(8,128)(2,1)} %get-tuple-element.46.refs_0_.q_ref), channel_id=1, source_target_pairs={{0,1},{1,0},{2,3},{3,2},{4,5},{5,4},{6,7},{7,6},{8,9},{9,8},{10,11... | collective-permute-start | bytes 503816 | tf_op jit(solution)/shard_map/ppermute | solution.py:407
  4.8 15.4 %collective-permute-start.3 = (bf16[656,128]{1,0:T(8,128)(2,1)}, bf16[656,128]{1,0:T(8,128)(2,1)S(1)}, u32[]{:S(2)}, u32[]{:S(2)}) collective-permute-start(bf16[656,128]{1,0:T(8,128)(2,1)} %get-tuple-element.46.refs_0_.q_ref), channel_id=1, source_target_pairs={{0,4},{1,5},{2,6},{3,7},{4,0},{5,1},{6,2},{7,3},{8,12},{9,13},{10,... | collective-permute-start | bytes 503816 | tf_op jit(solution)/shard_map/ppermute | solution.py:407
  6.4 15.5 %collective-permute-start.4 = (bf16[656,128]{1,0:T(8,128)(2,1)}, bf16[656,128]{1,0:T(8,128)(2,1)}, u32[]{:S(2)}, u32[]{:S(2)}) collective-permute-start(bf16[656,128]{1,0:T(8,128)(2,1)} %get-tuple-element.46.refs_0_.q_ref), channel_id=1, source_target_pairs={{0,5},{1,4},{2,7},{3,6},{4,1},{5,0},{6,3},{7,2},{8,13},{9,12},{10,... | collective-permute-start | bytes 503816 | tf_op jit(solution)/shard_map/ppermute | solution.py:407
  6.4 8.7 %collective-permute-start.8 = (bf16[656,128]{1,0:T(8,128)(2,1)}, bf16[656,128]{1,0:T(8,128)(2,1)}, u32[]{:S(2)}, u32[]{:S(2)}) collective-permute-start(bf16[656,128]{1,0:T(8,128)(2,1)} %get-tuple-element.46.refs_0_.q_ref), channel_id=1, source_target_pairs={{0,8},{2,10},{4,12},{6,14},{8,16},{10,18},{12,20},{14,22},{16,24},... | collective-permute-start | bytes 503816 | tf_op jit(solution)/shard_map/ppermute | solution.py:399
  10.2 16.6 %collective-permute-start.16 = (bf16[656,128]{1,0:T(8,128)(2,1)}, bf16[656,128]{1,0:T(8,128)(2,1)}, u32[]{:S(2)}, u32[]{:S(2)}) collective-permute-start(bf16[656,128]{1,0:T(8,128)(2,1)} %get-tuple-element.46.refs_0_.q_ref), channel_id=1, source_target_pairs={{0,16},{2,18},{4,20},{6,22},{8,24},{10,26},{12,28},{14,30},{16,0},... | collective-permute-start | bytes 503816 | tf_op jit(solution)/shard_map/ppermute | solution.py:399
  13.2 3.4 %collective-permute-start.1 = (s32[2,8]{1,0:T(2,128)S(1)}, s32[2,8]{1,0:T(2,128)S(1)}, u32[]{:S(2)}, u32[]{:S(2)}) collective-permute-start(s32[2,8]{1,0:T(2,128)S(1)} %constant_dynamic-slice_fusion), channel_id=1, source_target_pairs={{0,2},{2,0},{4,6},{6,4},{8,10},{10,8},{12,14},{14,12},{16,18},{18,... | collective-permute-start | bytes 200 | tf_op jit(solution)/shard_map/ppermute | solution.py:399
  15.0 15.7 %collective-permute-start.24 = (bf16[656,128]{1,0:T(8,128)(2,1)}, bf16[656,128]{1,0:T(8,128)(2,1)}, u32[]{:S(2)}, u32[]{:S(2)}) collective-permute-start(bf16[656,128]{1,0:T(8,128)(2,1)} %get-tuple-element.46.refs_0_.q_ref), channel_id=1, source_target_pairs={{0,24},{2,26},{4,28},{6,30},{8,0},{10,2},{12,4},{14,6},{16,8},{18,... | collective-permute-start | bytes 503816 | tf_op jit(solution)/shard_map/ppermute | solution.py:399
  16.6 12.1 %collective-permute-start.9 = (bf16[656,128]{1,0:T(8,128)(2,1)}, bf16[656,128]{1,0:T(8,128)(2,1)}, u32[]{:S(2)}, u32[]{:S(2)}) collective-permute-start(bf16[656,128]{1,0:T(8,128)(2,1)} %collective-permute-done.8.refs_0_), channel_id=1, source_target_pairs={{0,1},{1,0},{2,3},{3,2},{4,5},{5,4},{6,7},{7,6},{8,9},{9,8},{10,11... | collective-permute-start | bytes 503816 | tf_op jit(solution)/shard_map/ppermute | solution.py:407
  20.3 14.7 %collective-permute-start.10 = (bf16[656,128]{1,0:T(8,128)(2,1)}, bf16[656,128]{1,0:T(8,128)(2,1)}, u32[]{:S(2)}, u32[]{:S(2)}) collective-permute-start(bf16[656,128]{1,0:T(8,128)(2,1)} %collective-permute-done.8.refs_0_), channel_id=1, source_target_pairs={{0,4},{1,5},{2,6},{3,7},{4,0},{5,1},{6,2},{7,3},{8,12},{9,13},{10,... | collective-permute-start | bytes 503816 | tf_op jit(solution)/shard_map/ppermute | solution.py:407
  21.8 14.7 %collective-permute-start.11 = (bf16[656,128]{1,0:T(8,128)(2,1)}, bf16[656,128]{1,0:T(8,128)(2,1)}, u32[]{:S(2)}, u32[]{:S(2)}) collective-permute-start(bf16[656,128]{1,0:T(8,128)(2,1)} %collective-permute-done.8.refs_0_), channel_id=1, source_target_pairs={{0,5},{1,4},{2,7},{3,6},{4,1},{5,0},{6,3},{7,2},{8,13},{9,12},{10,... | collective-permute-start | bytes 503816 | tf_op jit(solution)/shard_map/ppermute | solution.py:407
  26.8 11.7 %collective-permute-start.5 = (bf16[656,128]{1,0:T(8,128)(2,1)}, bf16[656,128]{1,0:T(8,128)(2,1)S(1)}, u32[]{:S(2)}, u32[]{:S(2)}) collective-permute-start(bf16[656,128]{1,0:T(8,128)(2,1)} %get-tuple-element.34), channel_id=1, source_target_pairs={{0,1},{1,0},{2,3},{3,2},{4,5},{5,4},{6,7},{7,6},{8,9},{9,8},{10,11... | collective-permute-start | bytes 503816 | tf_op jit(solution)/shard_map/ppermute | solution.py:407
  28.7 9.8 %collective-permute-start.6 = (bf16[656,128]{1,0:T(8,128)(2,1)}, bf16[656,128]{1,0:T(8,128)(2,1)S(1)}, u32[]{:S(2)}, u32[]{:S(2)}) collective-permute-start(bf16[656,128]{1,0:T(8,128)(2,1)} %get-tuple-element.35), channel_id=1, source_target_pairs={{0,4},{1,5},{2,6},{3,7},{4,0},{5,1},{6,2},{7,3},{8,12},{9,13},{10,... | collective-permute-start | bytes 503816 | tf_op jit(solution)/shard_map/ppermute | solution.py:407
  30.7 9.3 %collective-permute-start.7 = (bf16[656,128]{1,0:T(8,128)(2,1)}, bf16[656,128]{1,0:T(8,128)(2,1)}, u32[]{:S(2)}, u32[]{:S(2)}) collective-permute-start(bf16[656,128]{1,0:T(8,128)(2,1)} %get-tuple-element.36), channel_id=1, source_target_pairs={{0,5},{1,4},{2,7},{3,6},{4,1},{5,0},{6,3},{7,2},{8,13},{9,12},{10,... | collective-permute-start | bytes 503816 | tf_op jit(solution)/shard_map/ppermute | solution.py:407
  35.0 11.8 %collective-permute-start.17 = (bf16[656,128]{1,0:T(8,128)(2,1)}, bf16[656,128]{1,0:T(8,128)(2,1)}, u32[]{:S(2)}, u32[]{:S(2)}) collective-permute-start(bf16[656,128]{1,0:T(8,128)(2,1)} %collective-permute-done.16.refs_0_), channel_id=1, source_target_pairs={{0,1},{1,0},{2,3},{3,2},{4,5},{5,4},{6,7},{7,6},{8,9},{9,8},{10,11... | collective-permute-start | bytes 503816 | tf_op jit(solution)/shard_map/ppermute | solution.py:407
  36.5 11.3 %collective-permute-start.18 = (bf16[656,128]{1,0:T(8,128)(2,1)}, bf16[656,128]{1,0:T(8,128)(2,1)}, u32[]{:S(2)}, u32[]{:S(2)}) collective-permute-start(bf16[656,128]{1,0:T(8,128)(2,1)} %collective-permute-done.16.refs_0_), channel_id=1, source_target_pairs={{0,4},{1,5},{2,6},{3,7},{4,0},{5,1},{6,2},{7,3},{8,12},{9,13},{10,... | collective-permute-start | bytes 503816 | tf_op jit(solution)/shard_map/ppermute | solution.py:407
  38.5 9.9 %collective-permute-start.19 = (bf16[656,128]{1,0:T(8,128)(2,1)}, bf16[656,128]{1,0:T(8,128)(2,1)}, u32[]{:S(2)}, u32[]{:S(2)}) collective-permute-start(bf16[656,128]{1,0:T(8,128)(2,1)} %collective-permute-done.16.refs_0_), channel_id=1, source_target_pairs={{0,5},{1,4},{2,7},{3,6},{4,1},{5,0},{6,3},{7,2},{8,13},{9,12},{10,... | collective-permute-start | bytes 503816 | tf_op jit(solution)/shard_map/ppermute | solution.py:407
  38.5 16.4 %collective-permute-start.25 = (bf16[656,128]{1,0:T(8,128)(2,1)}, bf16[656,128]{1,0:T(8,128)(2,1)}, u32[]{:S(2)}, u32[]{:S(2)}) collective-permute-start(bf16[656,128]{1,0:T(8,128)(2,1)} %collective-permute-done.24.refs_0_), channel_id=1, source_target_pairs={{0,1},{1,0},{2,3},{3,2},{4,5},{5,4},{6,7},{7,6},{8,9},{9,8},{10,11... | collective-permute-start | bytes 503816 | tf_op jit(solution)/shard_map/ppermute | solution.py:407
  40.0 16.2 %collective-permute-start.26 = (bf16[656,128]{1,0:T(8,128)(2,1)}, bf16[656,128]{1,0:T(8,128)(2,1)}, u32[]{:S(2)}, u32[]{:S(2)}) collective-permute-start(bf16[656,128]{1,0:T(8,128)(2,1)} %collective-permute-done.24.refs_0_), channel_id=1, source_target_pairs={{0,4},{1,5},{2,6},{3,7},{4,0},{5,1},{6,2},{7,3},{8,12},{9,13},{10,... | collective-permute-start | bytes 503816 | tf_op jit(solution)/shard_map/ppermute | solution.py:407
  46.8 9.4 %collective-permute-start.27 = (bf16[656,128]{1,0:T(8,128)(2,1)}, bf16[656,128]{1,0:T(8,128)(2,1)}, u32[]{:S(2)}, u32[]{:S(2)}) collective-permute-start(bf16[656,128]{1,0:T(8,128)(2,1)} %collective-permute-done.24.refs_0_), channel_id=1, source_target_pairs={{0,5},{1,4},{2,7},{3,6},{4,1},{5,0},{6,3},{7,2},{8,13},{9,12},{10,... | collective-permute-start | bytes 503816 | tf_op jit(solution)/shard_map/ppermute | solution.py:407
  47.9 15.0 %collective-permute-start.12 = (bf16[656,128]{1,0:T(8,128)(2,1)}, bf16[656,128]{1,0:T(8,128)(2,1)S(1)}, u32[]{:S(2)}, u32[]{:S(2)}) collective-permute-start(bf16[656,128]{1,0:T(8,128)(2,1)} %get-tuple-element.38), channel_id=1, source_target_pairs={{0,1},{1,0},{2,3},{3,2},{4,5},{5,4},{6,7},{7,6},{8,9},{9,8},{10,11... | collective-permute-start | bytes 503816 | tf_op jit(solution)/shard_map/ppermute | solution.py:407
  48.4 14.6 %collective-permute-start.13 = (bf16[656,128]{1,0:T(8,128)(2,1)}, bf16[656,128]{1,0:T(8,128)(2,1)S(1)}, u32[]{:S(2)}, u32[]{:S(2)}) collective-permute-start(bf16[656,128]{1,0:T(8,128)(2,1)} %get-tuple-element.39), channel_id=1, source_target_pairs={{0,4},{1,5},{2,6},{3,7},{4,0},{5,1},{6,2},{7,3},{8,12},{9,13},{10,... | collective-permute-start | bytes 503816 | tf_op jit(solution)/shard_map/ppermute | solution.py:407
  54.9 10.3 %collective-permute-start.14 = (bf16[656,128]{1,0:T(8,128)(2,1)}, bf16[656,128]{1,0:T(8,128)(2,1)}, u32[]{:S(2)}, u32[]{:S(2)}) collective-permute-start(bf16[656,128]{1,0:T(8,128)(2,1)} %get-tuple-element.40), channel_id=1, source_target_pairs={{0,5},{1,4},{2,7},{3,6},{4,1},{5,0},{6,3},{7,2},{8,13},{9,12},{10,... | collective-permute-start | bytes 503816 | tf_op jit(solution)/shard_map/ppermute | solution.py:407
  56.2 10.2 %collective-permute-start.20 = (bf16[656,128]{1,0:T(8,128)(2,1)}, bf16[656,128]{1,0:T(8,128)(2,1)}, u32[]{:S(2)}, u32[]{:S(2)}) collective-permute-start(bf16[656,128]{1,0:T(8,128)(2,1)} %get-tuple-element.43), channel_id=1, source_target_pairs={{0,1},{1,0},{2,3},{3,2},{4,5},{5,4},{6,7},{7,6},{8,9},{9,8},{10,11... | collective-permute-start | bytes 503816 | tf_op jit(solution)/shard_map/ppermute | solution.py:407
  56.2 12.5 %collective-permute-start.21 = (bf16[656,128]{1,0:T(8,128)(2,1)}, bf16[656,128]{1,0:T(8,128)(2,1)}, u32[]{:S(2)}, u32[]{:S(2)}) collective-permute-start(bf16[656,128]{1,0:T(8,128)(2,1)} %get-tuple-element.44), channel_id=1, source_target_pairs={{0,4},{1,5},{2,6},{3,7},{4,0},{5,1},{6,2},{7,3},{8,12},{9,13},{10,... | collective-permute-start | bytes 503816 | tf_op jit(solution)/shard_map/ppermute | solution.py:407
  62.9 7.7 %collective-permute-start.22 = (bf16[656,128]{1,0:T(8,128)(2,1)}, bf16[656,128]{1,0:T(8,128)(2,1)}, u32[]{:S(2)}, u32[]{:S(2)}) collective-permute-start(bf16[656,128]{1,0:T(8,128)(2,1)} %get-tuple-element.45), channel_id=1, source_target_pairs={{0,5},{1,4},{2,7},{3,6},{4,1},{5,0},{6,3},{7,2},{8,13},{9,12},{10,... | collective-permute-start | bytes 503816 | tf_op jit(solution)/shard_map/ppermute | solution.py:407
  63.0 11.4 %collective-permute-start.28 = (bf16[656,128]{1,0:T(8,128)(2,1)}, bf16[656,128]{1,0:T(8,128)(2,1)}, u32[]{:S(2)}, u32[]{:S(2)}) collective-permute-start(bf16[656,128]{1,0:T(8,128)(2,1)} %get-tuple-element.53), channel_id=1, source_target_pairs={{0,1},{1,0},{2,3},{3,2},{4,5},{5,4},{6,7},{7,6},{8,9},{9,8},{10,11... | collective-permute-start | bytes 503816 | tf_op jit(solution)/shard_map/ppermute | solution.py:407
  65.2 9.2 %collective-permute-start.29 = (bf16[656,128]{1,0:T(8,128)(2,1)}, bf16[656,128]{1,0:T(8,128)(2,1)}, u32[]{:S(2)}, u32[]{:S(2)}) collective-permute-start(bf16[656,128]{1,0:T(8,128)(2,1)} %get-tuple-element.54), channel_id=1, source_target_pairs={{0,4},{1,5},{2,6},{3,7},{4,0},{5,1},{6,2},{7,3},{8,12},{9,13},{10,... | collective-permute-start | bytes 503816 | tf_op jit(solution)/shard_map/ppermute | solution.py:407
  66.5 7.9 %collective-permute-start.30 = (bf16[656,128]{1,0:T(8,128)(2,1)}, bf16[656,128]{1,0:T(8,128)(2,1)}, u32[]{:S(2)}, u32[]{:S(2)}) collective-permute-start(bf16[656,128]{1,0:T(8,128)(2,1)} %get-tuple-element.55), channel_id=1, source_target_pairs={{0,5},{1,4},{2,7},{3,6},{4,1},{5,0},{6,3},{7,2},{8,13},{9,12},{10,... | collective-permute-start | bytes 503816 | tf_op jit(solution)/shard_map/ppermute | solution.py:407
  68.7 7.7 %collective-permute-start.15 = (bf16[656,128]{1,0:T(8,128)(2,1)}, bf16[656,128]{1,0:T(8,128)(2,1)S(1)}, u32[]{:S(2)}, u32[]{:S(2)}) collective-permute-start(bf16[656,128]{1,0:T(8,128)(2,1)} %merge.3), channel_id=1, source_target_pairs={{0,24},{2,26},{4,28},{6,30},{8,0},{10,2},{12,4},{14,6},{16,8},{18,... | collective-permute-start | bytes 503816 | tf_op jit(solution)/shard_map/ppermute | solution.py:399
  72.6 9.1 %collective-permute-start.23 = (bf16[656,128]{1,0:T(8,128)(2,1)}, bf16[656,128]{1,0:T(8,128)(2,1)S(1)}, u32[]{:S(2)}, u32[]{:S(2)}) collective-permute-start(bf16[656,128]{1,0:T(8,128)(2,1)} %merge.4), channel_id=1, source_target_pairs={{0,16},{2,18},{4,20},{6,22},{8,24},{10,26},{12,28},{14,30},{16,0},... | collective-permute-start | bytes 503816 | tf_op jit(solution)/shard_map/ppermute | solution.py:399
  76.4 7.5 %collective-permute-start.31 = (bf16[656,128]{1,0:T(8,128)(2,1)}, bf16[656,128]{1,0:T(8,128)(2,1)}, u32[]{:S(2)}, u32[]{:S(2)}) collective-permute-start(bf16[656,128]{1,0:T(8,128)(2,1)} %merge.5), channel_id=1, source_target_pairs={{0,8},{2,10},{4,12},{6,14},{8,16},{10,18},{12,20},{14,22},{16,24},... | collective-permute-start | bytes 503816 | tf_op jit(solution)/shard_map/ppermute | solution.py:399
  (8 other events, 48.0 us)
